TPU v7x, 256 devices: a whole 4x4x8 slice. The times are simulated.
256 devices in a mesh: row: 16 (over x, z_hi, core), col: 16 (over y, z_lo).
Axes of the slice: x: 4, y: 4, z: 8 (z_hi: 2, z_lo: 4; z = z_hi * 4 + z_lo), core: 2. Of those that a mesh axis runs over, the one named last changes fastest.
Arguments:
- pair: bfloat16 [768, 768, 512], P('row', 'col'), may hold values from -6 to 6
- w_bias: bfloat16 [512, 96], replicated, may hold values from -0.25 to 0.25
- queries: bfloat16 [768, 1536], P('row', 'col'), may hold values from -360 to 360
- keys: bfloat16 [768, 1536], P('col', 'row'), may hold values from -6 to 6
- values: bfloat16 [768, 1536], P('col', 'row'), may hold values from -6 to 6
- d_out: bfloat16 [768, 1536], P('row', 'col'), may hold values from -6 to 6
Outputs:
- d_pair: bfloat16 [768, 768, 512], P('row', 'col')
- d_wbias: float32 [512, 96], replicated
- d_queries: bfloat16 [768, 1536], P('row', 'col')
- d_keys: bfloat16 [768, 1536], P('col', 'row')
- d_values: bfloat16 [768, 1536], P('col', 'row')
All inputs are finite; a program needn't handle non-finite values.
Results may differ from a plain program's by a relative error of at most 0.0095.
Values may be sent and summed in bfloat16 or wider, within the bound.
No kernel may reach another device: no remote copies, remote signals or barrier semaphores. Data moves between devices by JAX's collectives and lax.ppermute only.
A program may use at most 64 MiB of HBM per device.

v0:
```python
import jax
import jax.numpy as jnp
from jax import lax
from jax.sharding import PartitionSpec as P

D = 1536
H = 96
P_SIZE = 512
HD = 16


def on_device(pair, w_bias, queries, keys, values, d_out):
    row_count = pair.shape[0]
    col_count = pair.shape[1]
    query_full, out_full = (
        lax.all_gather(queries, "col", axis=1, tiled=True),
        lax.all_gather(d_out, "col", axis=1, tiled=True),
    )
    key_full, value_full = (
        lax.all_gather(keys, "row", axis=1, tiled=True),
        lax.all_gather(values, "row", axis=1, tiled=True),
    )
    query_heads = query_full.reshape(row_count, H, HD)
    out_heads = out_full.reshape(row_count, H, HD)
    key_heads = key_full.reshape(col_count, H, HD)
    value_heads = value_full.reshape(col_count, H, HD)
    flat_pair = pair.reshape(row_count * col_count, P_SIZE)
    pair_bias = jnp.dot(flat_pair, w_bias, preferred_element_type=jnp.float32).reshape(
        row_count, col_count, H
    )
    scale = 1.0 / HD**0.5
    scores = jnp.einsum(
        "ihd,jhd->hij", query_heads, key_heads, preferred_element_type=jnp.float32
    ) * scale + pair_bias.transpose(2, 0, 1)
    grad_prob = jnp.einsum(
        "ihd,jhd->hij", out_heads, value_heads, preferred_element_type=jnp.float32
    )
    row_max = lax.pmax(jnp.max(scores, axis=-1), "col")
    exp_scores = jnp.exp(scores - row_max[..., None])
    row_total, row_upper = lax.psum(
        (jnp.sum(exp_scores, axis=-1), jnp.sum(exp_scores * grad_prob, axis=-1)), "col"
    )
    weights = exp_scores / row_total[..., None]
    row_delta = row_upper / row_total
    grad_score = (weights * (grad_prob - row_delta[..., None])).astype(jnp.bfloat16)
    weights_low = weights.astype(jnp.bfloat16)
    score_flat = grad_score.transpose(1, 2, 0).reshape(row_count * col_count, H)
    d_pair = (
        jnp.dot(score_flat, w_bias.T, preferred_element_type=jnp.float32)
        .astype(jnp.bfloat16)
        .reshape(row_count, col_count, P_SIZE)
    )
    weight_term = jnp.dot(flat_pair.T, score_flat, preferred_element_type=jnp.float32)
    d_wbias = lax.psum(weight_term, ("row", "col"))
    query_term = (
        jnp.einsum("hij,jhd->ihd", grad_score, key_heads, preferred_element_type=jnp.float32)
        * scale
    ).reshape(row_count, D)
    key_term = (
        jnp.einsum("hij,ihd->jhd", grad_score, query_heads, preferred_element_type=jnp.float32)
        * scale
    ).reshape(col_count, D)
    value_term = jnp.einsum(
        "hij,ihd->jhd", weights_low, out_heads, preferred_element_type=jnp.float32
    ).reshape(col_count, D)
    query_grad = lax.psum_scatter(query_term, "col", scatter_dimension=1, tiled=True)
    key_grad, value_grad = (
        lax.psum_scatter(key_term, "row", scatter_dimension=1, tiled=True),
        lax.psum_scatter(value_term, "row", scatter_dimension=1, tiled=True),
    )
    return (
        d_pair,
        d_wbias,
        query_grad.astype(jnp.bfloat16),
        key_grad.astype(jnp.bfloat16),
        value_grad.astype(jnp.bfloat16),
    )


def solution(mesh):
    return jax.shard_map(
        on_device,
        mesh=mesh,
        in_specs=(
            P("row", "col", None),
            P(),
            P("row", "col"),
            P("col", "row"),
            P("col", "row"),
            P("row", "col"),
        ),
        out_specs=(P("row", "col", None), P(), P("row", "col"), P("col", "row"), P("col", "row")),
        check_vma=False,
    )
```

profile of v0, /device:TPU:1, one launch (start us, length us, event | category | flops | bytes accessed | tf_op | source)
XLA Modules:
  0.0 599.3 jit_solution(17950416940972338113)
XLA Ops:
  8.0 0.0 copy-start
  8.0 0.0 copy-start.5
  8.0 0.0 reduce-scatter.14.cloned.1.call-start
  8.1 39.6 %all-gather = bf16[16,96,48]{1,2,0:T(8,128)(2,1)S(1)} all-gather(bf16[1,96,48]{1,2,0:T(8,128)(2,1)} %bitcast.116), channel_id=1, replica_groups=mesh['row'=16,'col'=16] {'col'}, dimensions={0}, use_global_device_ids=true | all-gather | bytes 156672 | tf_op jit(solution)/shard_map/all_gather | solution.py:16
  47.7 0.1 copy.56
  47.8 0.0 copy-start.6
  47.8 0.2 reshape.54
  48.0 38.8 %all-gather.1 = bf16[16,96,48]{1,2,0:T(8,128)(2,1)S(1)} all-gather(bf16[1,96,48]{1,2,0:T(8,128)(2,1)} %bitcast.117), channel_id=1, replica_groups=mesh['row'=16,'col'=16] {'row'}, dimensions={0}, use_global_device_ids=true | all-gather | bytes 156672 | tf_op jit(solution)/shard_map/all_gather | solution.py:20
  86.8 0.1 copy.58
  86.8 0.2 reshape.56
  87.0 0.0 copy-done.5
  87.1 25.3 %all-gather.3 = bf16[16,96,48]{1,2,0:T(8,128)(2,1)S(1)} all-gather(bf16[1,96,48]{1,2,0:T(8,128)(2,1)S(1)} %bitcast.118), channel_id=1, replica_groups=mesh['row'=16,'col'=16] {'row'}, dimensions={0}, use_global_device_ids=true | all-gather | bytes 156672 | tf_op jit(solution)/shard_map/all_gather | solution.py:21
  112.3 0.1 copy.63
  112.4 0.9 reshape.60
  113.3 0.0 copy-done.6
  113.3 31.3 %all-gather.2 = bf16[16,96,48]{1,2,0:T(8,128)(2,1)S(1)} all-gather(bf16[1,96,48]{1,2,0:T(8,128)(2,1)S(1)} %bitcast.119), channel_id=1, replica_groups=mesh['row'=16,'col'=16] {'col'}, dimensions={0}, use_global_device_ids=true | all-gather | bytes 156672 | tf_op jit(solution)/shard_map/all_gather | solution.py:17
  144.6 0.1 copy.61
  144.6 0.2 reshape.58
  144.8 0.2 copy.62
  145.1 0.0 copy-start.2
  145.1 1.3 copy.64
  146.4 0.9 copy.59
  147.3 0.9 copy.57
  148.2 0.0 copy-done.2
  148.2 1.9 fusion.12
  150.2 2.1 copy.65
  152.3 3.0 fusion.11
  155.3 2.9 copy.60
  158.2 0.0 copy-done
  158.2 4.1 fusion.10
  162.3 62.7 %pmax.7 = f32[96,48]{0,1:T(8,128)} all-reduce(f32[96,48]{0,1:T(8,128)} %get-tuple-element.9), channel_id=1, replica_groups=mesh['row'=16,'col'=16] {'col'}, use_global_device_ids=true, to_apply=%region_1.0 | all-reduce | flops 4608 | bytes 36864 | tf_op jit(solution)/shard_map/pmax | solution.py:38
  225.0 2.3 fusion.6
  227.3 62.0 %all-reduce = (f32[96,48]{0,1:T(8,128)}, f32[96,48]{0,1:T(8,128)}) all-reduce(f32[96,48]{0,1:T(8,128)} %get-tuple-element.6, f32[96,48]{0,1:T(8,128)} %get-tuple-element.5), channel_id=1, replica_groups=mesh['row'=16,'col'=16] {'col'}, use_global_device_ids=true, to_apply=%region_5.0 | all-reduce | flops 9216 | bytes 73728 | tf_op jit(solution)/shard_map/psum | solution.py:40
  289.4 0.8 div.21
  290.1 0.0 copy-start.4
  290.1 2.7 fusion.7
  292.8 0.0 copy-done.4
  292.8 2.4 copy.72
  295.2 2.7 fusion.13
  298.0 0.0 reduce-scatter.14.cloned.1.call-update
  298.0 0.0 reduce-scatter.12.cloned.1.call-start
  298.0 2.4 copy.68
  300.4 2.7 convolution_multiply_fusion
  303.1 0.0 reduce-scatter.12.cloned.1.call-update
  303.2 0.0 reduce-scatter.10.cloned.1.call-start
  303.2 3.0 convolution_multiply_fusion.1
  306.2 0.0 reduce-scatter.10.cloned.1.call-update
  306.2 0.0 all-reduce.3.cloned.1.call-start
  306.2 2.1 fusion.1
  308.3 0.0 copy-start.1
  308.3 0.8 copy-done.1
  309.1 0.0 copy-start.3
  309.1 1.2 convolution_bitcast_fusion
  310.3 0.0 all-reduce.3.cloned.1.call-update
  310.4 0.0 copy-done.3
  310.4 3.2 convolution_convert_fusion
  313.6 91.2 %reduce-scatter.14.cloned.1.call-done = f32[96,48]{1,0:T(8,128)} async-done(((f32[1536,48]{1,0:T(8,128)}), f32[96,48]{1,0:T(8,128)}) %reduce-scatter.14.cloned.1.call-update) | async-done | bytes 18448
  404.8 1.5 copy.79
  406.2 76.7 %reduce-scatter.12.cloned.1.call-done = f32[96,48]{1,0:T(8,128)} async-done(((f32[1536,48]{1,0:T(8,128)}), f32[96,48]{1,0:T(8,128)}) %reduce-scatter.12.cloned.1.call-update) | async-done | bytes 18448
  483.0 1.5 copy.77
  484.4 74.1 %reduce-scatter.10.cloned.1.call-done = f32[96,48]{1,0:T(8,128)} async-done(((f32[1536,48]{1,0:T(8,128)}), f32[96,48]{1,0:T(8,128)}) %reduce-scatter.10.cloned.1.call-update) | async-done | bytes 18448
  558.5 1.5 copy.75
  560.0 30.5 %all-reduce.3.cloned.1.call-done = f32[512,96]{0,1:T(8,128)} async-done(((f32[512,96]{0,1:T(8,128)}), f32[512,96]{0,1:T(8,128)}) %all-reduce.3.cloned.1.call-update) | async-done | bytes 196624 | tf_op jit(solution)/shard_map/psum | solution.py:54
  590.5 1.6 copy.81
Async XLA Ops:
  8.0 150.2 %copy-start = (bf16[48,48,512]{2,1,0:T(8,128)(2,1)S(1)}, bf16[48,48,512]{2,1,0:T(8,128)(2,1)}, u32[]{:S(2)}) copy-start(bf16[48,48,512]{2,1,0:T(8,128)(2,1)} %param.6) | copy-start | bytes 7077892
  8.0 79.0 %copy-start.5 = (bf16[48,96]{1,0:T(8,128)(2,1)S(1)}, bf16[48,96]{1,0:T(8,128)(2,1)}, u32[]{:S(2)}) copy-start(bf16[48,96]{1,0:T(8,128)(2,1)} %param.10) | copy-start | bytes 27652
  8.0 396.7 %reduce-scatter.14.cloned.1.call-start = ((), (), s32[]{:S(2)}) async-start(), calls=%async_computation.6 | async-start | bytes 835584
  47.8 65.5 %copy-start.6 = (bf16[48,96]{1,0:T(8,128)(2,1)S(1)}, bf16[48,96]{1,0:T(8,128)(2,1)}, u32[]{:S(2)}) copy-start(bf16[48,96]{1,0:T(8,128)(2,1)} %param.11) | copy-start | bytes 27652
  145.1 3.2 copy-start.2
  290.1 2.7 copy-start.4
  298.0 185.0 %reduce-scatter.12.cloned.1.call-start = ((), (), s32[]{:S(2)}) async-start(), calls=%async_computation.5 | async-start | bytes 835584
  303.2 255.3 %reduce-scatter.10.cloned.1.call-start = ((), (), s32[]{:S(2)}) async-start(), calls=%async_computation.4 | async-start | bytes 835584
  306.2 284.3 %all-reduce.3.cloned.1.call-start = ((), (), s32[]{:S(2)}) async-start(), calls=%async_computation.3 | async-start | bytes 393216 | tf_op jit(solution)/shard_map/psum | solution.py:54
  308.3 0.8 copy-start.1
  309.1 1.2 copy-start.3
Sparse Core Ops, SparseCore 0:
  298.1 106.6 reduce-scatter.13
  408.8 74.1 reduce-scatter.11
  485.5 72.9 reduce-scatter.9
Sparse Core Ops, SparseCore 1:
  312.8 277.7 all-reduce.2
where the time goes:
time: 600 us; the launch traced here: 599 us
  waiting for transfers between devices  273 us (46%)
  blocking collectives  260 us (43%)
  matrix products  21.9 us (4%)
  local copies, waits for them, and re-layouts  21.7 us (4%)
  between operations  15.3 us (3%)
  other arithmetic  7.86 us (1%)
    unnamed x7, waiting for transfers between devices  242 us
    pmax x1, blocking collectives, on_device(): row_max = lax.pmax(jnp.max(scores, axis=-1), 'col')  62.7 us
    psum x1, blocking collectives, on_device(): lax.psum((jnp.sum(exp_scores, axis=-1), jnp.sum(exp_scores * grad_prob, a...  62 us
    all_gather x1, blocking collectives, on_device(): lax.all_gather(queries, 'col', axis=1, tiled=True)  39.6 us
    all_gather x1, blocking collectives, on_device(): lax.all_gather(keys, 'row', axis=1, tiled=True)  38.8 us
    all_gather x1, blocking collectives, on_device(): lax.all_gather(d_out, 'col', axis=1, tiled=True)  31.3 us
    psum x1, waiting for transfers between devices, on_device(): d_wbias = lax.psum(weight_term, ('row', 'col'))  30.5 us
    all_gather x1, blocking collectives, on_device(): lax.all_gather(values, 'row', axis=1, tiled=True)  25.3 us
  transfers between devices with their start and end apart: 4, of which 4 were waited for; matrix products, arithmetic and copies ran while one was open for 3% of the time, Pallas kernels for 0%

commit v1 on v0

v1 whole, which is shorter than its diff:
```python
import jax
import jax.numpy as jnp
from jax import lax
from jax.sharding import PartitionSpec as P

D = 1536
H = 96
P_SIZE = 512
HD = 16


def send_to_all(x, axis, n, groups=None):
    return lax.all_to_all(
        jnp.broadcast_to(x[None], (n,) + x.shape), axis, 0, 0, axis_index_groups=groups
    )


def on_device(rows, cols, pair, w_bias, queries, keys, values, d_out):
    row_count = pair.shape[0]
    col_count = pair.shape[1]
    chips = rows // 2
    cores_apart = [[2 * k + c for k in range(chips)] for c in range(2)]
    cores_together = [[2 * k, 2 * k + 1] for k in range(chips)]
    own_width = queries.shape[1]
    row_side = send_to_all(jnp.concatenate([queries, d_out], axis=0), "col", cols)
    row_side = row_side.reshape(cols, 2, row_count, own_width).transpose(1, 2, 0, 3)
    query_heads, out_heads = row_side.reshape(2, row_count, H, HD)
    col_side = send_to_all(jnp.concatenate([keys, values], axis=0), "row", chips, cores_apart)
    col_side = lax.all_gather(col_side, "row", axis_index_groups=cores_together)
    col_side = col_side.reshape(2, chips, 2, col_count, own_width).transpose(2, 3, 1, 0, 4)
    key_heads, value_heads = col_side.reshape(2, col_count, H, HD)
    flat_pair = pair.reshape(row_count * col_count, P_SIZE)
    pair_bias = jnp.dot(flat_pair, w_bias, preferred_element_type=jnp.float32).reshape(
        row_count, col_count, H
    )
    scale = 1.0 / HD**0.5
    scores = jnp.einsum(
        "ihd,jhd->hij", query_heads, key_heads, preferred_element_type=jnp.float32
    ) * scale + pair_bias.transpose(2, 0, 1)
    grad_prob = jnp.einsum(
        "ihd,jhd->hij", out_heads, value_heads, preferred_element_type=jnp.float32
    )
    own_max = jnp.max(scores, axis=-1)
    exp_scores = jnp.exp(scores - own_max[..., None])
    own_total = jnp.sum(exp_scores, axis=-1)
    own_upper = jnp.sum(exp_scores * grad_prob, axis=-1)
    stats = jnp.stack([own_max, own_total, own_upper]).reshape(-1, 128)
    stats = send_to_all(stats, "col", cols).reshape(cols, 3, H, row_count)
    row_max = jnp.max(stats[:, 0], axis=0)
    factors = jnp.exp(stats[:, 0] - row_max)
    row_total = jnp.sum(factors * stats[:, 1], axis=0)
    row_delta = jnp.sum(factors * stats[:, 2], axis=0) / row_total
    weights = exp_scores * (jnp.exp(own_max - row_max) / row_total)[..., None]
    grad_score = (weights * (grad_prob - row_delta[..., None])).astype(jnp.bfloat16)
    weights_low = weights.astype(jnp.bfloat16)
    score_flat = grad_score.transpose(1, 2, 0).reshape(row_count * col_count, H)
    d_pair = (
        jnp.dot(score_flat, w_bias.T, preferred_element_type=jnp.float32)
        .astype(jnp.bfloat16)
        .reshape(row_count, col_count, P_SIZE)
    )
    weight_term = jnp.dot(flat_pair.T, score_flat, preferred_element_type=jnp.float32)
    query_term = (
        jnp.einsum("hij,jhd->ihd", grad_score, key_heads, preferred_element_type=jnp.float32)
        * scale
    ).reshape(row_count, cols, own_width)
    key_term = (
        jnp.einsum("hij,ihd->jhd", grad_score, query_heads, preferred_element_type=jnp.float32)
        * scale
    ).reshape(col_count, rows, own_width)
    value_term = jnp.einsum(
        "hij,ihd->jhd", weights_low, out_heads, preferred_element_type=jnp.float32
    ).reshape(col_count, rows, own_width)
    low = jnp.bfloat16
    col_parts = jnp.concatenate(
        [
            query_term.astype(low).transpose(1, 0, 2),
            weight_term.astype(low).reshape(cols, P_SIZE // cols, H),
        ],
        axis=1,
    )
    col_parts = lax.all_to_all(col_parts, "col", 0, 0)
    col_sum = jnp.sum(col_parts.astype(jnp.float32), axis=0)
    query_grad, weight_part = col_sum[:row_count], col_sum[row_count:]
    row_parts = jnp.concatenate(
        [
            key_term.astype(low).transpose(1, 0, 2),
            value_term.astype(low).transpose(1, 0, 2),
            jnp.broadcast_to(weight_part.astype(low)[None], (rows,) + weight_part.shape),
        ],
        axis=1,
    )
    row_parts = lax.all_to_all(row_parts, "row", 0, 0)
    row_sum = jnp.sum(row_parts.astype(jnp.float32), axis=0)
    key_grad = row_sum[:col_count]
    value_grad = row_sum[col_count : 2 * col_count]
    weight_shard = row_sum[2 * col_count :].astype(low)
    d_wbias = send_to_all(weight_shard, "col", cols).reshape(P_SIZE, H).astype(jnp.float32)
    return d_pair, d_wbias, query_grad.astype(low), key_grad.astype(low), value_grad.astype(low)


def solution(mesh):
    def step(*arrays):
        return on_device(mesh.shape["row"], mesh.shape["col"], *arrays)

    return jax.shard_map(
        step,
        mesh=mesh,
        in_specs=(
            P("row", "col", None),
            P(),
            P("row", "col"),
            P("col", "row"),
            P("col", "row"),
            P("row", "col"),
        ),
        out_specs=(P("row", "col", None), P(), P("row", "col"), P("col", "row"), P("col", "row")),
        check_vma=False,
    )
```

time: 600 us -> 181 us (0.30)
  waiting for transfers between devices: 273 us -> 39.5 us
  blocking collectives: 260 us -> 32.9 us
  starting transfers between devices: 0.17 us -> 31.8 us
  local copies, waits for them, and re-layouts: 21.7 us -> 36.3 us
  between operations: 15.3 us -> 0.82 us
  other arithmetic: 7.86 us -> 20 us
    unnamed x7 -> x0, waiting for transfers between devices: 242 us -> none
    all_gather x4 -> x1, blocking collectives: 135 us -> 4.81 us  [on_device(): col_side = lax.all_gather(col_side, 'row', axis_index_groups=cores_together)]
    pmax x1 -> x0, blocking collectives: 62.7 us -> none  [on_device(): row_max = lax.pmax(jnp.max(scores, axis=-1), 'col')]
    psum x1 -> x0, blocking collectives: 62 us -> none  [on_device(): lax.psum((jnp.sum(exp_scores, axis=-1), jnp.sum(exp_scores * grad_prob, a...]
    all_to_all x0 -> x5, waiting for transfers between devices: none -> 39.5 us  [the longest x3 20.3 us: send_to_all(): lax.all_to_all(jnp.broadcast_to(x[None], (n,) + x.shape), axis, 0, 0, axi...]
    all_to_all x0 -> x5, starting transfers between devices: none -> 31.8 us  [the longest x3 21.8 us: send_to_all(): lax.all_to_all(jnp.broadcast_to(x[None], (n,) + x.shape), axis, 0, 0, axi...]
    psum x1 -> x0, waiting for transfers between devices: 30.5 us -> none  [on_device(): d_wbias = lax.psum(weight_term, ('row', 'col'))]
    all_to_all x0 -> x1, blocking collectives: none -> 28 us  [send_to_all(): lax.all_to_all(jnp.broadcast_to(x[None], (n,) + x.shape), axis, 0, 0, axi...]
  transfers between devices with their start and end apart: 4 -> 5, of which waited for: 4 -> 5; matrix products, arithmetic and copies ran while one was open for 3% -> 5% of each run, Pallas kernels for 0% -> 0%
where the time goes in v1:
time: 181 us; the launch traced here: 179 us
  waiting for transfers between devices  39.5 us (22%)
  local copies, waits for them, and re-layouts  36.3 us (20%)
  blocking collectives  32.9 us (18%)
  starting transfers between devices  31.8 us (18%)
  other arithmetic  20 us (11%)
  matrix products  17.4 us (10%)
    all_to_all x1, blocking collectives, send_to_all(): lax.all_to_all(jnp.broadcast_to(x[None], (n,) + x.shape), axis, 0, 0, axi...  28 us
    all_to_all x3, starting transfers between devices, send_to_all(): lax.all_to_all(jnp.broadcast_to(x[None], (n,) + x.shape), axis, 0, 0, axi...  21.8 us
    all_to_all x3, waiting for transfers between devices, send_to_all(): lax.all_to_all(jnp.broadcast_to(x[None], (n,) + x.shape), axis, 0, 0, axi...  20.3 us
    all_to_all x1, waiting for transfers between devices, on_device(): row_parts = lax.all_to_all(row_parts, 'row', 0, 0)  12 us
    all_to_all x1, waiting for transfers between devices, on_device(): col_parts = lax.all_to_all(col_parts, 'col', 0, 0)  7.26 us
    all_to_all x1, starting transfers between devices, on_device(): row_parts = lax.all_to_all(row_parts, 'row', 0, 0)  5.81 us
    unnamed x24, local copies, waits for them, and re-layouts  5.07 us
    all_gather x1, blocking collectives, on_device(): col_side = lax.all_gather(col_side, 'row', axis_index_groups=cores_together)  4.81 us
  transfers between devices with their start and end apart: 5, of which 5 were waited for; matrix products, arithmetic and copies ran while one was open for 5% of the time, Pallas kernels for 0%

profile of v1, /device:TPU:1, one launch (start us, length us, event | category | flops | bytes accessed | tf_op | source)
XLA Modules:
  0.0 178.7 jit_solution(11099831826357727567)
XLA Ops:
  0.6 0.9 pad_maximum_fusion.4
  1.5 0.7 broadcast_in_dim.13
  2.2 11.5 %all-to-all-start.1 = ((bf16[8,96,96]{2,1,0:T(8,128)(2,1)}), bf16[8,96,96]{2,1,0:T(8,128)(2,1)S(1)}, u32[]{:S(2)}, u32[]{:S(2)}) async-start(bf16[8,96,96]{2,1,0:T(8,128)(2,1)} %broadcast_in_dim.13), calls=%async_computation.1 | async-start | bytes 393216 | tf_op jit(solution)/shard_map/all_to_all | solution.py:13
  13.7 0.7 pad_maximum_fusion.3
  14.4 9.1 %all-to-all-done.1 = bf16[8,96,96]{2,1,0:T(8,128)(2,1)S(1)} async-done(((bf16[8,96,96]{2,1,0:T(8,128)(2,1)}), bf16[8,96,96]{2,1,0:T(8,128)(2,1)S(1)}, u32[]{:S(2)}, u32[]{:S(2)}) %all-to-all-start.1) | async-done | bytes 147488 | tf_op jit(solution)/shard_map/all_to_all | solution.py:13
  23.5 0.8 broadcast_in_dim.12
  24.3 6.1 %all-to-all-start = ((bf16[16,96,96]{2,1,0:T(8,128)(2,1)}), bf16[16,96,96]{2,1,0:T(8,128)(2,1)S(1)}, u32[]{:S(2)}, u32[]{:S(2)}) async-start(bf16[16,96,96]{2,1,0:T(8,128)(2,1)} %broadcast_in_dim.12), calls=%async_computation | async-start | bytes 786432 | tf_op jit(solution)/shard_map/all_to_all | solution.py:13
  30.5 4.8 %all-gather = bf16[16,96,96]{2,1,0:T(8,128)(2,1)S(1)} all-gather(bf16[8,96,96]{2,1,0:T(8,128)(2,1)S(1)} %all-to-all-done.1), channel_id=2, replica_groups={{0,16},{32,48},{64,80},{96,112},{128,144},{160,176},{192,208},{224,240}..., dimensions={0}, use_global_device_ids=true | all-gather | bytes 442368 | tf_op jit(solution)/shard_map/all_gather | solution.py:29
  35.3 0.9 copy.111
  36.3 0.2 copy.114
  36.5 5.4 %all-to-all-done = bf16[16,96,96]{2,1,0:T(8,128)(2,1)S(1)} async-done(((bf16[16,96,96]{2,1,0:T(8,128)(2,1)}), bf16[16,96,96]{2,1,0:T(8,128)(2,1)S(1)}, u32[]{:S(2)}, u32[]{:S(2)}) %all-to-all-start) | async-done | bytes 294944 | tf_op jit(solution)/shard_map/all_to_all | solution.py:13
  41.9 0.9 copy.110
  42.8 0.2 copy.113
  43.0 0.8 copy-done.5
  43.8 1.9 %fusion.23 = f32[96,48,48]{1,2,0:T(8,128)} fusion(bf16[48,96,16]{0,2,1:T(8,128)(2,1)S(1)} %bitcast.123, bf16[48,96,16]{0,2,1:T(8,128)(2,1)S(1)} %bitcast.127), kind=kOutput, calls=%fused_computation.49 | convolution fusion | flops 7077888 | bytes 1179648 | tf_op jit(solution)/shard_map/ihd,jhd->hij/dot_general | solution.py:40
  45.7 2.1 %copy.115 = f32[96,48,48]{0,2,1:T(8,128)S(1)} copy(f32[96,48,48]{1,2,0:T(8,128)} %fusion.23) | data formatting | bytes 1769472 | tf_op jit(solution)/shard_map/ihd,jhd->hij/dot_general | solution.py:40
  47.8 3.0 %fusion.22 = f32[96,48,48]{1,2,0:T(8,128)} fusion(bf16[48,96,16]{0,2,1:T(8,128)(2,1)} %bitcast.121, bf16[48,96,16]{0,2,1:T(8,128)(2,1)} %bitcast.119), kind=kOutput, calls=%fused_computation.48 | convolution fusion | flops 7077888 | bytes 1179648 | tf_op jit(solution)/shard_map/ihd,jhd->hij/dot_general | solution.py:37
  50.9 2.9 %copy.112 = f32[96,48,48]{0,2,1:T(8,128)} copy(f32[96,48,48]{1,2,0:T(8,128)} %fusion.22) | data formatting | bytes 1769472 | tf_op jit(solution)/shard_map/ihd,jhd->hij/dot_general | solution.py:37
  53.8 3.1 %fusion.18 = (f32[96,48]{0,1:T(8,128)S(1)}, f32[96,48,48]{0,2,1:T(8,128)S(1)}, f32[48,48,96]{2,1,0:T(8,128)}) fusion(f32[96,48,48]{0,2,1:T(8,128)} %copy.112, bf16[48,48,512]{2,1,0:T(8,128)(2,1)S(1)} %copy-done, bf16[512,96]{0,1:T(8,128)(2,1)} %param.7), kind=kOutput, calls=%fused_computation.44 | convolution fusion | flops 227151360 | bytes 5130240 | tf_op jit(solution)/shard_map/dot_general | solution.py:33
  56.9 0.5 fusion.14
  57.4 0.5 copy-done.1
  57.9 0.6 pad_maximum_fusion.2
  58.6 1.7 copy.116
  60.2 1.6 broadcast_in_dim.14
  61.9 0.9 broadcast_in_dim.15
  62.8 28.0 %all_to_all.30 = f32[16,108,128]{2,1,0:T(8,128)} all-to-all(f32[16,108,128]{2,1,0:T(8,128)S(1)} %broadcast_in_dim.15), channel_id=1, replica_groups=mesh['row'=16,'col'=16] {'col'}, dimensions={0} | all-to-all | bytes 1769472 | tf_op jit(solution)/shard_map/all_to_all | solution.py:13
  90.8 3.1 %reshape.74 = f32[16,3,96,48]{3,2,1,0:T(8,128)} reshape(f32[16,108,128]{2,1,0:T(8,128)} %all_to_all.30) | data formatting | bytes 1769472 | tf_op jit(solution)/shard_map/reshape | solution.py:48
  93.9 1.2 bitcast_reduce_fusion
  95.1 0.6 copy-done.8
  95.7 2.5 %fusion.12 = (f32[96,48]{1,0:T(8,128)}, f32[96,48]{1,0:T(8,128)}) fusion(f32[16,3,96,48]{3,2,1,0:T(8,128)} %reshape.74, f32[96,48]{1,0:T(8,128)S(1)} %bitcast_reduce_fusion), kind=kLoop, calls=%fused_computation.26 | loop fusion | flops 359424 | bytes 940032 | tf_op jit(solution)/shard_map/reduce_sum | solution.py:51
  98.2 1.5 copy.118
  99.7 1.5 copy.120
  101.2 1.5 div.23
  102.6 1.5 copy.122
  104.1 1.5 copy.125
  105.6 1.4 exponential_divide_fusion
  107.0 0.8 bitcast_divide_fusion.1
  107.8 2.0 %fusion.3 = bf16[48,48,96]{2,1,0:T(8,128)(2,1)S(1)} fusion(f32[96,48,48]{0,2,1:T(8,128)S(1)} %copy.115, f32[48,48,96]{2,1,0:T(8,128)} %get-tuple-element.46, f32[96,48,48]{0,2,1:T(8,128)} %copy.112, f32[48,96]{1,0:T(8,128)S(1)} %get-tuple-element.45, f32[48,96]{1,0:T(8,128)S(1)} %get-tuple-element.44, f32[48,96]{1,0:T(8,128)} %bitcast.133), kind=kLoop, calls=%fused_computation.8 | loop fusion | flops 1548288 | bytes 3151872 | tf_op jit(solution)/shard_map/convert_element_type | solution.py:54
  109.9 0.8 copy-done.2
  110.7 1.2 fusion.8
  111.9 1.7 copy.131
  113.5 2.7 %multiply_convert_fusion.1 = (bf16[96,48,48]{0,2,1:T(8,128)(2,1)}, bf16[96,48,48]{0,2,1:T(8,128)(2,1)}) fusion(f32[96,48,48]{0,2,1:T(8,128)} %copy-done.1, f32[96,48]{0,1:T(8,128)} %exponential_divide_fusion, f32[96,48]{0,1:T(8,128)} %copy-done.7, f32[96,48,48]{0,2,1:T(8,128)S(1)} %copy.115, f32[96,48]{0,1:T(8,128)} %copy.125), kind=kLoop, calls=%fused_computation.20 | loop fusion | flops 1327104 | bytes 2709504 | tf_op jit(solution)/shard_map/convert_element_type | solution.py:55
  116.2 2.4 %copy.128 = bf16[96,48,48]{2,1,0:T(8,128)(2,1)} copy(bf16[96,48,48]{0,2,1:T(8,128)(2,1)} %get-tuple-element.36) | data formatting | bytes 884736 | tf_op jit(solution)/shard_map/convert_element_type | solution.py:55
  118.6 1.7 copy.127
  120.3 2.5 %fusion.1 = bf16[96,16,48]{2,1,0:T(8,128)(2,1)} fusion(bf16[48,96,16]{0,2,1:T(8,128)(2,1)} %bitcast.120, bf16[96,48,48]{2,1,0:T(8,128)(2,1)S(1)} %copy.127), kind=kOutput, calls=%fused_computation.4 | convolution fusion | flops 7225344 | bytes 737280 | tf_op jit(solution)/shard_map/hij,jhd->ihd/dot_general | solution.py:64
  122.8 1.8 %copy.130 = bf16[48,16,96]{2,0,1:T(8,128)(2,1)} copy(bf16[48,16,96]{0,2,1:T(8,128)(2,1)} %bitcast.129) | data formatting | bytes 294912 | tf_op jit(solution)/shard_map/convert_element_type | solution.py:77
  124.6 1.8 %pad_maximum_fusion.1 = bf16[16,80,96]{2,1,0:T(8,128)(2,1)} fusion(bf16[16,32,96]{2,1,0:T(8,128)(2,1)} %bitcast.135, bf16[16,48,96]{2,1,0:T(8,128)(2,1)} %bitcast.134), kind=kLoop, calls=%fused_computation.32 | loop fusion | flops 491520 | bytes 491520 | tf_op jit(solution)/shard_map/concatenate | solution.py:75
  126.4 4.2 %all-to-all-start.3 = ((bf16[16,80,96]{2,1,0:T(8,128)(2,1)}), bf16[16,80,96]{2,1,0:T(8,128)(2,1)}, u32[]{:S(2)}, u32[]{:S(2)}) async-start(bf16[16,80,96]{2,1,0:T(8,128)(2,1)} %pad_maximum_fusion.1), calls=%async_computation.3 | async-start | bytes 655360 | tf_op jit(solution)/shard_map/all_to_all | solution.py:82
  130.6 2.3 %fusion = bf16[96,16,48]{2,1,0:T(8,128)(2,1)} fusion(bf16[48,96,16]{0,2,1:T(8,128)(2,1)} %bitcast.122, bf16[96,48,48]{2,1,0:T(8,128)(2,1)S(1)} %copy.127), kind=kOutput, calls=%fused_computation.3 | convolution fusion | flops 7225344 | bytes 737280 | tf_op jit(solution)/shard_map/hij,ihd->jhd/dot_general | solution.py:68
  132.9 1.2 convolution_convert_fusion.1
  134.1 7.3 %all-to-all-done.3 = bf16[16,80,96]{2,1,0:T(8,128)(2,1)} async-done(((bf16[16,80,96]{2,1,0:T(8,128)(2,1)}), bf16[16,80,96]{2,1,0:T(8,128)(2,1)}, u32[]{:S(2)}, u32[]{:S(2)}) %all-to-all-start.3) | async-done | bytes 245792 | tf_op jit(solution)/shard_map/all_to_all | solution.py:82
  141.4 1.0 reduce.1
  142.4 0.1 copy.141
  142.6 2.3 %pad_maximum_fusion = bf16[16,128,96]{1,2,0:T(8,128)(2,1)} fusion(bf16[16,32,96]{1,2,0:T(8,128)(2,1)S(1)} %broadcast_in_dim.16, bf16[16,48,96]{1,2,0:T(8,128)(2,1)} %bitcast.131, bf16[16,48,96]{1,2,0:T(8,128)(2,1)} %bitcast.130), kind=kLoop, calls=%fused_computation.31 | loop fusion | flops 1179648 | bytes 786432 | tf_op jit(solution)/shard_map/concatenate | solution.py:85
  144.9 5.8 %all-to-all-start.4 = ((bf16[16,128,96]{1,2,0:T(8,128)(2,1)}), bf16[16,128,96]{1,2,0:T(8,128)(2,1)S(1)}, u32[]{:S(2)}, u32[]{:S(2)}) async-start(bf16[16,128,96]{1,2,0:T(8,128)(2,1)} %pad_maximum_fusion), calls=%async_computation.4 | async-start | bytes 786432 | tf_op jit(solution)/shard_map/all_to_all | solution.py:93
  150.8 2.2 %convolution_convert_fusion = bf16[2304,512]{1,0:T(8,128)(2,1)} fusion(bf16[2304,96]{1,0:T(8,128)(2,1)S(1)} %bitcast.118, bf16[512,96]{0,1:T(8,128)(2,1)S(1)} %copy-done.9), kind=kOutput, calls=%fused_computation | convolution fusion | flops 227672064 | bytes 2899968 | tf_op jit(solution)/shard_map/dot_general | solution.py:58
  152.9 0.6 slice.47
  153.5 12.0 %all-to-all-done.4 = bf16[16,128,96]{1,2,0:T(8,128)(2,1)S(1)} async-done(((bf16[16,128,96]{1,2,0:T(8,128)(2,1)}), bf16[16,128,96]{1,2,0:T(8,128)(2,1)S(1)}, u32[]{:S(2)}, u32[]{:S(2)}) %all-to-all-start.4) | async-done | bytes 393248 | tf_op jit(solution)/shard_map/all_to_all | solution.py:93
  165.8 0.7 broadcast_in_dim.17
  166.5 4.2 %all-to-all-start.5 = ((bf16[16,32,96]{2,1,0:T(8,128)(2,1)}), bf16[16,32,96]{2,1,0:T(8,128)(2,1)S(1)}, u32[]{:S(2)}, u32[]{:S(2)}) async-start(bf16[16,32,96]{2,1,0:T(8,128)(2,1)} %broadcast_in_dim.17), calls=%async_computation.5 | async-start | bytes 262144 | tf_op jit(solution)/shard_map/all_to_all | solution.py:13
  170.7 0.7 copy.137
  171.4 0.7 copy.136
  172.1 5.8 %all-to-all-done.5 = bf16[16,32,96]{2,1,0:T(8,128)(2,1)S(1)} async-done(((bf16[16,32,96]{2,1,0:T(8,128)(2,1)}), bf16[16,32,96]{2,1,0:T(8,128)(2,1)S(1)}, u32[]{:S(2)}, u32[]{:S(2)}) %all-to-all-start.5) | async-done | bytes 98336 | tf_op jit(solution)/shard_map/all_to_all | solution.py:13
  177.9 0.8 copy.134
  (25 shorter events, 0.5 us)
Async XLA Ops:
  0.6 53.1 %copy-start = (bf16[48,48,512]{2,1,0:T(8,128)(2,1)S(1)}, bf16[48,48,512]{2,1,0:T(8,128)(2,1)}, u32[]{:S(2)}) copy-start(bf16[48,48,512]{2,1,0:T(8,128)(2,1)} %param.6) | copy-start | bytes 7077892
  2.2 21.3 %all-to-all-start.1 = ((bf16[8,96,96]{2,1,0:T(8,128)(2,1)}), bf16[8,96,96]{2,1,0:T(8,128)(2,1)S(1)}, u32[]{:S(2)}, u32[]{:S(2)}) async-start(bf16[8,96,96]{2,1,0:T(8,128)(2,1)} %broadcast_in_dim.13), calls=%async_computation.1 | async-start | bytes 393216 | tf_op jit(solution)/shard_map/all_to_all | solution.py:13
  24.3 17.5 %all-to-all-start = ((bf16[16,96,96]{2,1,0:T(8,128)(2,1)}), bf16[16,96,96]{2,1,0:T(8,128)(2,1)S(1)}, u32[]{:S(2)}, u32[]{:S(2)}) async-start(bf16[16,96,96]{2,1,0:T(8,128)(2,1)} %broadcast_in_dim.12), calls=%async_computation | async-start | bytes 786432 | tf_op jit(solution)/shard_map/all_to_all | solution.py:13
  43.0 0.8 copy-start.5
  56.9 1.0 copy-start.1
  56.9 1.0 copy-start.7
  95.1 0.6 copy-start.8
  109.9 0.8 copy-start.2
  126.4 15.0 %all-to-all-start.3 = ((bf16[16,80,96]{2,1,0:T(8,128)(2,1)}), bf16[16,80,96]{2,1,0:T(8,128)(2,1)}, u32[]{:S(2)}, u32[]{:S(2)}) async-start(bf16[16,80,96]{2,1,0:T(8,128)(2,1)} %pad_maximum_fusion.1), calls=%async_computation.3 | async-start | bytes 655360 | tf_op jit(solution)/shard_map/all_to_all | solution.py:82
  130.6 2.3 %copy-start.4 = (bf16[96,48,48]{2,1,0:T(8,128)(2,1)S(1)}, bf16[96,48,48]{2,1,0:T(8,128)(2,1)}, u32[]{:S(2)}) copy-start(bf16[96,48,48]{2,1,0:T(8,128)(2,1)} %copy.128) | copy-start | bytes 1327108
  130.6 2.3 %copy-start.6 = (bf16[1,48,16,96]{1,3,2,0:T(8,128)(2,1)S(1)}, bf16[1,48,16,96]{1,3,2,0:T(8,128)(2,1)}, u32[]{:S(2)}) copy-start(bf16[1,48,16,96]{1,3,2,0:T(8,128)(2,1)} %copy-done.5) | copy-start | bytes 442372
  142.6 8.1 %copy-start.3 = (bf16[48,48,96]{2,1,0:T(8,128)(2,1)S(1)}, bf16[48,48,96]{2,1,0:T(8,128)(2,1)}, u32[]{:S(2)}) copy-start(bf16[48,48,96]{2,1,0:T(8,128)(2,1)} %copy-done.2) | copy-start | bytes 1327108
  142.6 8.1 %copy-start.9 = (bf16[512,96]{0,1:T(8,128)(2,1)S(1)}, bf16[512,96]{0,1:T(8,128)(2,1)}, u32[]{:S(2)}) copy-start(bf16[512,96]{0,1:T(8,128)(2,1)} %param.7) | copy-start | bytes 294916
  144.9 20.6 %all-to-all-start.4 = ((bf16[16,128,96]{1,2,0:T(8,128)(2,1)}), bf16[16,128,96]{1,2,0:T(8,128)(2,1)S(1)}, u32[]{:S(2)}, u32[]{:S(2)}) async-start(bf16[16,128,96]{1,2,0:T(8,128)(2,1)} %pad_maximum_fusion), calls=%async_computation.4 | async-start | bytes 786432 | tf_op jit(solution)/shard_map/all_to_all | solution.py:93
  166.5 11.4 %all-to-all-start.5 = ((bf16[16,32,96]{2,1,0:T(8,128)(2,1)}), bf16[16,32,96]{2,1,0:T(8,128)(2,1)S(1)}, u32[]{:S(2)}, u32[]{:S(2)}) async-start(bf16[16,32,96]{2,1,0:T(8,128)(2,1)} %broadcast_in_dim.17), calls=%async_computation.5 | async-start | bytes 262144 | tf_op jit(solution)/shard_map/all_to_all | solution.py:13

commit v2 on v0

v2 whole, which is shorter than its diff:
```python
import jax
import jax.numpy as jnp
from jax import lax
from jax.experimental import pallas as pl
from jax.experimental.pallas import tpu as pltpu
from jax.sharding import PartitionSpec as P


H = 96
P_SIZE = 512
HD = 16
SIDE = 16
PLACES = 6
LANES = 128
N_I = 48
N_J = 48
CELLS = N_I * N_J
LOW = jnp.bfloat16
F32 = jnp.float32
VMEM_LIMIT = 48 * 1024 * 1024

X_GROUPS = [[4 * x + o for x in range(4)] for o in range(4)]
CORE_GROUPS = [[2 * k, 2 * k + 1] for k in range(8)]
Z_SWAP = [(r, r ^ 2) for r in range(SIDE)]


def call(kernel, out_shape, *args, cost=None, scratch=(), smem=0):
    specs = [pl.BlockSpec(memory_space=pltpu.SMEM)] * smem
    specs += [pl.BlockSpec(memory_space=pltpu.VMEM)] * (len(args) - smem)
    single = isinstance(out_shape, jax.ShapeDtypeStruct)
    out_spec = pl.BlockSpec(memory_space=pltpu.VMEM)
    return pl.pallas_call(
        kernel,
        out_shape=out_shape,
        in_specs=specs,
        out_specs=out_spec if single else [out_spec] * len(out_shape),
        scratch_shapes=list(scratch),
        cost_estimate=cost,
        compiler_params=pltpu.CompilerParams(vmem_limit_bytes=VMEM_LIMIT),
    )(*args)


def array(shape, dtype):
    return jax.ShapeDtypeStruct(shape, dtype)


def one_hot_features():
    f = lax.broadcasted_iota(jnp.int32, (H, LANES), 0)
    lane = lax.broadcasted_iota(jnp.int32, (H, LANES), 1)
    hit = ((lane >> 3) == (f & 15)) & ((lane & 7) == (f >> 4))
    return jnp.where(hit, 1.0, 0.0).astype(LOW)


def one_hot_heads():
    h = lax.broadcasted_iota(jnp.int32, (H, LANES), 0)
    lane = lax.broadcasted_iota(jnp.int32, (H, LANES), 1)
    hit = ((lane >> 3) * PLACES + (lane & 7) == h) & ((lane & 7) < PLACES)
    return jnp.where(hit, 1.0, 0.0).astype(LOW)


def contract(a, b, a_dim, b_dim):
    return lax.dot_general(
        a, b, (((a_dim,), (b_dim,)), ((), ())), preferred_element_type=F32
    )


def swap_blocks(parts):
    rows = parts[0].shape[0]
    block = lax.broadcasted_iota(jnp.int32, (rows, LANES), 1) >> 3
    for s in (1, 2, 4, 8):
        low_half = (block & s) == 0
        out = list(parts)
        for a in range(SIDE):
            if a & s:
                continue
            b = a | s
            out[a] = jnp.where(low_half, parts[a], pltpu.roll(parts[b], 8 * s, 1))
            out[b] = jnp.where(low_half, pltpu.roll(parts[a], LANES - 8 * s, 1), parts[b])
        parts = out
    return parts


def prepare_kernel(q_ref, o_ref, k_ref, v_ref, qo_ref, kv_ref):
    hot = one_hot_features()
    q = (jnp.dot(q_ref[...], hot, preferred_element_type=F32) * (1.0 / HD**0.5)).astype(LOW)
    o = jnp.dot(o_ref[...], hot, preferred_element_type=F32).astype(LOW)
    for c in range(SIDE):
        qo_ref[c, :N_I, :] = q
        qo_ref[c, N_I:, :] = o
    kv_ref[:N_J, :] = jnp.dot(k_ref[...], hot, preferred_element_type=F32).astype(LOW)
    kv_ref[N_J:, :] = jnp.dot(v_ref[...], hot, preferred_element_type=F32).astype(LOW)


BIAS_ROWS = 384


def bias_kernel(pair_ref, w_ref, bias_ref, wide_ref):
    wide = jnp.dot(w_ref[...], one_hot_heads(), preferred_element_type=F32).astype(LOW)
    wide_ref[...] = wide
    bias_ref[...] = jnp.dot(pair_ref[...], wide, preferred_element_type=F32)


def pair_bias(flat_pair, w_bias):
    return pl.pallas_call(
        bias_kernel,
        grid=(CELLS // BIAS_ROWS,),
        in_specs=[
            pl.BlockSpec((BIAS_ROWS, P_SIZE), lambda i: (i, 0)),
            pl.BlockSpec((P_SIZE, H), lambda i: (0, 0)),
        ],
        out_specs=[
            pl.BlockSpec((BIAS_ROWS, LANES), lambda i: (i, 0)),
            pl.BlockSpec((P_SIZE, LANES), lambda i: (0, 0)),
        ],
        out_shape=[array((CELLS, LANES), F32), array((P_SIZE, LANES), LOW)],
        cost_estimate=pl.CostEstimate(
            flops=2 * CELLS * P_SIZE * LANES, bytes_accessed=4_000_000, transcendentals=0
        ),
    )(flat_pair, w_bias)


def pair_grad_kernel(score_ref, wide_ref, out_ref):
    out_ref[...] = contract(score_ref[...], wide_ref[...], 1, 1).astype(LOW)


def pair_grad(score, wide):
    return pl.pallas_call(
        pair_grad_kernel,
        grid=(CELLS // BIAS_ROWS,),
        in_specs=[
            pl.BlockSpec((BIAS_ROWS, LANES), lambda i: (i, 0)),
            pl.BlockSpec((P_SIZE, LANES), lambda i: (0, 0)),
        ],
        out_specs=pl.BlockSpec((BIAS_ROWS, P_SIZE), lambda i: (i, 0)),
        out_shape=array((CELLS, P_SIZE), LOW),
        cost_estimate=pl.CostEstimate(
            flops=2 * CELLS * P_SIZE * LANES, bytes_accessed=4_000_000, transcendentals=0
        ),
    )(score, wide)


def place_of(shape):
    return lax.broadcasted_iota(jnp.int32, shape, 1) & 7


def pack_stats(first, second):
    place = place_of((N_I, LANES))
    top = jnp.where(place < PLACES, first, pltpu.roll(second, 6, 1))
    half = N_I // 2
    place = place_of((half, LANES))
    middle = (place >= 2) & (place < PLACES)
    bottom = jnp.where(middle, second[:half], pltpu.roll(second[half:], 4, 1))
    return top, bottom


def unpack_stats(top, bottom):
    place = place_of((N_I, LANES))
    half = N_I // 2
    second = jnp.concatenate([bottom, pltpu.roll(bottom, LANES - 4, 1)], axis=0)
    second = jnp.where(place < 2, pltpu.roll(top, LANES - 6, 1), second)
    used = place < PLACES
    return jnp.where(used, top, 0.0), jnp.where(used, second, 0.0)


def scores_kernel(z_ref, qo_ref, kv_ref, bias_ref, e_ref, gp_ref, m_ref, stat_ref, q2_ref, o2_ref, k2_ref, v2_ref, lse_ref, delta_ref):
    z = z_ref[0]
    for t in range(N_I // 16):
        at = slice(16 * t, 16 * t + 16)
        for first, out in ((0, q2_ref), (N_I, o2_ref)):
            src = slice(first + 16 * t, first + 16 * t + 16)
            parts = swap_blocks([qo_ref[c, src, :].astype(F32) for c in range(SIDE)])
            for d in range(HD):
                out[d, at, :] = parts[d]
        for first, out in ((0, k2_ref), (N_J, v2_ref)):
            src = slice(first + 16 * t, first + 16 * t + 16)
            parts = swap_blocks(
                [kv_ref[r & 1, r >> 2, ((r >> 1) & 1) ^ z, src, :].astype(F32) for r in range(SIDE)]
            )
            for d in range(HD):
                out[d, at, :] = parts[d]

    def row(i, carry):
        at = pl.ds(pl.multiple_of(i * N_J, N_J), N_J)
        score = bias_ref[at, :]
        grad = jnp.zeros((N_J, LANES), F32)
        for d in range(HD):
            score = score + q2_ref[d, pl.ds(i, 1), :] * k2_ref[d]
            grad = grad + o2_ref[d, pl.ds(i, 1), :] * v2_ref[d]
        top = jnp.max(score, axis=0, keepdims=True)
        e = jnp.exp(score - top)
        total = jnp.sum(e, axis=0, keepdims=True)
        upper = jnp.sum(e * grad, axis=0, keepdims=True)
        e_ref[at, :] = e
        gp_ref[at, :] = grad
        m_ref[pl.ds(i, 1), :] = top
        lse_ref[pl.ds(i, 1), :] = top + jnp.log(total)
        delta_ref[pl.ds(i, 1), :] = upper / total
        return carry

    lax.fori_loop(0, N_I, row, 0)
    top, bottom = pack_stats(lse_ref[...], delta_ref[...])
    for c in range(SIDE):
        stat_ref[c, :N_I, :] = top
        stat_ref[c, N_I:, :] = bottom


def grad_kernel(stat_ref, m_ref, e_ref, gp_ref, pair_ref, score_ref, weight_ref, part_ref, factor_ref, delta_ref):
    stats = [unpack_stats(stat_ref[c, :N_I, :], stat_ref[c, N_I:, :]) for c in range(SIDE)]
    top = stats[0][0]
    for c in range(1, SIDE):
        top = jnp.maximum(top, stats[c][0])
    total = jnp.zeros((N_I, LANES), F32)
    upper = jnp.zeros((N_I, LANES), F32)
    for lse, delta in stats:
        share = jnp.exp(lse - top)
        total = total + share
        upper = upper + share * delta
    factor_ref[...] = jnp.exp(m_ref[...] - top) / total
    delta_ref[...] = upper / total

    def row(i, carry):
        at = pl.ds(pl.multiple_of(i * N_J, N_J), N_J)
        weight = e_ref[at, :] * factor_ref[pl.ds(i, 1), :]
        score = weight * (gp_ref[at, :] - delta_ref[pl.ds(i, 1), :])
        weight_ref[at, :] = weight.astype(LOW)
        score_ref[at, :] = score.astype(LOW)
        return carry

    lax.fori_loop(0, N_I, row, 0, unroll=2)
    term = contract(score_ref[...], pair_ref[...], 0, 0)
    for c in range(SIDE):
        rows = term[8 * c : 8 * c + 8]
        part_ref[c] = jnp.concatenate(
            [rows[:, LANES * t : LANES * (t + 1)] for t in range(P_SIZE // LANES)], axis=0
        ).astype(LOW)


D_BLOCK = 4


def weighted_sums(count, load, rows_ref, out_ref):
    for first in range(0, HD, D_BLOCK):

        def step(x, sums):
            tile = load(x)
            return tuple(
                s + tile * rows_ref[first + k, pl.ds(x, 1), :] for k, s in enumerate(sums)
            )

        zero = jnp.zeros((N_J, LANES), F32)
        sums = lax.fori_loop(0, count, step, (zero,) * D_BLOCK, unroll=2)
        for k in range(D_BLOCK):
            out_ref[first + k] = sums[k]


def store_blocks(sum_ref, out_ref, first):
    for t in range(N_J // 16):
        at = slice(16 * t, 16 * t + 16)
        parts = swap_blocks([sum_ref[d, at, :] for d in range(HD)])
        for c in range(SIDE):
            out_ref[c, first + 16 * t : first + 16 * t + 16, :] = parts[c].astype(LOW)


def key_kernel(score_ref, weight_ref, q2_ref, o2_ref, out_ref, sum_ref):
    def tile_of(ref):
        return lambda i: ref[pl.ds(pl.multiple_of(i * N_J, N_J), N_J), :].astype(F32)

    weighted_sums(N_I, tile_of(score_ref), q2_ref, sum_ref)
    store_blocks(sum_ref, out_ref, 0)
    weighted_sums(N_I, tile_of(weight_ref), o2_ref, sum_ref)
    store_blocks(sum_ref, out_ref, N_J)


def query_kernel(score_ref, k2_ref, out_ref, wide_ref, sum_ref):
    wide_ref[...] = score_ref[...].astype(F32)
    weighted_sums(N_J, lambda j: wide_ref[pl.ds(j, N_I, stride=N_J), :], k2_ref, sum_ref)
    store_blocks(sum_ref, out_ref, 0)


W_ROWS = 32


def row_send_kernel(part_ref, blocks_ref, out_ref):
    total = part_ref[0].astype(F32)
    for c in range(1, SIDE):
        total = total + part_ref[c].astype(F32)
    total = total.astype(LOW)
    for r in range(SIDE):
        out_ref[r, : 2 * N_J, :] = blocks_ref[r]
        out_ref[r, 2 * N_J :, :] = total


def from_block(x):
    return contract(x.astype(LOW), one_hot_features(), 1, 1).astype(LOW)


def row_sum_kernel(recv_ref, query_ref, key_ref, value_ref, out_ref):
    total = recv_ref[0].astype(F32)
    for r in range(1, SIDE):
        total = total + recv_ref[r].astype(F32)
    key_ref[...] = from_block(total[:N_J])
    value_ref[...] = from_block(total[N_J : 2 * N_J])
    shard = total[2 * N_J :].astype(LOW)
    for c in range(SIDE):
        out_ref[c, :W_ROWS, :] = shard
        out_ref[c, W_ROWS:, :] = query_ref[c]


def final_kernel(recv_ref, query_ref, w_ref, wide_ref):
    total = recv_ref[0, W_ROWS:, :].astype(F32)
    for c in range(1, SIDE):
        total = total + recv_ref[c, W_ROWS:, :].astype(F32)
    query_ref[...] = from_block(total * (1.0 / HD**0.5))
    for c in range(SIDE):
        rows = recv_ref[c, :W_ROWS, :].astype(F32)
        for t in range(P_SIZE // LANES):
            wide_ref[8 * c : 8 * c + 8, LANES * t : LANES * (t + 1)] = rows[8 * t : 8 * t + 8]
    w_ref[...] = contract(wide_ref[...].astype(LOW), one_hot_heads(), 0, 1)


def on_device(pair, w_bias, queries, keys, values, d_out):
    flat_pair = pair.reshape(CELLS, P_SIZE)
    qo_send, kv_own = call(
        prepare_kernel,
        [array((SIDE, 2 * N_I, LANES), LOW), array((2 * N_J, LANES), LOW)],
        queries, d_out, keys, values,
    )
    kv_other = lax.ppermute(kv_own, "row", Z_SWAP)
    qo = lax.all_to_all(qo_send, "col", 0, 0)
    bias, wide = pair_bias(flat_pair, w_bias)
    kv_both = jnp.stack([kv_own, kv_other])
    kv = lax.all_to_all(
        jnp.broadcast_to(kv_both[None], (4,) + kv_both.shape), "row", 0, 0, axis_index_groups=X_GROUPS
    )
    kv = lax.all_gather(kv, "row", axis_index_groups=CORE_GROUPS)
    z = ((lax.axis_index("row") >> 1) & 1).astype(jnp.int32).reshape(1)
    feature = array((HD, N_I, LANES), F32)
    e, gp, own_max, stats, q2, o2, k2, v2 = call(
        scores_kernel,
        [array((CELLS, LANES), F32)] * 2
        + [array((N_I, LANES), F32), array((SIDE, 72, LANES), F32)]
        + [feature] * 4,
        z, qo, kv, bias,
        smem=1,
        scratch=[pltpu.VMEM((N_I, LANES), F32)] * 2,
    )
    del v2
    stats = lax.all_to_all(stats, "col", 0, 0)
    score, weight, part = call(
        grad_kernel,
        [array((CELLS, LANES), LOW)] * 2 + [array((SIDE, W_ROWS, LANES), LOW)],
        stats, own_max, e, gp, flat_pair,
        scratch=[pltpu.VMEM((N_I, LANES), F32)] * 2,
    )
    part = lax.all_to_all(part, "col", 0, 0)
    vpu_cost = pl.CostEstimate(flops=4_000_000_000, bytes_accessed=4_000_000, transcendentals=0)
    key_blocks = call(
        key_kernel,
        array((SIDE, 2 * N_J, LANES), LOW),
        score, weight, q2, o2,
        scratch=[pltpu.VMEM((HD, N_J, LANES), F32)],
        cost=vpu_cost,
    )
    row_send = call(
        row_send_kernel, array((SIDE, 2 * N_J + W_ROWS, LANES), LOW), part, key_blocks
    )
    row_recv = lax.all_to_all(row_send, "row", 0, 0)
    query_blocks = call(
        query_kernel,
        array((SIDE, N_I, LANES), LOW),
        score, k2,
        scratch=[pltpu.VMEM((CELLS, LANES), F32), pltpu.VMEM((HD, N_I, LANES), F32)],
        cost=vpu_cost,
    )
    d_pair = pair_grad(score, wide)
    d_keys, d_values, col_send = call(
        row_sum_kernel,
        [array((N_J, H), LOW)] * 2 + [array((SIDE, W_ROWS + N_I, LANES), LOW)],
        row_recv, query_blocks,
    )
    col_recv = lax.all_to_all(col_send, "col", 0, 0)
    d_queries, d_wbias = call(
        final_kernel,
        [array((N_I, H), LOW), array((P_SIZE, H), F32)],
        col_recv,
        scratch=[pltpu.VMEM((LANES, P_SIZE), F32)],
    )
    return d_pair.reshape(pair.shape), d_wbias, d_queries, d_keys, d_values


def solution(mesh):
    return jax.shard_map(
        on_device,
        mesh=mesh,
        in_specs=(
            P("row", "col", None),
            P(),
            P("row", "col"),
            P("col", "row"),
            P("col", "row"),
            P("row", "col"),
        ),
        out_specs=(P("row", "col", None), P(), P("row", "col"), P("col", "row"), P("col", "row")),
        check_vma=False,
    )
```

time: 600 us -> 135 us (0.23)
  waiting for transfers between devices: 273 us -> 20.9 us
  blocking collectives: 260 us -> 38.4 us
  Pallas kernels: 0 us -> 35.4 us
  starting transfers between devices: 0.17 us -> 33.8 us
  matrix products: 21.9 us -> 0 us
  local copies, waits for them, and re-layouts: 21.7 us -> 4.42 us
  between operations: 15.3 us -> 0.71 us
  other arithmetic: 7.86 us -> 0.01 us
    unnamed x7 -> x0, waiting for transfers between devices: 242 us -> none
    all_gather x4 -> x1, blocking collectives: 135 us -> 5.24 us  [on_device(): kv = lax.all_gather(kv, 'row', axis_index_groups=CORE_GROUPS)]
    pmax x1 -> x0, blocking collectives: 62.7 us -> none  [on_device(): row_max = lax.pmax(jnp.max(scores, axis=-1), 'col')]
    psum x1 -> x0, blocking collectives: 62 us -> none  [on_device(): lax.psum((jnp.sum(exp_scores, axis=-1), jnp.sum(exp_scores * grad_prob, a...]
    pallas_call x0 -> x10, Pallas kernels: none -> 35.4 us  [the longest x8 24.4 us: call(): pl.pallas_call(kernel, out_shape=out_shape, in_specs=specs, out_specs=out...]
    all_to_all x0 -> x2, blocking collectives: none -> 33.2 us  [the longest x1 24.2 us: on_device(): stats = lax.all_to_all(stats, 'col', 0, 0)]
    psum x1 -> x0, waiting for transfers between devices: 30.5 us -> none  [on_device(): d_wbias = lax.psum(weight_term, ('row', 'col'))]
    all_to_all x0 -> x4, starting transfers between devices: none -> 26.1 us  [the longest x1 8.62 us: on_device(): row_recv = lax.all_to_all(row_send, 'row', 0, 0)]
  transfers between devices with their start and end apart: 4 -> 5, of which waited for: 4 -> 4; matrix products, arithmetic and copies ran while one was open for 3% -> 1% of each run, Pallas kernels for 0% -> 15%
where the time goes in v2:
time: 135 us; the launch traced here: 134 us
  blocking collectives  38.4 us (28%)
  Pallas kernels  35.4 us (26%)
  starting transfers between devices  33.8 us (25%)
  waiting for transfers between devices  20.9 us (15%)
  local copies, waits for them, and re-layouts  4.42 us (3%)
    pallas_call x8, Pallas kernels, call(): pl.pallas_call(kernel, out_shape=out_shape, in_specs=specs, out_specs=out...  24.4 us
    all_to_all x1, blocking collectives, on_device(): stats = lax.all_to_all(stats, 'col', 0, 0)  24.2 us
    all_to_all x1, waiting for transfers between devices, on_device(): row_recv = lax.all_to_all(row_send, 'row', 0, 0)  11.8 us
    all_to_all x1, blocking collectives, on_device(): lax.all_to_all(jnp.broadcast_to(kv_both[None], (4,) + kv_both.shape), 'ro...  9 us
    all_to_all x1, starting transfers between devices, on_device(): row_recv = lax.all_to_all(row_send, 'row', 0, 0)  8.62 us
    ppermute x1, starting transfers between devices, on_device(): kv_other = lax.ppermute(kv_own, 'row', Z_SWAP)  7.73 us
    all_to_all x1, starting transfers between devices, on_device(): qo = lax.all_to_all(qo_send, 'col', 0, 0)  6.81 us
    all_to_all x1, starting transfers between devices, on_device(): col_recv = lax.all_to_all(col_send, 'col', 0, 0)  6.54 us
  transfers between devices with their start and end apart: 5, of which 4 were waited for; matrix products, arithmetic and copies ran while one was open for 1% of the time, Pallas kernels for 15%

profile of v2, /device:TPU:1, one launch (start us, length us, event | category | flops | bytes accessed | tf_op | source)
XLA Modules:
  0.0 133.7 jit_solution(8023905030126751101)
XLA Ops:
  0.6 0.0 copy-start.1
  0.6 0.7 copy-done.1
  1.3 0.0 copy-start.2
  1.3 0.7 copy-done.2
  2.0 0.0 copy-start.3
  2.1 0.7 copy-done.3
  2.8 0.0 copy-start.4
  2.8 0.7 copy-done.4
  3.5 0.0 copy-start.5
  3.5 0.9 shard_map.101
  4.4 7.7 %collective-permute-start = (bf16[96,128]{1,0:T(8,128)(2,1)S(1)}, bf16[96,128]{1,0:T(8,128)(2,1)S(1)}, u32[]{:S(2)}, u32[]{:S(2)}) collective-permute-start(bf16[96,128]{1,0:T(8,128)(2,1)S(1)} %get-tuple-element.25), channel_id=1, source_target_pairs={{0,32},{16,48},{32,0},{48,16},{64,96},{80,112},{96,64},{112,80},{1... | collective-permute-start | bytes 73736 | tf_op jit(solution)/shard_map/ppermute | solution.py:328
  12.1 1.2 collective-permute-done
  13.4 9.0 %all_to_all.30 = bf16[4,2,96,128]{3,2,1,0:T(8,128)(2,1)S(1)} all-to-all(bf16[4,2,96,128]{3,2,1,0:T(8,128)(2,1)S(1)} %broadcast_in_dim.2), channel_id=1, replica_groups={{0,64,128,192},{16,80,144,208},{32,96,160,224},{48,112,176,240},{1,65,1..., dimensions={0} | all-to-all | bytes 393216 | tf_op jit(solution)/shard_map/all_to_all | solution.py:332
  22.4 6.8 %all-to-all-start = ((bf16[16,96,128]{2,1,0:T(8,128)(2,1)}), bf16[16,96,128]{2,1,0:T(8,128)(2,1)S(1)}, u32[]{:S(2)}, u32[]{:S(2)}) async-start(bf16[16,96,128]{2,1,0:T(8,128)(2,1)} %get-tuple-element.24), calls=%async_computation | async-start | bytes 786432 | tf_op jit(solution)/shard_map/all_to_all | solution.py:329
  29.2 0.0 copy-done.5
  29.2 0.8 copy.13.w_ref
  30.0 5.8 %shard_map.102 = (f32[2304,128]{1,0:T(8,128)}, bf16[512,128]{1,0:T(8,128)(2,1)}) custom-call(bf16[2304,512]{1,0:T(8,128)(2,1)} %bitcast.8, bf16[512,96]{1,0:T(8,128)(2,1)} %copy.13.w_ref), custom_call_target="tpu_custom_call" | custom-call | flops 301989888 | bytes 4000000 | tf_op jit(solution)/shard_map/pallas_call | solution.py:104
  35.7 5.2 %all-gather = bf16[8,2,96,128]{3,2,1,0:T(8,128)(2,1)S(1)} all-gather(bf16[4,2,96,128]{3,2,1,0:T(8,128)(2,1)S(1)} %all_to_all.30), channel_id=2, replica_groups={{0,16},{32,48},{64,80},{96,112},{128,144},{160,176},{192,208},{224,240}..., dimensions={0}, use_global_device_ids=true | all-gather | bytes 589824 | tf_op jit(solution)/shard_map/all_gather | solution.py:335
  41.0 0.0 all-to-all-done.qo_ref
  41.0 8.4 %shard_map.103 = (f32[2304,128]{1,0:T(8,128)S(1)}, f32[2304,128]{1,0:T(8,128)S(1)}, f32[48,128]{1,0:T(8,128)S(1)}, f32[16,72,128]{2,1,0:T(8,128)S(1)}, f32[16,48...) custom-call(s32[1]{0:T(128)} %bitcast.z_ref, ...), custom_call_target="tpu_custom_call" | custom-call | tf_op jit(solution)/shard_map/pallas_call | solution.py:32
  49.4 24.2 %all_to_all.31.stat_ref = f32[16,72,128]{2,1,0:T(8,128)S(1)} all-to-all(f32[16,72,128]{2,1,0:T(8,128)S(1)} %get-tuple-element.27), channel_id=1, replica_groups=mesh['row'=16,'col'=16] {'col'}, dimensions={0} | all-to-all | bytes 1179648 | tf_op jit(solution)/shard_map/all_to_all | solution.py:348
  73.6 3.3 %shard_map.104 = (bf16[2304,128]{1,0:T(8,128)(2,1)S(1)}, bf16[2304,128]{1,0:T(8,128)(2,1)S(1)}, bf16[16,32,128]{2,1,0:T(8,128)(2,1)}) custom-call(f32[16,72,128]{2,1,0:T(8,128)S(1)} %all_to_all.31.stat_ref, f32[48,128]{1,0:T(8,128)S(1)} %get-tuple-element.28.m_ref, f32[2304,128]{1,0:T(8,128)S(1)} %get-tuple-element.29.e_ref, ...), custom_call_target="tpu_custom_call" | custom-call | tf_op jit(solution)/shard_map/pallas_call | solution.py:32
  76.9 0.0 copy-start
  76.9 4.1 %all-to-all-start.3 = ((bf16[16,32,128]{2,1,0:T(8,128)(2,1)}), bf16[16,32,128]{2,1,0:T(8,128)(2,1)S(1)}, u32[]{:S(2)}, u32[]{:S(2)}) async-start(bf16[16,32,128]{2,1,0:T(8,128)(2,1)} %get-tuple-element.33), calls=%async_computation.3 | async-start | bytes 262144 | tf_op jit(solution)/shard_map/all_to_all | solution.py:355
  81.0 5.1 %shard_map.106.blocks_ref = bf16[16,96,128]{2,1,0:T(8,128)(2,1)S(1)} custom-call(bf16[2304,128]{1,0:T(8,128)(2,1)S(1)} %get-tuple-element.31.score_ref, bf16[2304,128]{1,0:T(8,128)(2,1)S(1)} %get-tuple-element.34.weight_ref, f32[16,48,128]{2,1,0:T(8,128)S(1)} %get-tuple-element.35.q2_ref, f32[16,48,128]{2,1,0:T(8,128)S(1)} %get-tuple-element.36.o2_ref), custom_call_target="tpu_custom_call" | custom-call | flops 4000000000 | bytes 4000000 | tf_op jit(solution)/shard_map/pallas_call | solution.py:32
  86.2 2.1 %all-to-all-done.3.part_ref = bf16[16,32,128]{2,1,0:T(8,128)(2,1)S(1)} async-done(((bf16[16,32,128]{2,1,0:T(8,128)(2,1)}), bf16[16,32,128]{2,1,0:T(8,128)(2,1)S(1)}, u32[]{:S(2)}, u32[]{:S(2)}) %all-to-all-start.3) | async-done | bytes 131104 | tf_op jit(solution)/shard_map/all_to_all | solution.py:355
  88.3 0.8 shard_map.107
  89.1 8.6 %all-to-all-start.4 = ((bf16[16,128,128]{2,1,0:T(8,128)(2,1)}), bf16[16,128,128]{2,1,0:T(8,128)(2,1)S(1)}, u32[]{:S(2)}, u32[]{:S(2)}) async-start(bf16[16,128,128]{2,1,0:T(8,128)(2,1)} %shard_map.107), calls=%async_computation.4 | async-start | bytes 1048576 | tf_op jit(solution)/shard_map/all_to_all | solution.py:367
  97.7 0.0 copy-done
  97.7 4.0 %shard_map.108.query_ref = bf16[16,48,128]{2,1,0:T(8,128)(2,1)S(1)} custom-call(bf16[2304,128]{1,0:T(8,128)(2,1)S(1)} %get-tuple-element.31.score_ref, f32[16,48,128]{2,1,0:T(8,128)S(1)} %get-tuple-element.37.k2_ref), custom_call_target="tpu_custom_call" | custom-call | flops 4000000000 | bytes 4000000 | tf_op jit(solution)/shard_map/pallas_call | solution.py:32
  101.8 11.8 %all-to-all-done.4.recv_ref = bf16[16,128,128]{2,1,0:T(8,128)(2,1)S(1)} async-done(((bf16[16,128,128]{2,1,0:T(8,128)(2,1)}), bf16[16,128,128]{2,1,0:T(8,128)(2,1)S(1)}, u32[]{:S(2)}, u32[]{:S(2)}) %all-to-all-start.4) | async-done | bytes 524320 | tf_op jit(solution)/shard_map/all_to_all | solution.py:367
  113.6 0.9 shard_map.109
  114.5 6.5 %all-to-all-start.5 = ((bf16[16,80,128]{2,1,0:T(8,128)(2,1)}), bf16[16,80,128]{2,1,0:T(8,128)(2,1)S(1)}, u32[]{:S(2)}, u32[]{:S(2)}) async-start(bf16[16,80,128]{2,1,0:T(8,128)(2,1)} %get-tuple-element.38), calls=%async_computation.5 | async-start | bytes 655360 | tf_op jit(solution)/shard_map/all_to_all | solution.py:381
  121.1 5.2 %shard_map.105 = bf16[2304,512]{1,0:T(8,128)(2,1)} custom-call(bf16[2304,128]{1,0:T(8,128)(2,1)} %copy-done, bf16[512,128]{1,0:T(8,128)(2,1)} %get-tuple-element.32.wide_ref), custom_call_target="tpu_custom_call" | custom-call | flops 301989888 | bytes 4000000 | tf_op jit(solution)/shard_map/pallas_call | solution.py:127
  126.3 5.8 %all-to-all-done.5.recv_ref = bf16[16,80,128]{2,1,0:T(8,128)(2,1)S(1)} async-done(((bf16[16,80,128]{2,1,0:T(8,128)(2,1)}), bf16[16,80,128]{2,1,0:T(8,128)(2,1)S(1)}, u32[]{:S(2)}, u32[]{:S(2)}) %all-to-all-start.5) | async-done | bytes 327712 | tf_op jit(solution)/shard_map/all_to_all | solution.py:381
  132.1 0.8 shard_map.110
  132.9 0.8 copy.14
  (2 shorter events, 0.0 us)
Async XLA Ops:
  0.6 0.7 copy-start.1
  1.3 0.7 copy-start.2
  2.0 0.7 copy-start.3
  2.8 0.7 copy-start.4
  3.5 25.7 %copy-start.5 = (bf16[512,96]{0,1:T(8,128)(2,1)S(1)}, bf16[512,96]{0,1:T(8,128)(2,1)}, u32[]{:S(2)}) copy-start(bf16[512,96]{0,1:T(8,128)(2,1)} %param.7) | copy-start | bytes 294916
  4.4 8.9 %collective-permute-start = (bf16[96,128]{1,0:T(8,128)(2,1)S(1)}, bf16[96,128]{1,0:T(8,128)(2,1)S(1)}, u32[]{:S(2)}, u32[]{:S(2)}) collective-permute-start(bf16[96,128]{1,0:T(8,128)(2,1)S(1)} %get-tuple-element.25), channel_id=1, source_target_pairs={{0,32},{16,48},{32,0},{48,16},{64,96},{80,112},{96,64},{112,80},{1... | collective-permute-start | bytes 73736 | tf_op jit(solution)/shard_map/ppermute | solution.py:328
  22.4 18.6 %all-to-all-start = ((bf16[16,96,128]{2,1,0:T(8,128)(2,1)}), bf16[16,96,128]{2,1,0:T(8,128)(2,1)S(1)}, u32[]{:S(2)}, u32[]{:S(2)}) async-start(bf16[16,96,128]{2,1,0:T(8,128)(2,1)} %get-tuple-element.24), calls=%async_computation | async-start | bytes 786432 | tf_op jit(solution)/shard_map/all_to_all | solution.py:329
  76.9 20.8 %copy-start = (bf16[2304,128]{1,0:T(8,128)(2,1)}, bf16[2304,128]{1,0:T(8,128)(2,1)S(1)}, u32[]{:S(2)}) copy-start(bf16[2304,128]{1,0:T(8,128)(2,1)S(1)} %get-tuple-element.31.score_ref) | copy-start | bytes 1769476
  76.9 11.4 %all-to-all-start.3 = ((bf16[16,32,128]{2,1,0:T(8,128)(2,1)}), bf16[16,32,128]{2,1,0:T(8,128)(2,1)S(1)}, u32[]{:S(2)}, u32[]{:S(2)}) async-start(bf16[16,32,128]{2,1,0:T(8,128)(2,1)} %get-tuple-element.33), calls=%async_computation.3 | async-start | bytes 262144 | tf_op jit(solution)/shard_map/all_to_all | solution.py:355
  89.1 24.5 %all-to-all-start.4 = ((bf16[16,128,128]{2,1,0:T(8,128)(2,1)}), bf16[16,128,128]{2,1,0:T(8,128)(2,1)S(1)}, u32[]{:S(2)}, u32[]{:S(2)}) async-start(bf16[16,128,128]{2,1,0:T(8,128)(2,1)} %shard_map.107), calls=%async_computation.4 | async-start | bytes 1048576 | tf_op jit(solution)/shard_map/all_to_all | solution.py:367
  114.5 17.6 %all-to-all-start.5 = ((bf16[16,80,128]{2,1,0:T(8,128)(2,1)}), bf16[16,80,128]{2,1,0:T(8,128)(2,1)S(1)}, u32[]{:S(2)}, u32[]{:S(2)}) async-start(bf16[16,80,128]{2,1,0:T(8,128)(2,1)} %get-tuple-element.38), calls=%async_computation.5 | async-start | bytes 655360 | tf_op jit(solution)/shard_map/all_to_all | solution.py:381

commit v3 on v2

--- a/solution.py
+++ b/solution.py
@@ -80,8 +80,18 @@
     return parts
 
 
-def prepare_kernel(q_ref, o_ref, k_ref, v_ref, qo_ref, kv_ref):
+def prepare_kernel(q_hbm, o_hbm, k_hbm, v_hbm, qo_ref, kv_ref, q_ref, o_ref, k_ref, v_ref, sems):
+    copies = [
+        pltpu.make_async_copy(src, dst, sems.at[n])
+        for n, (src, dst) in enumerate(
+            ((q_hbm, q_ref), (o_hbm, o_ref), (k_hbm, k_ref), (v_hbm, v_ref))
+        )
+    ]
+    for copy in copies:
+        copy.start()
     hot = one_hot_features()
+    for copy in copies:
+        copy.wait()
     q = (jnp.dot(q_ref[...], hot, preferred_element_type=F32) * (1.0 / HD**0.5)).astype(LOW)
     o = jnp.dot(o_ref[...], hot, preferred_element_type=F32).astype(LOW)
     for c in range(SIDE):
@@ -91,79 +101,38 @@
     kv_ref[N_J:, :] = jnp.dot(v_ref[...], hot, preferred_element_type=F32).astype(LOW)
 
 
-BIAS_ROWS = 384
-
-
-def bias_kernel(pair_ref, w_ref, bias_ref, wide_ref):
-    wide = jnp.dot(w_ref[...], one_hot_heads(), preferred_element_type=F32).astype(LOW)
-    wide_ref[...] = wide
-    bias_ref[...] = jnp.dot(pair_ref[...], wide, preferred_element_type=F32)
-
-
-def pair_bias(flat_pair, w_bias):
-    return pl.pallas_call(
-        bias_kernel,
-        grid=(CELLS // BIAS_ROWS,),
-        in_specs=[
-            pl.BlockSpec((BIAS_ROWS, P_SIZE), lambda i: (i, 0)),
-            pl.BlockSpec((P_SIZE, H), lambda i: (0, 0)),
-        ],
-        out_specs=[
-            pl.BlockSpec((BIAS_ROWS, LANES), lambda i: (i, 0)),
-            pl.BlockSpec((P_SIZE, LANES), lambda i: (0, 0)),
-        ],
-        out_shape=[array((CELLS, LANES), F32), array((P_SIZE, LANES), LOW)],
-        cost_estimate=pl.CostEstimate(
-            flops=2 * CELLS * P_SIZE * LANES, bytes_accessed=4_000_000, transcendentals=0
-        ),
-    )(flat_pair, w_bias)
-
-
-def pair_grad_kernel(score_ref, wide_ref, out_ref):
-    out_ref[...] = contract(score_ref[...], wide_ref[...], 1, 1).astype(LOW)
-
-
-def pair_grad(score, wide):
-    return pl.pallas_call(
-        pair_grad_kernel,
-        grid=(CELLS // BIAS_ROWS,),
-        in_specs=[
-            pl.BlockSpec((BIAS_ROWS, LANES), lambda i: (i, 0)),
-            pl.BlockSpec((P_SIZE, LANES), lambda i: (0, 0)),
-        ],
-        out_specs=pl.BlockSpec((BIAS_ROWS, P_SIZE), lambda i: (i, 0)),
-        out_shape=array((CELLS, P_SIZE), LOW),
-        cost_estimate=pl.CostEstimate(
-            flops=2 * CELLS * P_SIZE * LANES, bytes_accessed=4_000_000, transcendentals=0
-        ),
-    )(score, wide)
-
-
 def place_of(shape):
     return lax.broadcasted_iota(jnp.int32, shape, 1) & 7
 
 
-def pack_stats(first, second):
+def pack_stats(first, second, third):
     place = place_of((N_I, LANES))
-    top = jnp.where(place < PLACES, first, pltpu.roll(second, 6, 1))
-    half = N_I // 2
-    place = place_of((half, LANES))
-    middle = (place >= 2) & (place < PLACES)
-    bottom = jnp.where(middle, second[:half], pltpu.roll(second[half:], 4, 1))
-    return top, bottom
-
-
-def unpack_stats(top, bottom):
+    top = jnp.where(place < PLACES, first, pltpu.roll(third, 6, 1))
+    middle = jnp.where(place < PLACES, second, pltpu.roll(third, 4, 1))
+    place = place_of((16, LANES))
+    bottom = jnp.where(
+        place < 2,
+        pltpu.roll(third[32:48], LANES - 4, 1),
+        jnp.where(place < PLACES, third[:16], pltpu.roll(third[16:32], 2, 1)),
+    )
+    return top, middle, bottom
+
+
+def unpack_stats(top, middle, bottom):
     place = place_of((N_I, LANES))
-    half = N_I // 2
-    second = jnp.concatenate([bottom, pltpu.roll(bottom, LANES - 4, 1)], axis=0)
-    second = jnp.where(place < 2, pltpu.roll(top, LANES - 6, 1), second)
+    third = jnp.concatenate(
+        [bottom, pltpu.roll(bottom, LANES - 2, 1), pltpu.roll(bottom, 4, 1)], axis=0
+    )
+    third = jnp.where(place < 4, pltpu.roll(middle, LANES - 4, 1), third)
+    third = jnp.where(place < 2, pltpu.roll(top, LANES - 6, 1), third)
     used = place < PLACES
-    return jnp.where(used, top, 0.0), jnp.where(used, second, 0.0)
-
-
-def scores_kernel(z_ref, qo_ref, kv_ref, bias_ref, e_ref, gp_ref, m_ref, stat_ref, q2_ref, o2_ref, k2_ref, v2_ref, lse_ref, delta_ref):
-    z = z_ref[0]
+    return tuple(jnp.where(used, x, 0.0) for x in (top, middle, third))
+
+
+STAT_ROWS = 2 * N_I + 16
+
+
+def rows_kernel(qo_ref, q2_ref, o2_ref):
     for t in range(N_I // 16):
         at = slice(16 * t, 16 * t + 16)
         for first, out in ((0, q2_ref), (N_I, o2_ref)):
@@ -171,6 +140,12 @@
             parts = swap_blocks([qo_ref[c, src, :].astype(F32) for c in range(SIDE)])
             for d in range(HD):
                 out[d, at, :] = parts[d]
+
+
+def scores_kernel(z_ref, q2_ref, o2_ref, kv_ref, bias_ref, e_ref, gp_ref, own_ref, stat_ref, k2_ref, v2_ref):
+    z = z_ref[0]
+    for t in range(N_J // 16):
+        at = slice(16 * t, 16 * t + 16)
         for first, out in ((0, k2_ref), (N_J, v2_ref)):
             src = slice(first + 16 * t, first + 16 * t + 16)
             parts = swap_blocks(
@@ -179,49 +154,66 @@
             for d in range(HD):
                 out[d, at, :] = parts[d]
 
-    def row(i, carry):
-        at = pl.ds(pl.multiple_of(i * N_J, N_J), N_J)
-        score = bias_ref[at, :]
-        grad = jnp.zeros((N_J, LANES), F32)
+    def rows(pair_at, carry):
+        here = [2 * pair_at, 2 * pair_at + 1]
+        at = [pl.ds(pl.multiple_of(i * N_J, N_J), N_J) for i in here]
+        score = [bias_ref[a, :] for a in at]
+        grad = [jnp.zeros((N_J, LANES), F32) for a in at]
         for d in range(HD):
-            score = score + q2_ref[d, pl.ds(i, 1), :] * k2_ref[d]
-            grad = grad + o2_ref[d, pl.ds(i, 1), :] * v2_ref[d]
-        top = jnp.max(score, axis=0, keepdims=True)
-        e = jnp.exp(score - top)
-        total = jnp.sum(e, axis=0, keepdims=True)
-        upper = jnp.sum(e * grad, axis=0, keepdims=True)
-        e_ref[at, :] = e
-        gp_ref[at, :] = grad
-        m_ref[pl.ds(i, 1), :] = top
-        lse_ref[pl.ds(i, 1), :] = top + jnp.log(total)
-        delta_ref[pl.ds(i, 1), :] = upper / total
+            k, v = k2_ref[d], v2_ref[d]
+            for n, i in enumerate(here):
+                score[n] = score[n] + q2_ref[d, pl.ds(i, 1), :] * k
+                grad[n] = grad[n] + o2_ref[d, pl.ds(i, 1), :] * v
+        for n, i in enumerate(here):
+            shift = jnp.max(score[n], axis=0, keepdims=True).astype(LOW).astype(F32)
+            e = jnp.exp(score[n] - shift)
+            total = jnp.sum(e, axis=0, keepdims=True)
+            upper = jnp.sum(e * grad[n], axis=0, keepdims=True)
+            e_ref[at[n], :] = e
+            gp_ref[at[n], :] = grad[n]
+            own_ref[0, pl.ds(i, 1), :] = shift
+            own_ref[1, pl.ds(i, 1), :] = total
+            own_ref[2, pl.ds(i, 1), :] = upper / total
         return carry
 
-    lax.fori_loop(0, N_I, row, 0)
-    top, bottom = pack_stats(lse_ref[...], delta_ref[...])
+    lax.fori_loop(0, N_I // 2, rows, 0)
+    packed = [x.astype(LOW) for x in pack_stats(own_ref[0], own_ref[1], own_ref[2])]
     for c in range(SIDE):
-        stat_ref[c, :N_I, :] = top
-        stat_ref[c, N_I:, :] = bottom
-
-
-def grad_kernel(stat_ref, m_ref, e_ref, gp_ref, pair_ref, score_ref, weight_ref, part_ref, factor_ref, delta_ref):
-    stats = [unpack_stats(stat_ref[c, :N_I, :], stat_ref[c, N_I:, :]) for c in range(SIDE)]
+        stat_ref[c, :N_I, :] = packed[0]
+        stat_ref[c, N_I : 2 * N_I, :] = packed[1]
+        stat_ref[c, 2 * N_I :, :] = packed[2]
+
+
+def grad_kernel(stat_ref, own_ref, e_ref, gp_ref, pair_ref, score_ref, weight_ref, part_ref, factor_ref, offset_ref):
+    def stats_of(c):
+        return unpack_stats(
+            stat_ref[c, :N_I, :].astype(F32),
+            stat_ref[c, N_I : 2 * N_I, :].astype(F32),
+            stat_ref[c, 2 * N_I :, :].astype(F32),
+        )
+
+    used = place_of((N_I, LANES)) < PLACES
+    shift, own_total, own_delta = own_ref[0], own_ref[1], own_ref[2]
+    stats = [stats_of(c) for c in range(SIDE)]
     top = stats[0][0]
     for c in range(1, SIDE):
         top = jnp.maximum(top, stats[c][0])
-    total = jnp.zeros((N_I, LANES), F32)
-    upper = jnp.zeros((N_I, LANES), F32)
-    for lse, delta in stats:
-        share = jnp.exp(lse - top)
+    own_scale = jnp.exp(shift - top)
+    low_total = own_total.astype(LOW).astype(F32)
+    low_delta = own_delta.astype(LOW).astype(F32)
+    total = own_scale * (own_total - low_total)
+    offset = -own_scale * low_total * (own_delta - low_delta)
+    for other_shift, other_total, other_delta in stats:
+        share = jnp.exp(other_shift - top) * other_total
         total = total + share
-        upper = upper + share * delta
-    factor_ref[...] = jnp.exp(m_ref[...] - top) / total
-    delta_ref[...] = upper / total
+        offset = offset + share * (own_delta - other_delta)
+    factor_ref[...] = jnp.where(used, own_scale / total, 0.0)
+    offset_ref[...] = jnp.where(used, offset / total, 0.0)
 
     def row(i, carry):
         at = pl.ds(pl.multiple_of(i * N_J, N_J), N_J)
         weight = e_ref[at, :] * factor_ref[pl.ds(i, 1), :]
-        score = weight * (gp_ref[at, :] - delta_ref[pl.ds(i, 1), :])
+        score = weight * ((gp_ref[at, :] - own_ref[2, pl.ds(i, 1), :]) + offset_ref[pl.ds(i, 1), :])
         weight_ref[at, :] = weight.astype(LOW)
         score_ref[at, :] = score.astype(LOW)
         return carry
@@ -315,41 +307,51 @@
         rows = recv_ref[c, :W_ROWS, :].astype(F32)
         for t in range(P_SIZE // LANES):
             wide_ref[8 * c : 8 * c + 8, LANES * t : LANES * (t + 1)] = rows[8 * t : 8 * t + 8]
-    w_ref[...] = contract(wide_ref[...].astype(LOW), one_hot_heads(), 0, 1)
+    w_ref[...] = contract(one_hot_heads(), wide_ref[...].astype(LOW), 1, 0)
 
 
 def on_device(pair, w_bias, queries, keys, values, d_out):
     flat_pair = pair.reshape(CELLS, P_SIZE)
-    qo_send, kv_own = call(
+    own = pltpu.VMEM((N_I, H), LOW)
+    qo_send, kv_own = pl.pallas_call(
         prepare_kernel,
-        [array((SIDE, 2 * N_I, LANES), LOW), array((2 * N_J, LANES), LOW)],
-        queries, d_out, keys, values,
-    )
+        out_shape=[array((SIDE, 2 * N_I, LANES), LOW), array((2 * N_J, LANES), LOW)],
+        in_specs=[pl.BlockSpec(memory_space=pl.ANY)] * 4,
+        out_specs=[pl.BlockSpec(memory_space=pltpu.VMEM)] * 2,
+        scratch_shapes=[own] * 4 + [pltpu.SemaphoreType.DMA((4,))],
+    )(queries, d_out, keys, values)
     kv_other = lax.ppermute(kv_own, "row", Z_SWAP)
     qo = lax.all_to_all(qo_send, "col", 0, 0)
-    bias, wide = pair_bias(flat_pair, w_bias)
+    wide = jnp.pad(w_bias.T.reshape(SIDE, PLACES, P_SIZE), ((0, 0), (0, 2), (0, 0)))
+    wide = wide.reshape(LANES, P_SIZE)
+    bias = contract(flat_pair, wide, 1, 1)
     kv_both = jnp.stack([kv_own, kv_other])
-    kv = lax.all_to_all(
-        jnp.broadcast_to(kv_both[None], (4,) + kv_both.shape), "row", 0, 0, axis_index_groups=X_GROUPS
+    kv_send = jnp.broadcast_to(kv_both[None], (4,) + kv_both.shape)
+    kv_send, qo = lax.optimization_barrier((kv_send, qo))
+    kv = lax.all_to_all(kv_send, "row", 0, 0, axis_index_groups=X_GROUPS)
+    feature = array((HD, N_I, LANES), F32)
+    q2, o2 = call(
+        rows_kernel,
+        [feature] * 2,
+        qo,
+        cost=pl.CostEstimate(flops=1_000_000_000, bytes_accessed=2_000_000, transcendentals=0),
     )
     kv = lax.all_gather(kv, "row", axis_index_groups=CORE_GROUPS)
     z = ((lax.axis_index("row") >> 1) & 1).astype(jnp.int32).reshape(1)
-    feature = array((HD, N_I, LANES), F32)
-    e, gp, own_max, stats, q2, o2, k2, v2 = call(
+    e, gp, own_stats, stats, k2, v2 = call(
         scores_kernel,
         [array((CELLS, LANES), F32)] * 2
-        + [array((N_I, LANES), F32), array((SIDE, 72, LANES), F32)]
-        + [feature] * 4,
-        z, qo, kv, bias,
+        + [array((3, N_I, LANES), F32), array((SIDE, STAT_ROWS, LANES), LOW)]
+        + [feature] * 2,
+        z, q2, o2, kv, bias,
         smem=1,
-        scratch=[pltpu.VMEM((N_I, LANES), F32)] * 2,
     )
     del v2
     stats = lax.all_to_all(stats, "col", 0, 0)
     score, weight, part = call(
         grad_kernel,
         [array((CELLS, LANES), LOW)] * 2 + [array((SIDE, W_ROWS, LANES), LOW)],
-        stats, own_max, e, gp, flat_pair,
+        stats, own_stats, e, gp, flat_pair,
         scratch=[pltpu.VMEM((N_I, LANES), F32)] * 2,
     )
     part = lax.all_to_all(part, "col", 0, 0)
@@ -372,7 +374,8 @@
         scratch=[pltpu.VMEM((CELLS, LANES), F32), pltpu.VMEM((HD, N_I, LANES), F32)],
         cost=vpu_cost,
     )
-    d_pair = pair_grad(score, wide)
+    d_pair = jnp.dot(score, wide, preferred_element_type=F32).astype(LOW)
+    row_recv, query_blocks, d_pair = lax.optimization_barrier((row_recv, query_blocks, d_pair))
     d_keys, d_values, col_send = call(
         row_sum_kernel,
         [array((N_J, H), LOW)] * 2 + [array((SIDE, W_ROWS + N_I, LANES), LOW)],
@@ -381,11 +384,11 @@
     col_recv = lax.all_to_all(col_send, "col", 0, 0)
     d_queries, d_wbias = call(
         final_kernel,
-        [array((N_I, H), LOW), array((P_SIZE, H), F32)],
+        [array((N_I, H), LOW), array((H, P_SIZE), F32)],
         col_recv,
         scratch=[pltpu.VMEM((LANES, P_SIZE), F32)],
     )
-    return d_pair.reshape(pair.shape), d_wbias, d_queries, d_keys, d_values
+    return d_pair.reshape(pair.shape), d_wbias.T, d_queries, d_keys, d_values
 
 
 def solution(mesh):

time: 135 us -> 122 us (0.904)
  Pallas kernels: 35.4 us -> 23.1 us
  starting transfers between devices: 33.8 us -> 27.6 us
  matrix products: 0 us -> 4.6 us
  blocking collectives: 38.4 us -> 41.8 us
  local copies, waits for them, and re-layouts: 4.42 us -> 1.63 us
    pallas_call x2 -> x1, Pallas kernels: 11 us -> 1.7 us  [on_device(): pl.pallas_call(prepare_kernel, out_shape=[array((SIDE, 2 * N_I, LANES), L...]
    all_to_all x1, blocking collectives: 9 us -> 17.4 us  [on_device(): col_recv = lax.all_to_all(col_send, 'col', 0, 0)]
    ppermute x1, waiting for transfers between devices: 1.21 us -> 6.05 us  [on_device(): kv_other = lax.ppermute(kv_own, 'row', Z_SWAP)]
    dot_general x0 -> x2, matrix products: none -> 4.6 us  [the longest x1 2.43 us: contract(): lax.dot_general(a, b, (((a_dim,), (b_dim,)), ((), ())), preferred_element...]
    all_to_all x1, blocking collectives: 24.2 us -> 19.6 us  [on_device(): stats = lax.all_to_all(stats, 'col', 0, 0)]
    unnamed x14 -> x0, local copies, waits for them, and re-layouts: 4.39 us -> none
    all_to_all x1, waiting for transfers between devices: 5.81 us -> 1.6 us  [on_device(): kv = lax.all_to_all(kv_send, 'row', 0, 0, axis_index_groups=X_GROUPS)]
    ppermute x1, starting transfers between devices: 7.73 us -> 4.3 us  [on_device(): kv_other = lax.ppermute(kv_own, 'row', Z_SWAP)]
  transfers between devices with their start and end apart: 5 -> 5, of which waited for: 4 -> 5; matrix products, arithmetic and copies ran while one was open for 1% -> 5% of each run, Pallas kernels for 15% -> 8%
where the time goes in v3:
time: 122 us
  blocking collectives  41.8 us (34%)
  starting transfers between devices  27.6 us (23%)
  Pallas kernels  23.1 us (19%)
  waiting for transfers between devices  21.3 us (17%)
  matrix products  4.6 us (4%)
  local copies, waits for them, and re-layouts  1.63 us (1%)
    pallas_call x8, Pallas kernels, call(): pl.pallas_call(kernel, out_shape=out_shape, in_specs=specs, out_specs=out...  21.4 us
    all_to_all x1, blocking collectives, on_device(): stats = lax.all_to_all(stats, 'col', 0, 0)  19.6 us
    all_to_all x1, blocking collectives, on_device(): col_recv = lax.all_to_all(col_send, 'col', 0, 0)  17.4 us
    all_to_all x1, waiting for transfers between devices, on_device(): row_recv = lax.all_to_all(row_send, 'row', 0, 0)  9.64 us
    all_to_all x1, starting transfers between devices, on_device(): qo = lax.all_to_all(qo_send, 'col', 0, 0)  9.19 us
    all_to_all x1, starting transfers between devices, on_device(): row_recv = lax.all_to_all(row_send, 'row', 0, 0)  6.11 us
    ppermute x1, waiting for transfers between devices, on_device(): kv_other = lax.ppermute(kv_own, 'row', Z_SWAP)  6.05 us
    all_gather x1, blocking collectives, on_device(): kv = lax.all_gather(kv, 'row', axis_index_groups=CORE_GROUPS)  4.88 us
  transfers between devices with their start and end apart: 5, of which 5 were waited for; matrix products, arithmetic and copies ran while one was open for 5% of the time, Pallas kernels for 8%

profile of v3, /device:TPU:1, one launch (start us, length us, event | category | flops | bytes accessed | tf_op | source)
XLA Modules:
  0.0 121.6 jit_solution(14131277483300851388)
XLA Ops:
  0.6 1.7 %shard_map.101 = (bf16[16,96,128]{2,1,0:T(8,128)(2,1)}, bf16[96,128]{1,0:T(8,128)(2,1)}) custom-call(bf16[48,96]{1,0:T(8,128)(2,1)} %q_hbm.1, bf16[48,96]{1,0:T(8,128)(2,1)} %o_hbm.1, bf16[48,96]{1,0:T(8,128)(2,1)} %k_hbm.1, bf16[48,96]{1,0:T(8,128)(2,1)} %v_hbm.1), custom_call_target="tpu_custom_call" | custom-call | tf_op jit(solution)/shard_map/pallas_call | solution.py:316
  2.3 9.2 %all-to-all-start = ((bf16[16,96,128]{2,1,0:T(8,128)(2,1)}), bf16[16,96,128]{2,1,0:T(8,128)(2,1)S(1)}, u32[]{:S(2)}, u32[]{:S(2)}) async-start(bf16[16,96,128]{2,1,0:T(8,128)(2,1)} %get-tuple-element.28), calls=%async_computation | async-start | bytes 786432 | tf_op jit(solution)/shard_map/all_to_all | solution.py:324
  11.5 4.3 %collective-permute-start = (bf16[96,128]{1,0:T(8,128)(2,1)}, bf16[96,128]{1,0:T(8,128)(2,1)S(1)}, u32[]{:S(2)}, u32[]{:S(2)}) collective-permute-start(bf16[96,128]{1,0:T(8,128)(2,1)} %get-tuple-element.27), channel_id=1, source_target_pairs={{0,32},{16,48},{32,0},{48,16},{64,96},{80,112},{96,64},{112,80},{1... | collective-permute-start | bytes 73736 | tf_op jit(solution)/shard_map/ppermute | solution.py:323
  15.8 0.9 reshape.27
  16.8 6.0 %collective-permute-done = bf16[96,128]{1,0:T(8,128)(2,1)S(1)} collective-permute-done((bf16[96,128]{1,0:T(8,128)(2,1)}, bf16[96,128]{1,0:T(8,128)(2,1)S(1)}, u32[]{:S(2)}, u32[]{:S(2)}) %collective-permute-start) | collective-permute-done | bytes 24608 | tf_op jit(solution)/shard_map/ppermute | solution.py:323
  22.8 0.7 pad_maximum_fusion
  23.6 1.9 %all-to-all-done.qo_ref = bf16[16,96,128]{2,1,0:T(8,128)(2,1)S(1)} async-done(((bf16[16,96,128]{2,1,0:T(8,128)(2,1)}), bf16[16,96,128]{2,1,0:T(8,128)(2,1)S(1)}, u32[]{:S(2)}, u32[]{:S(2)}) %all-to-all-start) | async-done | bytes 393248 | tf_op jit(solution)/shard_map/all_to_all | solution.py:324
  25.5 0.7 broadcast_in_dim.2
  26.2 4.0 %all-to-all-start.1 = ((bf16[4,2,96,128]{3,2,1,0:T(8,128)(2,1)}), bf16[4,2,96,128]{3,2,1,0:T(8,128)(2,1)S(1)}, u32[]{:S(2)}, u32[]{:S(2)}) async-start(bf16[4,2,96,128]{3,2,1,0:T(8,128)(2,1)} %broadcast_in_dim.2), calls=%async_computation.1 | async-start | bytes 393216 | tf_op jit(solution)/shard_map/all_to_all | solution.py:331
  30.2 2.4 %convolution_bitcast_fusion.bias_ref = f32[2304,128]{1,0:T(8,128)S(1)} fusion(bf16[2304,512]{1,0:T(8,128)(2,1)} %bitcast.18, bf16[16,6,512]{2,1,0:T(8,128)(2,1)S(1)} %reshape.27), kind=kOutput, calls=%fused_computation.1 | convolution fusion | flops 301989888 | bytes 3637248 | tf_op jit(solution)/shard_map/dot_general | solution.py:62
  32.7 1.1 shard_map.102
  33.8 1.6 %all-to-all-done.1 = bf16[4,2,96,128]{3,2,1,0:T(8,128)(2,1)S(1)} async-done(((bf16[4,2,96,128]{3,2,1,0:T(8,128)(2,1)}), bf16[4,2,96,128]{3,2,1,0:T(8,128)(2,1)S(1)}, u32[]{:S(2)}, u32[]{:S(2)}) %all-to-all-start.1) | async-done | bytes 196640 | tf_op jit(solution)/shard_map/all_to_all | solution.py:331
  35.4 4.9 %all-gather = bf16[8,2,96,128]{3,2,1,0:T(8,128)(2,1)S(1)} all-gather(bf16[4,2,96,128]{3,2,1,0:T(8,128)(2,1)S(1)} %all-to-all-done.1), channel_id=2, replica_groups={{0,16},{32,48},{64,80},{96,112},{128,144},{160,176},{192,208},{224,240}..., dimensions={0}, use_global_device_ids=true | all-gather | bytes 589824 | tf_op jit(solution)/shard_map/all_gather | solution.py:339
  40.3 5.2 %shard_map.103 = (f32[2304,128]{1,0:T(8,128)S(1)}, f32[2304,128]{1,0:T(8,128)S(1)}, f32[3,48,128]{2,1,0:T(8,128)S(1)}, bf16[16,112,128]{2,1,0:T(8,128)(2,1)S(1)}...) custom-call(s32[1]{0:T(128)} %bitcast.z_ref, f32[16,48,128]{2,1,0:T(8,128)S(1)} %get-tuple-element.30.q2_ref, ...), custom_call_target="tpu_custom_call" | custom-call | tf_op jit(solution)/shard_map/pallas_call | solution.py:32
  45.5 19.6 %all_to_all.30.stat_ref = bf16[16,112,128]{2,1,0:T(8,128)(2,1)S(1)} all-to-all(bf16[16,112,128]{2,1,0:T(8,128)(2,1)S(1)} %get-tuple-element.33), channel_id=1, replica_groups=mesh['row'=16,'col'=16] {'col'}, dimensions={0} | all-to-all | bytes 917504 | tf_op jit(solution)/shard_map/all_to_all | solution.py:350
  65.1 3.4 %shard_map.104 = (bf16[2304,128]{1,0:T(8,128)(2,1)S(1)}, bf16[2304,128]{1,0:T(8,128)(2,1)S(1)}, bf16[16,32,128]{2,1,0:T(8,128)(2,1)}) custom-call(bf16[16,112,128]{2,1,0:T(8,128)(2,1)S(1)} %all_to_all.30.stat_ref, f32[3,48,128]{2,1,0:T(8,128)S(1)} %get-tuple-element.34.own_ref, f32[2304,128]{1,0:T(8,128)S(1)} %get-tuple-element.35.e_ref, ...), custom_call_target="tpu_custom_call" | custom-call | tf_op jit(solution)/shard_map/pallas_call | solution.py:32
  68.5 4.0 %all-to-all-start.3 = ((bf16[16,32,128]{2,1,0:T(8,128)(2,1)}), bf16[16,32,128]{2,1,0:T(8,128)(2,1)S(1)}, u32[]{:S(2)}, u32[]{:S(2)}) async-start(bf16[16,32,128]{2,1,0:T(8,128)(2,1)} %get-tuple-element.37), calls=%async_computation.3 | async-start | bytes 262144 | tf_op jit(solution)/shard_map/all_to_all | solution.py:357
  72.5 5.1 %shard_map.105.blocks_ref = bf16[16,96,128]{2,1,0:T(8,128)(2,1)S(1)} custom-call(bf16[2304,128]{1,0:T(8,128)(2,1)S(1)} %get-tuple-element.38.score_ref, bf16[2304,128]{1,0:T(8,128)(2,1)S(1)} %get-tuple-element.39.weight_ref, f32[16,48,128]{2,1,0:T(8,128)S(1)} %get-tuple-element.30.q2_ref, f32[16,48,128]{2,1,0:T(8,128)S(1)} %get-tuple-element.31.o2_ref), custom_call_target="tpu_custom_call" | custom-call | flops 4000000000 | bytes 4000000 | tf_op jit(solution)/shard_map/pallas_call | solution.py:32
  77.7 2.1 %all-to-all-done.3.part_ref = bf16[16,32,128]{2,1,0:T(8,128)(2,1)S(1)} async-done(((bf16[16,32,128]{2,1,0:T(8,128)(2,1)}), bf16[16,32,128]{2,1,0:T(8,128)(2,1)S(1)}, u32[]{:S(2)}, u32[]{:S(2)}) %all-to-all-start.3) | async-done | bytes 131104 | tf_op jit(solution)/shard_map/all_to_all | solution.py:357
  79.8 0.8 shard_map.106
  80.6 6.1 %all-to-all-start.4 = ((bf16[16,128,128]{2,1,0:T(8,128)(2,1)}), bf16[16,128,128]{2,1,0:T(8,128)(2,1)S(1)}, u32[]{:S(2)}, u32[]{:S(2)}) async-start(bf16[16,128,128]{2,1,0:T(8,128)(2,1)} %shard_map.106), calls=%async_computation.4 | async-start | bytes 1048576 | tf_op jit(solution)/shard_map/all_to_all | solution.py:369
  86.7 2.2 %convolution_convert_fusion = bf16[2304,512]{1,0:T(8,128)(2,1)} fusion(bf16[2304,128]{1,0:T(8,128)(2,1)S(1)} %get-tuple-element.38.score_ref, bf16[16,6,512]{2,1,0:T(8,128)(2,1)S(1)} %reshape.27), kind=kOutput, calls=%fused_computation | convolution fusion | flops 303169536 | bytes 3047424 | tf_op jit(solution)/shard_map/dot_general | solution.py:377
  88.9 4.0 %shard_map.107.query_ref = bf16[16,48,128]{2,1,0:T(8,128)(2,1)S(1)} custom-call(bf16[2304,128]{1,0:T(8,128)(2,1)S(1)} %get-tuple-element.38.score_ref, f32[16,48,128]{2,1,0:T(8,128)S(1)} %get-tuple-element.40.k2_ref), custom_call_target="tpu_custom_call" | custom-call | flops 4000000000 | bytes 4000000 | tf_op jit(solution)/shard_map/pallas_call | solution.py:32
  92.9 9.6 %all-to-all-done.4.recv_ref = bf16[16,128,128]{2,1,0:T(8,128)(2,1)S(1)} async-done(((bf16[16,128,128]{2,1,0:T(8,128)(2,1)}), bf16[16,128,128]{2,1,0:T(8,128)(2,1)S(1)}, u32[]{:S(2)}, u32[]{:S(2)}) %all-to-all-start.4) | async-done | bytes 524320 | tf_op jit(solution)/shard_map/all_to_all | solution.py:369
  102.6 0.8 shard_map.108
  103.4 17.4 %all_to_all.31.recv_ref = bf16[16,80,128]{2,1,0:T(8,128)(2,1)S(1)} all-to-all(bf16[16,80,128]{2,1,0:T(8,128)(2,1)S(1)} %get-tuple-element.44), channel_id=1, replica_groups=mesh['row'=16,'col'=16] {'col'}, dimensions={0} | all-to-all | bytes 655360 | tf_op jit(solution)/shard_map/all_to_all | solution.py:384
  120.7 0.9 shard_map.109
Async XLA Ops:
  2.3 23.2 %all-to-all-start = ((bf16[16,96,128]{2,1,0:T(8,128)(2,1)}), bf16[16,96,128]{2,1,0:T(8,128)(2,1)S(1)}, u32[]{:S(2)}, u32[]{:S(2)}) async-start(bf16[16,96,128]{2,1,0:T(8,128)(2,1)} %get-tuple-element.28), calls=%async_computation | async-start | bytes 786432 | tf_op jit(solution)/shard_map/all_to_all | solution.py:324
  11.5 11.3 %collective-permute-start = (bf16[96,128]{1,0:T(8,128)(2,1)}, bf16[96,128]{1,0:T(8,128)(2,1)S(1)}, u32[]{:S(2)}, u32[]{:S(2)}) collective-permute-start(bf16[96,128]{1,0:T(8,128)(2,1)} %get-tuple-element.27), channel_id=1, source_target_pairs={{0,32},{16,48},{32,0},{48,16},{64,96},{80,112},{96,64},{112,80},{1... | collective-permute-start | bytes 73736 | tf_op jit(solution)/shard_map/ppermute | solution.py:323
  26.2 9.2 %all-to-all-start.1 = ((bf16[4,2,96,128]{3,2,1,0:T(8,128)(2,1)}), bf16[4,2,96,128]{3,2,1,0:T(8,128)(2,1)S(1)}, u32[]{:S(2)}, u32[]{:S(2)}) async-start(bf16[4,2,96,128]{3,2,1,0:T(8,128)(2,1)} %broadcast_in_dim.2), calls=%async_computation.1 | async-start | bytes 393216 | tf_op jit(solution)/shard_map/all_to_all | solution.py:331
  68.5 11.2 %all-to-all-start.3 = ((bf16[16,32,128]{2,1,0:T(8,128)(2,1)}), bf16[16,32,128]{2,1,0:T(8,128)(2,1)S(1)}, u32[]{:S(2)}, u32[]{:S(2)}) async-start(bf16[16,32,128]{2,1,0:T(8,128)(2,1)} %get-tuple-element.37), calls=%async_computation.3 | async-start | bytes 262144 | tf_op jit(solution)/shard_map/all_to_all | solution.py:357
  80.6 22.0 %all-to-all-start.4 = ((bf16[16,128,128]{2,1,0:T(8,128)(2,1)}), bf16[16,128,128]{2,1,0:T(8,128)(2,1)S(1)}, u32[]{:S(2)}, u32[]{:S(2)}) async-start(bf16[16,128,128]{2,1,0:T(8,128)(2,1)} %shard_map.106), calls=%async_computation.4 | async-start | bytes 1048576 | tf_op jit(solution)/shard_map/all_to_all | solution.py:369

commit v4 on v3

--- a/solution.py
+++ b/solution.py
@@ -17,14 +17,20 @@
 CELLS = N_I * N_J
 LOW = jnp.bfloat16
 F32 = jnp.float32
-VMEM_LIMIT = 48 * 1024 * 1024
+VMEM_LIMIT = 52 * 1024 * 1024
+VMEM_SMALL = 52 * 1024 * 1024
 
 X_GROUPS = [[4 * x + o for x in range(4)] for o in range(4)]
 CORE_GROUPS = [[2 * k, 2 * k + 1] for k in range(8)]
+CORE_APART = [[2 * k + c for k in range(8)] for c in range(2)]
 Z_SWAP = [(r, r ^ 2) for r in range(SIDE)]
-
-
-def call(kernel, out_shape, *args, cost=None, scratch=(), smem=0):
+CORE_SWAP = [(r, r ^ 1) for r in range(SIDE)]
+PAIR_ROWS = N_I + N_I // 2
+W_ROWS = 24
+T = P_SIZE // LANES
+
+
+def call(kernel, out_shape, *args, cost=None, scratch=(), smem=0, limit=VMEM_SMALL):
     specs = [pl.BlockSpec(memory_space=pltpu.SMEM)] * smem
     specs += [pl.BlockSpec(memory_space=pltpu.VMEM)] * (len(args) - smem)
     single = isinstance(out_shape, jax.ShapeDtypeStruct)
@@ -36,7 +42,7 @@
         out_specs=out_spec if single else [out_spec] * len(out_shape),
         scratch_shapes=list(scratch),
         cost_estimate=cost,
-        compiler_params=pltpu.CompilerParams(vmem_limit_bytes=VMEM_LIMIT),
+        compiler_params=pltpu.CompilerParams(vmem_limit_bytes=limit),
     )(*args)
 
 
@@ -92,17 +98,81 @@
     hot = one_hot_features()
     for copy in copies:
         copy.wait()
-    q = (jnp.dot(q_ref[...], hot, preferred_element_type=F32) * (1.0 / HD**0.5)).astype(LOW)
-    o = jnp.dot(o_ref[...], hot, preferred_element_type=F32).astype(LOW)
-    for c in range(SIDE):
-        qo_ref[c, :N_I, :] = q
-        qo_ref[c, N_I:, :] = o
-    kv_ref[:N_J, :] = jnp.dot(k_ref[...], hot, preferred_element_type=F32).astype(LOW)
-    kv_ref[N_J:, :] = jnp.dot(v_ref[...], hot, preferred_element_type=F32).astype(LOW)
+    q, o, k, v = (
+        jnp.dot(ref[...], hot, preferred_element_type=F32) for ref in (q_ref, o_ref, k_ref, v_ref)
+    )
+    packed = pack_two(q * (1.0 / HD**0.5), o).astype(LOW)
+    for c in range(SIDE):
+        qo_ref[c] = packed
+    kv_ref[...] = pack_two(k, v).astype(LOW)
+
+
+def stack_kernel(own_ref, other_ref, out_ref):
+    for x in range(4):
+        out_ref[x, 0] = own_ref[...]
+        out_ref[x, 1] = other_ref[...]
 
 
 def place_of(shape):
     return lax.broadcasted_iota(jnp.int32, shape, 1) & 7
+
+
+def pack_two(first, second):
+    place = place_of((N_I, LANES))
+    top = jnp.where(place < PLACES, first, pltpu.roll(second, 6, 1))
+    half = N_I // 2
+    place = place_of((half, LANES))
+    bottom = jnp.where(
+        (place >= 2) & (place < PLACES), second[:half], pltpu.roll(second[half:], 4, 1)
+    )
+    return jnp.concatenate([top, bottom], axis=0)
+
+
+def unpack_two(packed):
+    place = place_of((N_I, LANES))
+    top, bottom = packed[:N_I], packed[N_I:]
+    second = jnp.concatenate([bottom, pltpu.roll(bottom, LANES - 4, 1)], axis=0)
+    second = jnp.where(place < 2, pltpu.roll(top, LANES - 6, 1), second)
+    used = place < PLACES
+    return jnp.where(used, top, 0.0), jnp.where(used, second, 0.0)
+
+
+def unpack_features(wide_ref, first_ref, second_ref):
+    place = place_of((8, LANES))
+    used = place < PLACES
+    for t in range(N_I // 8):
+        at = slice(8 * t, 8 * t + 8)
+        half = N_I + 8 * (t % 3)
+        first, second = [], []
+        for c in range(SIDE):
+            top = wide_ref[c, at, :]
+            bottom = wide_ref[c, half : half + 8, :]
+            if t >= 3:
+                bottom = pltpu.roll(bottom, LANES - 4, 1)
+            bottom = jnp.where(place < 2, pltpu.roll(top, LANES - 6, 1), bottom)
+            first.append(jnp.where(used, top, 0.0))
+            second.append(jnp.where(used, bottom, 0.0))
+        for parts, out in ((first, first_ref), (second, second_ref)):
+            for d, part in enumerate(swap_blocks(parts)):
+                out[d, at, :] = part
+
+
+def pack_shard(rows):
+    row = lax.broadcasted_iota(jnp.int32, (8, LANES), 0)
+    tiles = [rows[:, LANES * t : LANES * (t + 1)] for t in range(T)]
+    return jnp.concatenate(
+        [jnp.where(row < PLACES, tiles[t], pltpu.roll(tiles[3], 6 - 2 * t, 0)) for t in range(3)],
+        axis=0,
+    )
+
+
+def unpack_shard(packed):
+    row = lax.broadcasted_iota(jnp.int32, (8, LANES), 0)
+    tiles = [packed[8 * t : 8 * t + 8] for t in range(3)]
+    last = pltpu.roll(tiles[2], 6, 0)
+    last = jnp.where(row < 4, pltpu.roll(tiles[1], 4, 0), last)
+    last = jnp.where(row < 2, pltpu.roll(tiles[0], 2, 0), last)
+    return [jnp.where(row < PLACES, tile, 0.0) for tile in tiles + [last]]
 
 
 def pack_stats(first, second, third):
@@ -132,27 +202,17 @@
 STAT_ROWS = 2 * N_I + 16
 
 
-def rows_kernel(qo_ref, q2_ref, o2_ref):
-    for t in range(N_I // 16):
-        at = slice(16 * t, 16 * t + 16)
-        for first, out in ((0, q2_ref), (N_I, o2_ref)):
-            src = slice(first + 16 * t, first + 16 * t + 16)
-            parts = swap_blocks([qo_ref[c, src, :].astype(F32) for c in range(SIDE)])
-            for d in range(HD):
-                out[d, at, :] = parts[d]
-
-
-def scores_kernel(z_ref, q2_ref, o2_ref, kv_ref, bias_ref, e_ref, gp_ref, own_ref, stat_ref, k2_ref, v2_ref):
+def rows_kernel(qo_ref, q2_ref, o2_ref, wide_ref):
+    for c in range(SIDE):
+        wide_ref[c] = qo_ref[c].astype(F32)
+    unpack_features(wide_ref, q2_ref, o2_ref)
+
+
+def scores_kernel(z_ref, q2_ref, o2_ref, kv_ref, bias_ref, e_ref, gp_ref, own_ref, stat_ref, k2_ref, v2_ref, wide_ref):
     z = z_ref[0]
-    for t in range(N_J // 16):
-        at = slice(16 * t, 16 * t + 16)
-        for first, out in ((0, k2_ref), (N_J, v2_ref)):
-            src = slice(first + 16 * t, first + 16 * t + 16)
-            parts = swap_blocks(
-                [kv_ref[r & 1, r >> 2, ((r >> 1) & 1) ^ z, src, :].astype(F32) for r in range(SIDE)]
-            )
-            for d in range(HD):
-                out[d, at, :] = parts[d]
+    for r in range(SIDE):
+        wide_ref[r] = kv_ref[r & 1, r >> 2, ((r >> 1) & 1) ^ z].astype(F32)
+    unpack_features(wide_ref, k2_ref, v2_ref)
 
     def rows(pair_at, carry):
         here = [2 * pair_at, 2 * pair_at + 1]
@@ -184,7 +244,20 @@
         stat_ref[c, 2 * N_I :, :] = packed[2]
 
 
-def grad_kernel(stat_ref, own_ref, e_ref, gp_ref, pair_ref, score_ref, weight_ref, part_ref, factor_ref, offset_ref):
+PAIR_CUTS = 8
+
+
+def grad_kernel(stat_ref, own_ref, e_ref, gp_ref, pair_hbm, score_ref, weight_ref, part_ref, factor_ref, offset_ref, pair_ref, sems):
+    cut = CELLS // PAIR_CUTS
+    copies = [
+        pltpu.make_async_copy(
+            pair_hbm.at[pl.ds(n * cut, cut)], pair_ref.at[pl.ds(n * cut, cut)], sems.at[n]
+        )
+        for n in range(PAIR_CUTS)
+    ]
+    for copy in copies:
+        copy.start()
+
     def stats_of(c):
         return unpack_stats(
             stat_ref[c, :N_I, :].astype(F32),
@@ -219,12 +292,11 @@
         return carry
 
     lax.fori_loop(0, N_I, row, 0, unroll=2)
+    for copy in copies:
+        copy.wait()
     term = contract(score_ref[...], pair_ref[...], 0, 0)
     for c in range(SIDE):
-        rows = term[8 * c : 8 * c + 8]
-        part_ref[c] = jnp.concatenate(
-            [rows[:, LANES * t : LANES * (t + 1)] for t in range(P_SIZE // LANES)], axis=0
-        ).astype(LOW)
+        part_ref[c] = pack_shard(term[8 * c : 8 * c + 8]).astype(LOW)
 
 
 D_BLOCK = 4
@@ -245,68 +317,74 @@
             out_ref[first + k] = sums[k]
 
 
-def store_blocks(sum_ref, out_ref, first):
-    for t in range(N_J // 16):
-        at = slice(16 * t, 16 * t + 16)
-        parts = swap_blocks([sum_ref[d, at, :] for d in range(HD)])
-        for c in range(SIDE):
-            out_ref[c, first + 16 * t : first + 16 * t + 16, :] = parts[c].astype(LOW)
-
-
-def key_kernel(score_ref, weight_ref, q2_ref, o2_ref, out_ref, sum_ref):
+def blocks_of(sum_ref, out_ref):
+    for t in range(N_J // 8):
+        at = slice(8 * t, 8 * t + 8)
+        for c, part in enumerate(swap_blocks([sum_ref[d, at, :] for d in range(HD)])):
+            out_ref[c, at, :] = part
+
+
+def key_kernel(core_ref, score_ref, weight_ref, q2_ref, o2_ref, mine_ref, other_ref, sum_ref, key_ref, value_ref):
     def tile_of(ref):
         return lambda i: ref[pl.ds(pl.multiple_of(i * N_J, N_J), N_J), :].astype(F32)
 
     weighted_sums(N_I, tile_of(score_ref), q2_ref, sum_ref)
-    store_blocks(sum_ref, out_ref, 0)
+    blocks_of(sum_ref, key_ref)
     weighted_sums(N_I, tile_of(weight_ref), o2_ref, sum_ref)
-    store_blocks(sum_ref, out_ref, N_J)
-
-
-def query_kernel(score_ref, k2_ref, out_ref, wide_ref, sum_ref):
+    blocks_of(sum_ref, value_ref)
+    first_core = core_ref[0] == 0
+    for k in range(8):
+        even = pack_two(key_ref[2 * k], value_ref[2 * k])
+        odd = pack_two(key_ref[2 * k + 1], value_ref[2 * k + 1])
+        mine_ref[k] = jnp.where(first_core, even, odd).astype(LOW)
+        other_ref[k] = jnp.where(first_core, odd, even).astype(LOW)
+
+
+def query_kernel(score_ref, k2_ref, out_ref, wide_ref, sum_ref, block_ref):
     wide_ref[...] = score_ref[...].astype(F32)
     weighted_sums(N_J, lambda j: wide_ref[pl.ds(j, N_I, stride=N_J), :], k2_ref, sum_ref)
-    store_blocks(sum_ref, out_ref, 0)
-
-
-W_ROWS = 32
-
-
-def row_send_kernel(part_ref, blocks_ref, out_ref):
+    blocks_of(sum_ref, block_ref)
+    for c in range(SIDE):
+        out_ref[c] = block_ref[c].astype(LOW)
+
+
+def row_send_kernel(part_ref, mine_ref, partner_ref, out_ref):
     total = part_ref[0].astype(F32)
     for c in range(1, SIDE):
         total = total + part_ref[c].astype(F32)
-    total = total.astype(LOW)
-    for r in range(SIDE):
-        out_ref[r, : 2 * N_J, :] = blocks_ref[r]
-        out_ref[r, 2 * N_J :, :] = total
+    for k in range(8):
+        both = mine_ref[k].astype(F32) + partner_ref[k].astype(F32)
+        out_ref[k] = jnp.concatenate([both, total], axis=0).astype(LOW)
 
 
 def from_block(x):
     return contract(x.astype(LOW), one_hot_features(), 1, 1).astype(LOW)
 
 
-def row_sum_kernel(recv_ref, query_ref, key_ref, value_ref, out_ref):
+def row_sum_kernel(recv_ref, key_ref, value_ref, shard_ref):
     total = recv_ref[0].astype(F32)
-    for r in range(1, SIDE):
-        total = total + recv_ref[r].astype(F32)
-    key_ref[...] = from_block(total[:N_J])
-    value_ref[...] = from_block(total[N_J : 2 * N_J])
-    shard = total[2 * N_J :].astype(LOW)
-    for c in range(SIDE):
-        out_ref[c, :W_ROWS, :] = shard
-        out_ref[c, W_ROWS:, :] = query_ref[c]
+    for k in range(1, 8):
+        total = total + recv_ref[k].astype(F32)
+    key, value = unpack_two(total[:PAIR_ROWS])
+    key_ref[...] = from_block(key)
+    value_ref[...] = from_block(value)
+    shard_ref[...] = total[PAIR_ROWS:]
+
+
+def col_send_kernel(shard_ref, partner_ref, query_ref, out_ref):
+    shard = shard_ref[...] + partner_ref[...]
+    for c in range(SIDE):
+        out_ref[c] = jnp.concatenate([shard, query_ref[c].astype(F32)], axis=0).astype(LOW)
 
 
 def final_kernel(recv_ref, query_ref, w_ref, wide_ref):
-    total = recv_ref[0, W_ROWS:, :].astype(F32)
-    for c in range(1, SIDE):
-        total = total + recv_ref[c, W_ROWS:, :].astype(F32)
+    total = jnp.zeros((N_I, LANES), F32)
+    for c in range(SIDE):
+        block = recv_ref[c].astype(F32)
+        total = total + block[W_ROWS:]
+        for t, tile in enumerate(unpack_shard(block[:W_ROWS])):
+            wide_ref[8 * c : 8 * c + 8, LANES * t : LANES * (t + 1)] = tile
     query_ref[...] = from_block(total * (1.0 / HD**0.5))
-    for c in range(SIDE):
-        rows = recv_ref[c, :W_ROWS, :].astype(F32)
-        for t in range(P_SIZE // LANES):
-            wide_ref[8 * c : 8 * c + 8, LANES * t : LANES * (t + 1)] = rows[8 * t : 8 * t + 8]
     w_ref[...] = contract(one_hot_heads(), wide_ref[...].astype(LOW), 1, 0)
 
 
@@ -315,7 +393,7 @@
     own = pltpu.VMEM((N_I, H), LOW)
     qo_send, kv_own = pl.pallas_call(
         prepare_kernel,
-        out_shape=[array((SIDE, 2 * N_I, LANES), LOW), array((2 * N_J, LANES), LOW)],
+        out_shape=[array((SIDE, PAIR_ROWS, LANES), LOW), array((PAIR_ROWS, LANES), LOW)],
         in_specs=[pl.BlockSpec(memory_space=pl.ANY)] * 4,
         out_specs=[pl.BlockSpec(memory_space=pltpu.VMEM)] * 2,
         scratch_shapes=[own] * 4 + [pltpu.SemaphoreType.DMA((4,))],
@@ -325,8 +403,7 @@
     wide = jnp.pad(w_bias.T.reshape(SIDE, PLACES, P_SIZE), ((0, 0), (0, 2), (0, 0)))
     wide = wide.reshape(LANES, P_SIZE)
     bias = contract(flat_pair, wide, 1, 1)
-    kv_both = jnp.stack([kv_own, kv_other])
-    kv_send = jnp.broadcast_to(kv_both[None], (4,) + kv_both.shape)
+    kv_send = call(stack_kernel, array((4, 2, PAIR_ROWS, LANES), LOW), kv_own, kv_other)
     kv_send, qo = lax.optimization_barrier((kv_send, qo))
     kv = lax.all_to_all(kv_send, "row", 0, 0, axis_index_groups=X_GROUPS)
     feature = array((HD, N_I, LANES), F32)
@@ -334,10 +411,12 @@
         rows_kernel,
         [feature] * 2,
         qo,
+        scratch=[pltpu.VMEM((SIDE, PAIR_ROWS, LANES), F32)],
         cost=pl.CostEstimate(flops=1_000_000_000, bytes_accessed=2_000_000, transcendentals=0),
     )
     kv = lax.all_gather(kv, "row", axis_index_groups=CORE_GROUPS)
-    z = ((lax.axis_index("row") >> 1) & 1).astype(jnp.int32).reshape(1)
+    row_at = lax.axis_index("row").astype(jnp.int32).reshape(1)
+    z, core = (row_at >> 1) & 1, row_at & 1
     e, gp, own_stats, stats, k2, v2 = call(
         scores_kernel,
         [array((CELLS, LANES), F32)] * 2
@@ -345,41 +424,57 @@
         + [feature] * 2,
         z, q2, o2, kv, bias,
         smem=1,
+        limit=VMEM_LIMIT,
+        scratch=[pltpu.VMEM((SIDE, PAIR_ROWS, LANES), F32)],
     )
     del v2
     stats = lax.all_to_all(stats, "col", 0, 0)
-    score, weight, part = call(
+    vmem = pl.BlockSpec(memory_space=pltpu.VMEM)
+    score, weight, part = pl.pallas_call(
         grad_kernel,
-        [array((CELLS, LANES), LOW)] * 2 + [array((SIDE, W_ROWS, LANES), LOW)],
-        stats, own_stats, e, gp, flat_pair,
-        scratch=[pltpu.VMEM((N_I, LANES), F32)] * 2,
-    )
+        out_shape=[array((CELLS, LANES), LOW)] * 2 + [array((SIDE, W_ROWS, LANES), LOW)],
+        in_specs=[vmem] * 4 + [pl.BlockSpec(memory_space=pl.ANY)],
+        out_specs=[vmem] * 3,
+        scratch_shapes=[pltpu.VMEM((N_I, LANES), F32)] * 2
+        + [pltpu.VMEM((CELLS, P_SIZE), LOW), pltpu.SemaphoreType.DMA((PAIR_CUTS,))],
+        compiler_params=pltpu.CompilerParams(vmem_limit_bytes=VMEM_LIMIT),
+    )(stats, own_stats, e, gp, flat_pair)
     part = lax.all_to_all(part, "col", 0, 0)
     vpu_cost = pl.CostEstimate(flops=4_000_000_000, bytes_accessed=4_000_000, transcendentals=0)
-    key_blocks = call(
+    blocks = pltpu.VMEM((SIDE, N_J, LANES), F32)
+    mine, other = call(
         key_kernel,
-        array((SIDE, 2 * N_J, LANES), LOW),
-        score, weight, q2, o2,
-        scratch=[pltpu.VMEM((HD, N_J, LANES), F32)],
+        [array((8, PAIR_ROWS, LANES), LOW)] * 2,
+        core, score, weight, q2, o2,
+        smem=1,
+        limit=VMEM_LIMIT,
+        scratch=[pltpu.VMEM((HD, N_J, LANES), F32), blocks, blocks],
         cost=vpu_cost,
     )
+    partner = lax.ppermute(other, "row", CORE_SWAP)
     row_send = call(
-        row_send_kernel, array((SIDE, 2 * N_J + W_ROWS, LANES), LOW), part, key_blocks
-    )
-    row_recv = lax.all_to_all(row_send, "row", 0, 0)
+        row_send_kernel, array((8, PAIR_ROWS + W_ROWS, LANES), LOW), part, mine, partner
+    )
+    row_recv = lax.all_to_all(row_send, "row", 0, 0, axis_index_groups=CORE_APART)
     query_blocks = call(
         query_kernel,
         array((SIDE, N_I, LANES), LOW),
         score, k2,
-        scratch=[pltpu.VMEM((CELLS, LANES), F32), pltpu.VMEM((HD, N_I, LANES), F32)],
+        limit=VMEM_LIMIT,
+        scratch=[pltpu.VMEM((CELLS, LANES), F32), pltpu.VMEM((HD, N_I, LANES), F32), blocks],
         cost=vpu_cost,
     )
     d_pair = jnp.dot(score, wide, preferred_element_type=F32).astype(LOW)
-    row_recv, query_blocks, d_pair = lax.optimization_barrier((row_recv, query_blocks, d_pair))
-    d_keys, d_values, col_send = call(
+    row_recv, query_blocks = lax.optimization_barrier((row_recv, query_blocks))
+    d_keys, d_values, shard = call(
         row_sum_kernel,
-        [array((N_J, H), LOW)] * 2 + [array((SIDE, W_ROWS + N_I, LANES), LOW)],
-        row_recv, query_blocks,
+        [array((N_J, H), LOW)] * 2 + [array((W_ROWS, LANES), F32)],
+        row_recv,
+    )
+    col_send = call(
+        col_send_kernel,
+        array((SIDE, W_ROWS + N_I, LANES), LOW),
+        shard, lax.ppermute(shard, "row", CORE_SWAP), query_blocks,
     )
     col_recv = lax.all_to_all(col_send, "col", 0, 0)
     d_queries, d_wbias = call(

time: 122 us -> 125 us (1.025)
  blocking collectives: 41.8 us -> 5.13 us
  starting transfers between devices: 27.6 us -> 44.6 us
  waiting for transfers between devices: 21.3 us -> 34.6 us
  Pallas kernels: 23.1 us -> 30.7 us
    all_to_all x2 -> x0, blocking collectives: 37 us -> none  [the longest x1 19.6 us: on_device(): stats = lax.all_to_all(stats, 'col', 0, 0)]
    all_to_all x1 -> x3, waiting for transfers between devices: 9.64 us -> 28.4 us  [the longest x1 14.3 us: on_device(): stats = lax.all_to_all(stats, 'col', 0, 0)]
    all_to_all x1 -> x3, starting transfers between devices: 6.11 us -> 20 us  [the longest x1 8.23 us: on_device(): col_recv = lax.all_to_all(col_send, 'col', 0, 0)]
    pallas_call x1 -> x2, Pallas kernels: 1.7 us -> 6.21 us  [the longest x1 4.47 us: on_device(): pl.pallas_call(grad_kernel, out_shape=[array((CELLS, LANES), LOW)] * 2 +...]
    ppermute x0 -> x2, starting transfers between devices: none -> 3.11 us  [the longest x1 1.79 us: on_device(): lax.ppermute(shard, 'row', CORE_SWAP)]
    pallas_call x8 -> x9, Pallas kernels: 21.4 us -> 24.5 us  [call(): pl.pallas_call(kernel, out_shape=out_shape, in_specs=specs, out_specs=out...]
    all_to_all x1, waiting for transfers between devices: 2.1 us -> 0.01 us  [on_device(): part = lax.all_to_all(part, 'col', 0, 0)]
    all_to_all x1, waiting for transfers between devices: 1.93 us -> 0.01 us  [on_device(): qo = lax.all_to_all(qo_send, 'col', 0, 0)]
  transfers between devices with their start and end apart: 5 -> 9, of which waited for: 5 -> 6; matrix products, arithmetic and copies ran while one was open for 5% -> 5% of each run, Pallas kernels for 8% -> 11%
where the time goes in v4:
time: 125 us; the launch traced here: 124 us
  starting transfers between devices  44.6 us (36%)
  waiting for transfers between devices  34.6 us (28%)
  Pallas kernels  30.7 us (25%)
  matrix products  5.62 us (4%)
  blocking collectives  5.13 us (4%)
  local copies, waits for them, and re-layouts  2.46 us (2%)
    pallas_call x9, Pallas kernels, call(): pl.pallas_call(kernel, out_shape=out_shape, in_specs=specs, out_specs=out...  24.5 us
    all_to_all x1, waiting for transfers between devices, on_device(): stats = lax.all_to_all(stats, 'col', 0, 0)  14.3 us
    all_to_all x1, starting transfers between devices, on_device(): qo = lax.all_to_all(qo_send, 'col', 0, 0)  9.2 us
    all_to_all x1, waiting for transfers between devices, on_device(): col_recv = lax.all_to_all(col_send, 'col', 0, 0)  8.31 us
    all_to_all x1, starting transfers between devices, on_device(): col_recv = lax.all_to_all(col_send, 'col', 0, 0)  8.23 us
    all_to_all x1, starting transfers between devices, on_device(): stats = lax.all_to_all(stats, 'col', 0, 0)  6.52 us
    all_to_all x1, waiting for transfers between devices, on_device(): lax.all_to_all(row_send, 'row', 0, 0, axis_index_groups=CORE_APART)  5.74 us
    all_to_all x1, starting transfers between devices, on_device(): lax.all_to_all(row_send, 'row', 0, 0, axis_index_groups=CORE_APART)  5.24 us
  transfers between devices with their start and end apart: 9, of which 6 were waited for; matrix products, arithmetic and copies ran while one was open for 5% of the time, Pallas kernels for 11%

profile of v4, /device:TPU:1, one launch (start us, length us, event | category | flops | bytes accessed | tf_op | source)
XLA Modules:
  0.0 123.8 jit_solution(1468761989561485617)
XLA Ops:
  0.6 1.7 %shard_map.101 = (bf16[16,72,128]{2,1,0:T(8,128)(2,1)}, bf16[72,128]{1,0:T(8,128)(2,1)}) custom-call(bf16[48,96]{1,0:T(8,128)(2,1)} %q_hbm.1, bf16[48,96]{1,0:T(8,128)(2,1)} %o_hbm.1, bf16[48,96]{1,0:T(8,128)(2,1)} %k_hbm.1, bf16[48,96]{1,0:T(8,128)(2,1)} %v_hbm.1), custom_call_target="tpu_custom_call" | custom-call | tf_op jit(solution)/shard_map/pallas_call | solution.py:394
  2.4 9.2 %all-to-all-start = ((bf16[16,72,128]{2,1,0:T(8,128)(2,1)}), bf16[16,72,128]{2,1,0:T(8,128)(2,1)S(1)}, u32[]{:S(2)}, u32[]{:S(2)}) async-start(bf16[16,72,128]{2,1,0:T(8,128)(2,1)} %get-tuple-element.29), calls=%async_computation | async-start | bytes 589824 | tf_op jit(solution)/shard_map/all_to_all | solution.py:402
  11.6 4.3 %collective-permute-start = (bf16[72,128]{1,0:T(8,128)(2,1)}, bf16[72,128]{1,0:T(8,128)(2,1)S(1)}, u32[]{:S(2)}, u32[]{:S(2)}) collective-permute-start(bf16[72,128]{1,0:T(8,128)(2,1)} %get-tuple-element.28.own_ref), channel_id=1, source_target_pairs={{0,32},{16,48},{32,0},{48,16},{64,96},{80,112},{96,64},{112,80},{1... | collective-permute-start | bytes 55304 | tf_op jit(solution)/shard_map/ppermute | solution.py:401
  15.9 0.9 reshape.29
  16.8 4.3 %collective-permute-done.other_ref = bf16[72,128]{1,0:T(8,128)(2,1)S(1)} collective-permute-done((bf16[72,128]{1,0:T(8,128)(2,1)}, bf16[72,128]{1,0:T(8,128)(2,1)S(1)}, u32[]{:S(2)}, u32[]{:S(2)}) %collective-permute-start) | collective-permute-done | bytes 18464 | tf_op jit(solution)/shard_map/ppermute | solution.py:401
  21.1 0.0 copy-start
  21.1 0.7 copy-done
  21.9 0.7 shard_map.102
  22.5 0.0 all-to-all-done.qo_ref
  22.5 4.0 %all-to-all-start.1 = ((bf16[4,2,72,128]{3,2,1,0:T(8,128)(2,1)}), bf16[4,2,72,128]{3,2,1,0:T(8,128)(2,1)S(1)}, u32[]{:S(2)}, u32[]{:S(2)}) async-start(bf16[4,2,72,128]{3,2,1,0:T(8,128)(2,1)} %shard_map.102), calls=%async_computation.1 | async-start | bytes 294912 | tf_op jit(solution)/shard_map/all_to_all | solution.py:408
  26.6 3.5 %convolution_bitcast_fusion.bias_ref = f32[2304,128]{1,0:T(8,128)} fusion(bf16[2304,512]{1,0:T(8,128)(2,1)} %bitcast.17, bf16[16,6,512]{2,1,0:T(8,128)(2,1)S(1)} %reshape.29), kind=kOutput, calls=%fused_computation.1 | convolution fusion | flops 301989888 | bytes 3637248 | tf_op jit(solution)/shard_map/dot_general | solution.py:68
  30.0 1.8 %shard_map.103 = (f32[16,48,128]{2,1,0:T(8,128)S(1)}, f32[16,48,128]{2,1,0:T(8,128)S(1)}) custom-call(bf16[16,72,128]{2,1,0:T(8,128)(2,1)S(1)} %all-to-all-done.qo_ref), custom_call_target="tpu_custom_call" | custom-call | flops 1000000000 | bytes 2000000 | tf_op jit(solution)/shard_map/pallas_call | solution.py:38
  31.8 0.0 all-to-all-done.1
  31.8 5.1 %all-gather = bf16[8,2,72,128]{3,2,1,0:T(8,128)(2,1)S(1)} all-gather(bf16[4,2,72,128]{3,2,1,0:T(8,128)(2,1)S(1)} %all-to-all-done.1), channel_id=2, replica_groups={{0,16},{32,48},{64,80},{96,112},{128,144},{160,176},{192,208},{224,240}..., dimensions={0}, use_global_device_ids=true | all-gather | bytes 442368 | tf_op jit(solution)/shard_map/all_gather | solution.py:417
  36.9 8.0 %shard_map.104 = (f32[2304,128]{1,0:T(8,128)}, f32[2304,128]{1,0:T(8,128)}, f32[3,48,128]{2,1,0:T(8,128)S(1)}, bf16[16,112,128]{2,1,0:T(8,128)(2,1)}, f32[16,48,...) custom-call(s32[1]{0:T(128)} %bitcast.z_ref, f32[16,48,128]{2,1,0:T(8,128)S(1)} %get-tuple-element.31.q2_ref, ...), custom_call_target="tpu_custom_call" | custom-call | tf_op jit(solution)/shard_map/pallas_call | solution.py:38
  44.9 6.5 %all-to-all-start.2 = ((bf16[16,112,128]{2,1,0:T(8,128)(2,1)}), bf16[16,112,128]{2,1,0:T(8,128)(2,1)S(1)}, u32[]{:S(2)}, u32[]{:S(2)}) async-start(bf16[16,112,128]{2,1,0:T(8,128)(2,1)} %get-tuple-element.34), calls=%async_computation.2 | async-start | bytes 917504 | tf_op jit(solution)/shard_map/all_to_all | solution.py:431
  51.5 14.3 %all-to-all-done.2.stat_ref = bf16[16,112,128]{2,1,0:T(8,128)(2,1)S(1)} async-done(((bf16[16,112,128]{2,1,0:T(8,128)(2,1)}), bf16[16,112,128]{2,1,0:T(8,128)(2,1)S(1)}, u32[]{:S(2)}, u32[]{:S(2)}) %all-to-all-start.2) | async-done | bytes 458784 | tf_op jit(solution)/shard_map/all_to_all | solution.py:431
  65.8 4.5 %shard_map.105 = (bf16[2304,128]{1,0:T(8,128)(2,1)S(1)}, bf16[2304,128]{1,0:T(8,128)(2,1)S(1)}, bf16[16,24,128]{2,1,0:T(8,128)(2,1)}) custom-call(bf16[16,112,128]{2,1,0:T(8,128)(2,1)S(1)} %all-to-all-done.2.stat_ref, f32[3,48,128]{2,1,0:T(8,128)S(1)} %get-tuple-element.35.own_ref, f32[2304,128]{1,0:T(8,128)} %get-tuple-element.36.e_ref, ...), custom_call_target="tpu_custom_call" | custom-call | tf_op jit(solution)/shard_map/pallas_call | solution.py:433
  70.3 0.0 copy-start.1
  70.3 0.8 copy-done.1
  71.1 4.0 %all-to-all-start.3 = ((bf16[16,24,128]{2,1,0:T(8,128)(2,1)}), bf16[16,24,128]{2,1,0:T(8,128)(2,1)S(1)}, u32[]{:S(2)}, u32[]{:S(2)}) async-start(bf16[16,24,128]{2,1,0:T(8,128)(2,1)} %get-tuple-element.39), calls=%async_computation.3 | async-start | bytes 196608 | tf_op jit(solution)/shard_map/all_to_all | solution.py:442
  75.1 6.9 %shard_map.106 = (bf16[8,72,128]{2,1,0:T(8,128)(2,1)S(1)}, bf16[8,72,128]{2,1,0:T(8,128)(2,1)S(1)}) custom-call(s32[1]{0:T(128)} %bitcast.7.core_ref, bf16[2304,128]{1,0:T(8,128)(2,1)S(1)} %get-tuple-element.38.score_ref, bf16[2304,128]{1,0:T(8,128)(2,1)} %copy-done.1, f32[16,48,128]{2,1,0:T(8,128)S(1)} %get-tuple-element.31.q2_ref, ...), custom_call_target="tpu_custom_call" | custom-call | flops 4000000000 | bytes 4000000 | tf_op jit(solution)/shard_map/pallas_call | solution.py:38
  82.0 1.3 %collective-permute-start.1 = (bf16[8,72,128]{2,1,0:T(8,128)(2,1)S(1)}, bf16[8,72,128]{2,1,0:T(8,128)(2,1)S(1)}, u32[]{:S(2)}, u32[]{:S(2)}) collective-permute-start(bf16[8,72,128]{2,1,0:T(8,128)(2,1)S(1)} %get-tuple-element.42), channel_id=1, source_target_pairs={{0,16},{16,0},{32,48},{48,32},{64,80},{80,64},{96,112},{112,96},{1... | collective-permute-start | bytes 442376 | tf_op jit(solution)/shard_map/ppermute | solution.py:454
  83.3 1.0 collective-permute-done.1.partner_ref
  84.3 0.0 all-to-all-done.3.part_ref
  84.3 0.7 shard_map.107
  85.0 5.2 %all-to-all-start.4 = ((bf16[8,96,128]{2,1,0:T(8,128)(2,1)}), bf16[8,96,128]{2,1,0:T(8,128)(2,1)S(1)}, u32[]{:S(2)}, u32[]{:S(2)}) async-start(bf16[8,96,128]{2,1,0:T(8,128)(2,1)} %shard_map.107), calls=%async_computation.4 | async-start | bytes 393216 | tf_op jit(solution)/shard_map/all_to_all | solution.py:458
  90.3 4.0 %shard_map.108.query_ref = bf16[16,48,128]{2,1,0:T(8,128)(2,1)S(1)} custom-call(bf16[2304,128]{1,0:T(8,128)(2,1)S(1)} %get-tuple-element.38.score_ref, f32[16,48,128]{2,1,0:T(8,128)S(1)} %get-tuple-element.43.k2_ref), custom_call_target="tpu_custom_call" | custom-call | flops 4000000000 | bytes 4000000 | tf_op jit(solution)/shard_map/pallas_call | solution.py:38
  94.3 5.7 %all-to-all-done.4.recv_ref = bf16[8,96,128]{2,1,0:T(8,128)(2,1)S(1)} async-done(((bf16[8,96,128]{2,1,0:T(8,128)(2,1)}), bf16[8,96,128]{2,1,0:T(8,128)(2,1)S(1)}, u32[]{:S(2)}, u32[]{:S(2)}) %all-to-all-start.4) | async-done | bytes 196640 | tf_op jit(solution)/shard_map/all_to_all | solution.py:458
  100.0 0.8 shard_map.109
  100.9 1.8 %collective-permute-start.2 = (f32[24,128]{1,0:T(8,128)S(1)}, f32[24,128]{1,0:T(8,128)S(1)}, u32[]{:S(2)}, u32[]{:S(2)}) collective-permute-start(f32[24,128]{1,0:T(8,128)S(1)} %get-tuple-element.45.shard_ref), channel_id=1, source_target_pairs={{0,16},{16,0},{32,48},{48,32},{64,80},{80,64},{96,112},{112,96},{1... | collective-permute-start | bytes 36872 | tf_op jit(solution)/shard_map/ppermute | solution.py:477
  102.6 0.8 collective-permute-done.2.partner_ref
  103.5 0.8 shard_map.110
  104.2 8.2 %all-to-all-start.5 = ((bf16[16,72,128]{2,1,0:T(8,128)(2,1)}), bf16[16,72,128]{2,1,0:T(8,128)(2,1)S(1)}, u32[]{:S(2)}, u32[]{:S(2)}) async-start(bf16[16,72,128]{2,1,0:T(8,128)(2,1)} %shard_map.110), calls=%async_computation.5 | async-start | bytes 589824 | tf_op jit(solution)/shard_map/all_to_all | solution.py:479
  112.5 2.2 %convolution_convert_fusion = bf16[2304,512]{1,0:T(8,128)(2,1)} fusion(bf16[2304,128]{1,0:T(8,128)(2,1)S(1)} %get-tuple-element.38.score_ref, bf16[16,6,512]{2,1,0:T(8,128)(2,1)S(1)} %reshape.29), kind=kOutput, calls=%fused_computation | convolution fusion | flops 303169536 | bytes 3047424 | tf_op jit(solution)/shard_map/dot_general | solution.py:467
  114.6 8.3 %all-to-all-done.5.recv_ref = bf16[16,72,128]{2,1,0:T(8,128)(2,1)S(1)} async-done(((bf16[16,72,128]{2,1,0:T(8,128)(2,1)}), bf16[16,72,128]{2,1,0:T(8,128)(2,1)S(1)}, u32[]{:S(2)}, u32[]{:S(2)}) %all-to-all-start.5) | async-done | bytes 294944 | tf_op jit(solution)/shard_map/all_to_all | solution.py:479
  122.9 0.9 shard_map.111
Async XLA Ops:
  2.4 20.2 %all-to-all-start = ((bf16[16,72,128]{2,1,0:T(8,128)(2,1)}), bf16[16,72,128]{2,1,0:T(8,128)(2,1)S(1)}, u32[]{:S(2)}, u32[]{:S(2)}) async-start(bf16[16,72,128]{2,1,0:T(8,128)(2,1)} %get-tuple-element.29), calls=%async_computation | async-start | bytes 589824 | tf_op jit(solution)/shard_map/all_to_all | solution.py:402
  11.6 9.6 %collective-permute-start = (bf16[72,128]{1,0:T(8,128)(2,1)}, bf16[72,128]{1,0:T(8,128)(2,1)S(1)}, u32[]{:S(2)}, u32[]{:S(2)}) collective-permute-start(bf16[72,128]{1,0:T(8,128)(2,1)} %get-tuple-element.28.own_ref), channel_id=1, source_target_pairs={{0,32},{16,48},{32,0},{48,16},{64,96},{80,112},{96,64},{112,80},{1... | collective-permute-start | bytes 55304 | tf_op jit(solution)/shard_map/ppermute | solution.py:401
  21.1 0.7 copy-start
  22.5 9.2 %all-to-all-start.1 = ((bf16[4,2,72,128]{3,2,1,0:T(8,128)(2,1)}), bf16[4,2,72,128]{3,2,1,0:T(8,128)(2,1)S(1)}, u32[]{:S(2)}, u32[]{:S(2)}) async-start(bf16[4,2,72,128]{3,2,1,0:T(8,128)(2,1)} %shard_map.102), calls=%async_computation.1 | async-start | bytes 294912 | tf_op jit(solution)/shard_map/all_to_all | solution.py:408
  44.9 20.9 %all-to-all-start.2 = ((bf16[16,112,128]{2,1,0:T(8,128)(2,1)}), bf16[16,112,128]{2,1,0:T(8,128)(2,1)S(1)}, u32[]{:S(2)}, u32[]{:S(2)}) async-start(bf16[16,112,128]{2,1,0:T(8,128)(2,1)} %get-tuple-element.34), calls=%async_computation.2 | async-start | bytes 917504 | tf_op jit(solution)/shard_map/all_to_all | solution.py:431
  70.3 0.8 copy-start.1
  71.1 13.2 %all-to-all-start.3 = ((bf16[16,24,128]{2,1,0:T(8,128)(2,1)}), bf16[16,24,128]{2,1,0:T(8,128)(2,1)S(1)}, u32[]{:S(2)}, u32[]{:S(2)}) async-start(bf16[16,24,128]{2,1,0:T(8,128)(2,1)} %get-tuple-element.39), calls=%async_computation.3 | async-start | bytes 196608 | tf_op jit(solution)/shard_map/all_to_all | solution.py:442
  82.0 2.3 %collective-permute-start.1 = (bf16[8,72,128]{2,1,0:T(8,128)(2,1)S(1)}, bf16[8,72,128]{2,1,0:T(8,128)(2,1)S(1)}, u32[]{:S(2)}, u32[]{:S(2)}) collective-permute-start(bf16[8,72,128]{2,1,0:T(8,128)(2,1)S(1)} %get-tuple-element.42), channel_id=1, source_target_pairs={{0,16},{16,0},{32,48},{48,32},{64,80},{80,64},{96,112},{112,96},{1... | collective-permute-start | bytes 442376 | tf_op jit(solution)/shard_map/ppermute | solution.py:454
  85.0 15.0 %all-to-all-start.4 = ((bf16[8,96,128]{2,1,0:T(8,128)(2,1)}), bf16[8,96,128]{2,1,0:T(8,128)(2,1)S(1)}, u32[]{:S(2)}, u32[]{:S(2)}) async-start(bf16[8,96,128]{2,1,0:T(8,128)(2,1)} %shard_map.107), calls=%async_computation.4 | async-start | bytes 393216 | tf_op jit(solution)/shard_map/all_to_all | solution.py:458
  100.9 2.6 %collective-permute-start.2 = (f32[24,128]{1,0:T(8,128)S(1)}, f32[24,128]{1,0:T(8,128)S(1)}, u32[]{:S(2)}, u32[]{:S(2)}) collective-permute-start(f32[24,128]{1,0:T(8,128)S(1)} %get-tuple-element.45.shard_ref), channel_id=1, source_target_pairs={{0,16},{16,0},{32,48},{48,32},{64,80},{80,64},{96,112},{112,96},{1... | collective-permute-start | bytes 36872 | tf_op jit(solution)/shard_map/ppermute | solution.py:477
  104.2 18.7 %all-to-all-start.5 = ((bf16[16,72,128]{2,1,0:T(8,128)(2,1)}), bf16[16,72,128]{2,1,0:T(8,128)(2,1)S(1)}, u32[]{:S(2)}, u32[]{:S(2)}) async-start(bf16[16,72,128]{2,1,0:T(8,128)(2,1)} %shard_map.110), calls=%async_computation.5 | async-start | bytes 589824 | tf_op jit(solution)/shard_map/all_to_all | solution.py:479

commit v5 on v4

--- a/solution.py
+++ b/solution.py
@@ -17,8 +17,8 @@
 CELLS = N_I * N_J
 LOW = jnp.bfloat16
 F32 = jnp.float32
-VMEM_LIMIT = 52 * 1024 * 1024
-VMEM_SMALL = 52 * 1024 * 1024
+VMEM_LIMIT = 48 * 1024 * 1024
+VMEM_SMALL = 48 * 1024 * 1024
 
 X_GROUPS = [[4 * x + o for x in range(4)] for o in range(4)]
 CORE_GROUPS = [[2 * k, 2 * k + 1] for k in range(8)]
@@ -209,7 +209,7 @@
 
 
 def scores_kernel(z_ref, q2_ref, o2_ref, kv_ref, bias_ref, e_ref, gp_ref, own_ref, stat_ref, k2_ref, v2_ref, wide_ref):
-    z = z_ref[0]
+    z = (z_ref[0] >> 1) & 1
     for r in range(SIDE):
         wide_ref[r] = kv_ref[r & 1, r >> 2, ((r >> 1) & 1) ^ z].astype(F32)
     unpack_features(wide_ref, k2_ref, v2_ref)
@@ -332,7 +332,7 @@
     blocks_of(sum_ref, key_ref)
     weighted_sums(N_I, tile_of(weight_ref), o2_ref, sum_ref)
     blocks_of(sum_ref, value_ref)
-    first_core = core_ref[0] == 0
+    first_core = (core_ref[0] & 1) == 0
     for k in range(8):
         even = pack_two(key_ref[2 * k], value_ref[2 * k])
         odd = pack_two(key_ref[2 * k + 1], value_ref[2 * k + 1])
@@ -390,6 +390,7 @@
 
 def on_device(pair, w_bias, queries, keys, values, d_out):
     flat_pair = pair.reshape(CELLS, P_SIZE)
+    row_at = lax.axis_index("row").astype(jnp.int32).reshape(1)
     own = pltpu.VMEM((N_I, H), LOW)
     qo_send, kv_own = pl.pallas_call(
         prepare_kernel,
@@ -415,14 +416,12 @@
         cost=pl.CostEstimate(flops=1_000_000_000, bytes_accessed=2_000_000, transcendentals=0),
     )
     kv = lax.all_gather(kv, "row", axis_index_groups=CORE_GROUPS)
-    row_at = lax.axis_index("row").astype(jnp.int32).reshape(1)
-    z, core = (row_at >> 1) & 1, row_at & 1
     e, gp, own_stats, stats, k2, v2 = call(
         scores_kernel,
         [array((CELLS, LANES), F32)] * 2
         + [array((3, N_I, LANES), F32), array((SIDE, STAT_ROWS, LANES), LOW)]
         + [feature] * 2,
-        z, q2, o2, kv, bias,
+        row_at, q2, o2, kv, bias,
         smem=1,
         limit=VMEM_LIMIT,
         scratch=[pltpu.VMEM((SIDE, PAIR_ROWS, LANES), F32)],
@@ -445,7 +444,7 @@
     mine, other = call(
         key_kernel,
         [array((8, PAIR_ROWS, LANES), LOW)] * 2,
-        core, score, weight, q2, o2,
+        row_at, score, weight, q2, o2,
         smem=1,
         limit=VMEM_LIMIT,
         scratch=[pltpu.VMEM((HD, N_J, LANES), F32), blocks, blocks],

time: 125 us -> 118 us (0.944)
  blocking collectives: 5.13 us -> 26.1 us
  waiting for transfers between devices: 34.6 us -> 20.9 us
  starting transfers between devices: 44.6 us -> 37.1 us
  Pallas kernels: 30.7 us -> 26 us
    all_to_all x0 -> x1, blocking collectives: none -> 20.7 us  [on_device(): stats = lax.all_to_all(stats, 'col', 0, 0)]
    all_to_all x1 -> x0, waiting for transfers between devices: 14.3 us -> none  [on_device(): stats = lax.all_to_all(stats, 'col', 0, 0)]
    all_to_all x1 -> x0, starting transfers between devices: 6.52 us -> none  [on_device(): stats = lax.all_to_all(stats, 'col', 0, 0)]
    pallas_call x9, Pallas kernels: 24.5 us -> 21.3 us  [call(): pl.pallas_call(kernel, out_shape=out_shape, in_specs=specs, out_specs=out...]
    pallas_call x1, Pallas kernels: 4.47 us -> 3 us  [on_device(): pl.pallas_call(grad_kernel, out_shape=[array((CELLS, LANES), LOW)] * 2 +...]
  transfers between devices with their start and end apart: 9 -> 8, of which waited for: 6 -> 6; matrix products, arithmetic and copies ran while one was open for 5% -> 5% of each run, Pallas kernels for 11% -> 10%
where the time goes in v5:
time: 118 us; the launch traced here: 117 us
  starting transfers between devices  37.1 us (31%)
  blocking collectives  26.1 us (22%)
  Pallas kernels  26 us (22%)
  waiting for transfers between devices  20.9 us (18%)
  matrix products  4.61 us (4%)
  local copies, waits for them, and re-layouts  1.65 us (1%)
    pallas_call x9, Pallas kernels, call(): pl.pallas_call(kernel, out_shape=out_shape, in_specs=specs, out_specs=out...  21.3 us
    all_to_all x1, blocking collectives, on_device(): stats = lax.all_to_all(stats, 'col', 0, 0)  20.7 us
    all_to_all x1, starting transfers between devices, on_device(): qo = lax.all_to_all(qo_send, 'col', 0, 0)  9.2 us
    all_to_all x1, waiting for transfers between devices, on_device(): col_recv = lax.all_to_all(col_send, 'col', 0, 0)  8.31 us
    all_to_all x1, starting transfers between devices, on_device(): col_recv = lax.all_to_all(col_send, 'col', 0, 0)  7.24 us
    all_to_all x1, waiting for transfers between devices, on_device(): lax.all_to_all(row_send, 'row', 0, 0, axis_index_groups=CORE_APART)  5.73 us
    all_gather x1, blocking collectives, on_device(): kv = lax.all_gather(kv, 'row', axis_index_groups=CORE_GROUPS)  5.44 us
    ppermute x1, waiting for transfers between devices, on_device(): kv_other = lax.ppermute(kv_own, 'row', Z_SWAP)  4.32 us
  transfers between devices with their start and end apart: 8, of which 6 were waited for; matrix products, arithmetic and copies ran while one was open for 5% of the time, Pallas kernels for 10%

profile of v5, /device:TPU:1, one launch (start us, length us, event | category | flops | bytes accessed | tf_op | source)
XLA Modules:
  0.0 117.1 jit_solution(13197951281757760341)
XLA Ops:
  0.6 1.7 %shard_map.101 = (bf16[16,72,128]{2,1,0:T(8,128)(2,1)}, bf16[72,128]{1,0:T(8,128)(2,1)}) custom-call(bf16[48,96]{1,0:T(8,128)(2,1)} %q_hbm.1, bf16[48,96]{1,0:T(8,128)(2,1)} %o_hbm.1, bf16[48,96]{1,0:T(8,128)(2,1)} %k_hbm.1, bf16[48,96]{1,0:T(8,128)(2,1)} %v_hbm.1), custom_call_target="tpu_custom_call" | custom-call | tf_op jit(solution)/shard_map/pallas_call | solution.py:395
  2.4 9.2 %all-to-all-start = ((bf16[16,72,128]{2,1,0:T(8,128)(2,1)}), bf16[16,72,128]{2,1,0:T(8,128)(2,1)S(1)}, u32[]{:S(2)}, u32[]{:S(2)}) async-start(bf16[16,72,128]{2,1,0:T(8,128)(2,1)} %get-tuple-element.29), calls=%async_computation | async-start | bytes 589824 | tf_op jit(solution)/shard_map/all_to_all | solution.py:403
  11.6 4.3 %collective-permute-start = (bf16[72,128]{1,0:T(8,128)(2,1)}, bf16[72,128]{1,0:T(8,128)(2,1)S(1)}, u32[]{:S(2)}, u32[]{:S(2)}) collective-permute-start(bf16[72,128]{1,0:T(8,128)(2,1)} %get-tuple-element.28.own_ref), channel_id=1, source_target_pairs={{0,32},{16,48},{32,0},{48,16},{64,96},{80,112},{96,64},{112,80},{1... | collective-permute-start | bytes 55304 | tf_op jit(solution)/shard_map/ppermute | solution.py:402
  15.9 0.9 reshape.26
  16.8 4.3 %collective-permute-done.other_ref = bf16[72,128]{1,0:T(8,128)(2,1)S(1)} collective-permute-done((bf16[72,128]{1,0:T(8,128)(2,1)}, bf16[72,128]{1,0:T(8,128)(2,1)S(1)}, u32[]{:S(2)}, u32[]{:S(2)}) %collective-permute-start) | collective-permute-done | bytes 18464 | tf_op jit(solution)/shard_map/ppermute | solution.py:402
  21.1 0.0 copy-start
  21.1 0.7 copy-done
  21.9 0.7 shard_map.102
  22.5 0.0 all-to-all-done.qo_ref
  22.5 4.0 %all-to-all-start.1 = ((bf16[4,2,72,128]{3,2,1,0:T(8,128)(2,1)}), bf16[4,2,72,128]{3,2,1,0:T(8,128)(2,1)S(1)}, u32[]{:S(2)}, u32[]{:S(2)}) async-start(bf16[4,2,72,128]{3,2,1,0:T(8,128)(2,1)} %shard_map.102), calls=%async_computation.1 | async-start | bytes 294912 | tf_op jit(solution)/shard_map/all_to_all | solution.py:409
  26.6 2.4 %convolution_bitcast_fusion.bias_ref = f32[2304,128]{1,0:T(8,128)S(1)} fusion(bf16[2304,512]{1,0:T(8,128)(2,1)} %bitcast.16, bf16[16,6,512]{2,1,0:T(8,128)(2,1)S(1)} %reshape.26), kind=kOutput, calls=%fused_computation.1 | convolution fusion | flops 301989888 | bytes 3637248 | tf_op jit(solution)/shard_map/dot_general | solution.py:68
  29.0 1.8 %shard_map.103 = (f32[16,48,128]{2,1,0:T(8,128)S(1)}, f32[16,48,128]{2,1,0:T(8,128)S(1)}) custom-call(bf16[16,72,128]{2,1,0:T(8,128)(2,1)S(1)} %all-to-all-done.qo_ref), custom_call_target="tpu_custom_call" | custom-call | flops 1000000000 | bytes 2000000 | tf_op jit(solution)/shard_map/pallas_call | solution.py:38
  30.8 0.7 all-to-all-done.1
  31.5 5.4 %all-gather = bf16[8,2,72,128]{3,2,1,0:T(8,128)(2,1)S(1)} all-gather(bf16[4,2,72,128]{3,2,1,0:T(8,128)(2,1)S(1)} %all-to-all-done.1), channel_id=2, replica_groups={{0,16},{32,48},{64,80},{96,112},{128,144},{160,176},{192,208},{224,240}..., dimensions={0}, use_global_device_ids=true | all-gather | bytes 442368 | tf_op jit(solution)/shard_map/all_gather | solution.py:418
  36.9 5.8 %shard_map.104 = (f32[2304,128]{1,0:T(8,128)S(1)}, f32[2304,128]{1,0:T(8,128)S(1)}, f32[3,48,128]{2,1,0:T(8,128)S(1)}, bf16[16,112,128]{2,1,0:T(8,128)(2,1)S(1)}...) custom-call(s32[1]{0:T(128)} %bitcast.z_ref.core_ref, f32[16,48,128]{2,1,0:T(8,128)S(1)} %get-tuple-element.31.q2_ref, ...), custom_call_target="tpu_custom_call" | custom-call | tf_op jit(solution)/shard_map/pallas_call | solution.py:38
  42.8 20.7 %all_to_all.30.stat_ref = bf16[16,112,128]{2,1,0:T(8,128)(2,1)S(1)} all-to-all(bf16[16,112,128]{2,1,0:T(8,128)(2,1)S(1)} %get-tuple-element.34), channel_id=1, replica_groups=mesh['row'=16,'col'=16] {'col'}, dimensions={0} | all-to-all | bytes 917504 | tf_op jit(solution)/shard_map/all_to_all | solution.py:430
  63.4 3.0 %shard_map.105 = (bf16[2304,128]{1,0:T(8,128)(2,1)S(1)}, bf16[2304,128]{1,0:T(8,128)(2,1)S(1)}, bf16[16,24,128]{2,1,0:T(8,128)(2,1)}) custom-call(bf16[16,112,128]{2,1,0:T(8,128)(2,1)S(1)} %all_to_all.30.stat_ref, f32[3,48,128]{2,1,0:T(8,128)S(1)} %get-tuple-element.35.own_ref, f32[2304,128]{1,0:T(8,128)S(1)} %get-tuple-element.36.e_ref, ...), custom_call_target="tpu_custom_call" | custom-call | tf_op jit(solution)/shard_map/pallas_call | solution.py:432
  66.4 4.0 %all-to-all-start.3 = ((bf16[16,24,128]{2,1,0:T(8,128)(2,1)}), bf16[16,24,128]{2,1,0:T(8,128)(2,1)S(1)}, u32[]{:S(2)}, u32[]{:S(2)}) async-start(bf16[16,24,128]{2,1,0:T(8,128)(2,1)} %get-tuple-element.39), calls=%async_computation.3 | async-start | bytes 196608 | tf_op jit(solution)/shard_map/all_to_all | solution.py:441
  70.4 5.8 %shard_map.106 = (bf16[8,72,128]{2,1,0:T(8,128)(2,1)S(1)}, bf16[8,72,128]{2,1,0:T(8,128)(2,1)S(1)}) custom-call(s32[1]{0:T(128)} %bitcast.z_ref.core_ref, bf16[2304,128]{1,0:T(8,128)(2,1)S(1)} %get-tuple-element.38.score_ref, bf16[2304,128]{1,0:T(8,128)(2,1)S(1)} %get-tuple-element.40.weight_ref, f32[16,48,128]{2,1,0:T(8,128)S(1)} %get-tuple-element.31.q2_ref, ...), custom_call_target="tpu_custom_call" | custom-call | flops 4000000000 | bytes 4000000 | tf_op jit(solution)/shard_map/pallas_call | solution.py:38
  76.2 1.3 %collective-permute-start.1 = (bf16[8,72,128]{2,1,0:T(8,128)(2,1)S(1)}, bf16[8,72,128]{2,1,0:T(8,128)(2,1)S(1)}, u32[]{:S(2)}, u32[]{:S(2)}) collective-permute-start(bf16[8,72,128]{2,1,0:T(8,128)(2,1)S(1)} %get-tuple-element.42), channel_id=1, source_target_pairs={{0,16},{16,0},{32,48},{48,32},{64,80},{80,64},{96,112},{112,96},{1... | collective-permute-start | bytes 442376 | tf_op jit(solution)/shard_map/ppermute | solution.py:453
  77.6 1.0 collective-permute-done.1.partner_ref
  78.6 0.0 all-to-all-done.3.part_ref
  78.6 0.7 shard_map.107
  79.3 4.2 %all-to-all-start.4 = ((bf16[8,96,128]{2,1,0:T(8,128)(2,1)}), bf16[8,96,128]{2,1,0:T(8,128)(2,1)S(1)}, u32[]{:S(2)}, u32[]{:S(2)}) async-start(bf16[8,96,128]{2,1,0:T(8,128)(2,1)} %shard_map.107), calls=%async_computation.4 | async-start | bytes 393216 | tf_op jit(solution)/shard_map/all_to_all | solution.py:457
  83.5 4.0 %shard_map.108.query_ref = bf16[16,48,128]{2,1,0:T(8,128)(2,1)S(1)} custom-call(bf16[2304,128]{1,0:T(8,128)(2,1)S(1)} %get-tuple-element.38.score_ref, f32[16,48,128]{2,1,0:T(8,128)S(1)} %get-tuple-element.43.k2_ref), custom_call_target="tpu_custom_call" | custom-call | flops 4000000000 | bytes 4000000 | tf_op jit(solution)/shard_map/pallas_call | solution.py:38
  87.6 5.7 %all-to-all-done.4.recv_ref = bf16[8,96,128]{2,1,0:T(8,128)(2,1)S(1)} async-done(((bf16[8,96,128]{2,1,0:T(8,128)(2,1)}), bf16[8,96,128]{2,1,0:T(8,128)(2,1)S(1)}, u32[]{:S(2)}, u32[]{:S(2)}) %all-to-all-start.4) | async-done | bytes 196640 | tf_op jit(solution)/shard_map/all_to_all | solution.py:457
  93.3 0.8 shard_map.109
  94.1 2.8 %collective-permute-start.2 = (f32[24,128]{1,0:T(8,128)S(1)}, f32[24,128]{1,0:T(8,128)S(1)}, u32[]{:S(2)}, u32[]{:S(2)}) collective-permute-start(f32[24,128]{1,0:T(8,128)S(1)} %get-tuple-element.45.shard_ref), channel_id=1, source_target_pairs={{0,16},{16,0},{32,48},{48,32},{64,80},{80,64},{96,112},{112,96},{1... | collective-permute-start | bytes 36872 | tf_op jit(solution)/shard_map/ppermute | solution.py:476
  96.9 0.8 collective-permute-done.2.partner_ref
  97.7 0.7 shard_map.110
  98.5 7.2 %all-to-all-start.5 = ((bf16[16,72,128]{2,1,0:T(8,128)(2,1)}), bf16[16,72,128]{2,1,0:T(8,128)(2,1)S(1)}, u32[]{:S(2)}, u32[]{:S(2)}) async-start(bf16[16,72,128]{2,1,0:T(8,128)(2,1)} %shard_map.110), calls=%async_computation.5 | async-start | bytes 589824 | tf_op jit(solution)/shard_map/all_to_all | solution.py:478
  105.7 2.2 %convolution_convert_fusion = bf16[2304,512]{1,0:T(8,128)(2,1)} fusion(bf16[2304,128]{1,0:T(8,128)(2,1)S(1)} %get-tuple-element.38.score_ref, bf16[16,6,512]{2,1,0:T(8,128)(2,1)S(1)} %reshape.26), kind=kOutput, calls=%fused_computation | convolution fusion | flops 303169536 | bytes 3047424 | tf_op jit(solution)/shard_map/dot_general | solution.py:466
  107.9 8.3 %all-to-all-done.5.recv_ref = bf16[16,72,128]{2,1,0:T(8,128)(2,1)S(1)} async-done(((bf16[16,72,128]{2,1,0:T(8,128)(2,1)}), bf16[16,72,128]{2,1,0:T(8,128)(2,1)S(1)}, u32[]{:S(2)}, u32[]{:S(2)}) %all-to-all-start.5) | async-done | bytes 294944 | tf_op jit(solution)/shard_map/all_to_all | solution.py:478
  116.2 0.9 shard_map.111
Async XLA Ops:
  2.4 20.2 %all-to-all-start = ((bf16[16,72,128]{2,1,0:T(8,128)(2,1)}), bf16[16,72,128]{2,1,0:T(8,128)(2,1)S(1)}, u32[]{:S(2)}, u32[]{:S(2)}) async-start(bf16[16,72,128]{2,1,0:T(8,128)(2,1)} %get-tuple-element.29), calls=%async_computation | async-start | bytes 589824 | tf_op jit(solution)/shard_map/all_to_all | solution.py:403
  11.6 9.6 %collective-permute-start = (bf16[72,128]{1,0:T(8,128)(2,1)}, bf16[72,128]{1,0:T(8,128)(2,1)S(1)}, u32[]{:S(2)}, u32[]{:S(2)}) collective-permute-start(bf16[72,128]{1,0:T(8,128)(2,1)} %get-tuple-element.28.own_ref), channel_id=1, source_target_pairs={{0,32},{16,48},{32,0},{48,16},{64,96},{80,112},{96,64},{112,80},{1... | collective-permute-start | bytes 55304 | tf_op jit(solution)/shard_map/ppermute | solution.py:402
  21.1 0.7 copy-start
  22.5 8.9 %all-to-all-start.1 = ((bf16[4,2,72,128]{3,2,1,0:T(8,128)(2,1)}), bf16[4,2,72,128]{3,2,1,0:T(8,128)(2,1)S(1)}, u32[]{:S(2)}, u32[]{:S(2)}) async-start(bf16[4,2,72,128]{3,2,1,0:T(8,128)(2,1)} %shard_map.102), calls=%async_computation.1 | async-start | bytes 294912 | tf_op jit(solution)/shard_map/all_to_all | solution.py:409
  66.4 12.2 %all-to-all-start.3 = ((bf16[16,24,128]{2,1,0:T(8,128)(2,1)}), bf16[16,24,128]{2,1,0:T(8,128)(2,1)S(1)}, u32[]{:S(2)}, u32[]{:S(2)}) async-start(bf16[16,24,128]{2,1,0:T(8,128)(2,1)} %get-tuple-element.39), calls=%async_computation.3 | async-start | bytes 196608 | tf_op jit(solution)/shard_map/all_to_all | solution.py:441
  76.2 2.3 %collective-permute-start.1 = (bf16[8,72,128]{2,1,0:T(8,128)(2,1)S(1)}, bf16[8,72,128]{2,1,0:T(8,128)(2,1)S(1)}, u32[]{:S(2)}, u32[]{:S(2)}) collective-permute-start(bf16[8,72,128]{2,1,0:T(8,128)(2,1)S(1)} %get-tuple-element.42), channel_id=1, source_target_pairs={{0,16},{16,0},{32,48},{48,32},{64,80},{80,64},{96,112},{112,96},{1... | collective-permute-start | bytes 442376 | tf_op jit(solution)/shard_map/ppermute | solution.py:453
  79.3 14.0 %all-to-all-start.4 = ((bf16[8,96,128]{2,1,0:T(8,128)(2,1)}), bf16[8,96,128]{2,1,0:T(8,128)(2,1)S(1)}, u32[]{:S(2)}, u32[]{:S(2)}) async-start(bf16[8,96,128]{2,1,0:T(8,128)(2,1)} %shard_map.107), calls=%async_computation.4 | async-start | bytes 393216 | tf_op jit(solution)/shard_map/all_to_all | solution.py:457
  94.1 3.6 %collective-permute-start.2 = (f32[24,128]{1,0:T(8,128)S(1)}, f32[24,128]{1,0:T(8,128)S(1)}, u32[]{:S(2)}, u32[]{:S(2)}) collective-permute-start(f32[24,128]{1,0:T(8,128)S(1)} %get-tuple-element.45.shard_ref), channel_id=1, source_target_pairs={{0,16},{16,0},{32,48},{48,32},{64,80},{80,64},{96,112},{112,96},{1... | collective-permute-start | bytes 36872 | tf_op jit(solution)/shard_map/ppermute | solution.py:476
  98.5 17.7 %all-to-all-start.5 = ((bf16[16,72,128]{2,1,0:T(8,128)(2,1)}), bf16[16,72,128]{2,1,0:T(8,128)(2,1)S(1)}, u32[]{:S(2)}, u32[]{:S(2)}) async-start(bf16[16,72,128]{2,1,0:T(8,128)(2,1)} %shard_map.110), calls=%async_computation.5 | async-start | bytes 589824 | tf_op jit(solution)/shard_map/all_to_all | solution.py:478

commit v6 on v5

--- a/solution.py
+++ b/solution.py
@@ -20,10 +20,7 @@
 VMEM_LIMIT = 48 * 1024 * 1024
 VMEM_SMALL = 48 * 1024 * 1024
 
-X_GROUPS = [[4 * x + o for x in range(4)] for o in range(4)]
-CORE_GROUPS = [[2 * k, 2 * k + 1] for k in range(8)]
 CORE_APART = [[2 * k + c for k in range(8)] for c in range(2)]
-Z_SWAP = [(r, r ^ 2) for r in range(SIDE)]
 CORE_SWAP = [(r, r ^ 1) for r in range(SIDE)]
 PAIR_ROWS = N_I + N_I // 2
 W_ROWS = 24
@@ -104,13 +101,9 @@
     packed = pack_two(q * (1.0 / HD**0.5), o).astype(LOW)
     for c in range(SIDE):
         qo_ref[c] = packed
-    kv_ref[...] = pack_two(k, v).astype(LOW)
-
-
-def stack_kernel(own_ref, other_ref, out_ref):
-    for x in range(4):
-        out_ref[x, 0] = own_ref[...]
-        out_ref[x, 1] = other_ref[...]
+    packed = pack_two(k, v).astype(LOW)
+    for r in range(8):
+        kv_ref[r] = packed
 
 
 def place_of(shape):
@@ -202,17 +195,18 @@
 STAT_ROWS = 2 * N_I + 16
 
 
-def rows_kernel(qo_ref, q2_ref, o2_ref, wide_ref):
+def keys_kernel(row_ref, kv_ref, partner_ref, k2_ref, v2_ref, wide_ref):
+    own_core = row_ref[0] & 1
+    for k in range(8):
+        wide_ref[2 * k + own_core] = kv_ref[k].astype(F32)
+        wide_ref[2 * k + (1 - own_core)] = partner_ref[k].astype(F32)
+    unpack_features(wide_ref, k2_ref, v2_ref)
+
+
+def scores_kernel(qo_ref, k2_ref, v2_ref, bias_ref, e_ref, gp_ref, own_ref, stat_ref, q2_ref, o2_ref, wide_ref):
     for c in range(SIDE):
         wide_ref[c] = qo_ref[c].astype(F32)
     unpack_features(wide_ref, q2_ref, o2_ref)
-
-
-def scores_kernel(z_ref, q2_ref, o2_ref, kv_ref, bias_ref, e_ref, gp_ref, own_ref, stat_ref, k2_ref, v2_ref, wide_ref):
-    z = (z_ref[0] >> 1) & 1
-    for r in range(SIDE):
-        wide_ref[r] = kv_ref[r & 1, r >> 2, ((r >> 1) & 1) ^ z].astype(F32)
-    unpack_features(wide_ref, k2_ref, v2_ref)
 
     def rows(pair_at, carry):
         here = [2 * pair_at, 2 * pair_at + 1]
@@ -392,41 +386,39 @@
     flat_pair = pair.reshape(CELLS, P_SIZE)
     row_at = lax.axis_index("row").astype(jnp.int32).reshape(1)
     own = pltpu.VMEM((N_I, H), LOW)
-    qo_send, kv_own = pl.pallas_call(
+    qo_send, kv_send = pl.pallas_call(
         prepare_kernel,
-        out_shape=[array((SIDE, PAIR_ROWS, LANES), LOW), array((PAIR_ROWS, LANES), LOW)],
+        out_shape=[array((SIDE, PAIR_ROWS, LANES), LOW), array((8, PAIR_ROWS, LANES), LOW)],
         in_specs=[pl.BlockSpec(memory_space=pl.ANY)] * 4,
         out_specs=[pl.BlockSpec(memory_space=pltpu.VMEM)] * 2,
         scratch_shapes=[own] * 4 + [pltpu.SemaphoreType.DMA((4,))],
     )(queries, d_out, keys, values)
-    kv_other = lax.ppermute(kv_own, "row", Z_SWAP)
-    qo = lax.all_to_all(qo_send, "col", 0, 0)
+    kv = lax.all_to_all(kv_send, "row", 0, 0, axis_index_groups=CORE_APART)
     wide = jnp.pad(w_bias.T.reshape(SIDE, PLACES, P_SIZE), ((0, 0), (0, 2), (0, 0)))
     wide = wide.reshape(LANES, P_SIZE)
     bias = contract(flat_pair, wide, 1, 1)
-    kv_send = call(stack_kernel, array((4, 2, PAIR_ROWS, LANES), LOW), kv_own, kv_other)
-    kv_send, qo = lax.optimization_barrier((kv_send, qo))
-    kv = lax.all_to_all(kv_send, "row", 0, 0, axis_index_groups=X_GROUPS)
+    qo_send, kv, bias = lax.optimization_barrier((qo_send, kv, bias))
+    qo = lax.all_to_all(qo_send, "col", 0, 0)
+    kv_partner = lax.ppermute(kv, "row", CORE_SWAP)
     feature = array((HD, N_I, LANES), F32)
-    q2, o2 = call(
-        rows_kernel,
+    wide_blocks = pltpu.VMEM((SIDE, PAIR_ROWS, LANES), F32)
+    k2, v2 = call(
+        keys_kernel,
         [feature] * 2,
-        qo,
-        scratch=[pltpu.VMEM((SIDE, PAIR_ROWS, LANES), F32)],
+        row_at, kv, kv_partner,
+        smem=1,
+        limit=VMEM_LIMIT,
+        scratch=[wide_blocks],
         cost=pl.CostEstimate(flops=1_000_000_000, bytes_accessed=2_000_000, transcendentals=0),
     )
-    kv = lax.all_gather(kv, "row", axis_index_groups=CORE_GROUPS)
-    e, gp, own_stats, stats, k2, v2 = call(
+    e, gp, own_stats, stats, q2, o2 = call(
         scores_kernel,
         [array((CELLS, LANES), F32)] * 2
         + [array((3, N_I, LANES), F32), array((SIDE, STAT_ROWS, LANES), LOW)]
         + [feature] * 2,
-        row_at, q2, o2, kv, bias,
-        smem=1,
-        limit=VMEM_LIMIT,
-        scratch=[pltpu.VMEM((SIDE, PAIR_ROWS, LANES), F32)],
-    )
-    del v2
+        qo, k2, v2, bias,
+        scratch=[wide_blocks],
+    )
     stats = lax.all_to_all(stats, "col", 0, 0)
     vmem = pl.BlockSpec(memory_space=pltpu.VMEM)
     score, weight, part = pl.pallas_call(

time: 118 us -> 116 us (0.983)
  blocking collectives: 26.1 us -> 19 us
  waiting for transfers between devices: 20.9 us -> 24.9 us
  starting transfers between devices: 37.1 us -> 39.1 us
    all_to_all x1, starting transfers between devices: 4.01 us -> 11.5 us  [on_device(): kv = lax.all_to_all(kv_send, 'row', 0, 0, axis_index_groups=CORE_APART)]
    all_gather x1 -> x0, blocking collectives: 5.44 us -> none  [on_device(): kv = lax.all_gather(kv, 'row', axis_index_groups=CORE_GROUPS)]
    all_to_all x1, waiting for transfers between devices: 0.71 us -> 6.14 us  [on_device(): kv = lax.all_to_all(kv_send, 'row', 0, 0, axis_index_groups=CORE_APART)]
    all_to_all x1, starting transfers between devices: 9.2 us -> 5.66 us  [on_device(): qo = lax.all_to_all(qo_send, 'col', 0, 0)]
    ppermute x1, waiting for transfers between devices: 4.32 us -> 1.01 us  [on_device(): kv_partner = lax.ppermute(kv, 'row', CORE_SWAP)]
    all_to_all x1, waiting for transfers between devices: 0.01 us -> 1.96 us  [on_device(): qo = lax.all_to_all(qo_send, 'col', 0, 0)]
    all_to_all x1, blocking collectives: 20.7 us -> 19 us  [on_device(): stats = lax.all_to_all(stats, 'col', 0, 0)]
    ppermute x1, starting transfers between devices: 4.3 us -> 2.97 us  [on_device(): kv_partner = lax.ppermute(kv, 'row', CORE_SWAP)]
  transfers between devices with their start and end apart: 8 -> 8, of which waited for: 6 -> 7; matrix products, arithmetic and copies ran while one was open for 5% -> 5% of each run, Pallas kernels for 10% -> 11%
where the time goes in v6:
time: 116 us; the launch traced here: 115 us
  starting transfers between devices  39.1 us (34%)
  Pallas kernels  25.7 us (22%)
  waiting for transfers between devices  24.9 us (21%)
  blocking collectives  19 us (16%)
  matrix products  4.61 us (4%)
    pallas_call x8, Pallas kernels, call(): pl.pallas_call(kernel, out_shape=out_shape, in_specs=specs, out_specs=out...  20.9 us
    all_to_all x1, blocking collectives, on_device(): stats = lax.all_to_all(stats, 'col', 0, 0)  19 us
    all_to_all x1, starting transfers between devices, on_device(): kv = lax.all_to_all(kv_send, 'row', 0, 0, axis_index_groups=CORE_APART)  11.5 us
    all_to_all x1, waiting for transfers between devices, on_device(): col_recv = lax.all_to_all(col_send, 'col', 0, 0)  8.31 us
    all_to_all x1, starting transfers between devices, on_device(): col_recv = lax.all_to_all(col_send, 'col', 0, 0)  7.24 us
    all_to_all x1, waiting for transfers between devices, on_device(): kv = lax.all_to_all(kv_send, 'row', 0, 0, axis_index_groups=CORE_APART)  6.14 us
    all_to_all x1, waiting for transfers between devices, on_device(): lax.all_to_all(row_send, 'row', 0, 0, axis_index_groups=CORE_APART)  5.67 us
    all_to_all x1, starting transfers between devices, on_device(): qo = lax.all_to_all(qo_send, 'col', 0, 0)  5.66 us
  transfers between devices with their start and end apart: 8, of which 7 were waited for; matrix products, arithmetic and copies ran while one was open for 5% of the time, Pallas kernels for 11%

profile of v6, /device:TPU:1, one launch (start us, length us, event | category | flops | bytes accessed | tf_op | source)
XLA Modules:
  0.0 115.1 jit_solution(3419315646679527242)
XLA Ops:
  0.6 1.8 %shard_map.101 = (bf16[16,72,128]{2,1,0:T(8,128)(2,1)}, bf16[8,72,128]{2,1,0:T(8,128)(2,1)}) custom-call(bf16[48,96]{1,0:T(8,128)(2,1)} %q_hbm.1, bf16[48,96]{1,0:T(8,128)(2,1)} %o_hbm.1, bf16[48,96]{1,0:T(8,128)(2,1)} %k_hbm.1, bf16[48,96]{1,0:T(8,128)(2,1)} %v_hbm.1), custom_call_target="tpu_custom_call" | custom-call | tf_op jit(solution)/shard_map/pallas_call | solution.py:389
  2.4 11.5 %all-to-all-start = ((bf16[8,72,128]{2,1,0:T(8,128)(2,1)}), bf16[8,72,128]{2,1,0:T(8,128)(2,1)S(1)}, u32[]{:S(2)}, u32[]{:S(2)}) async-start(bf16[8,72,128]{2,1,0:T(8,128)(2,1)} %get-tuple-element.31), calls=%async_computation | async-start | bytes 294912 | tf_op jit(solution)/shard_map/all_to_all | solution.py:396
  13.9 0.9 reshape.25
  14.8 2.4 %convolution_bitcast_fusion.bias_ref = f32[2304,128]{1,0:T(8,128)S(1)} fusion(bf16[2304,512]{1,0:T(8,128)(2,1)} %bitcast.14, bf16[16,6,512]{2,1,0:T(8,128)(2,1)S(1)} %reshape.25), kind=kOutput, calls=%fused_computation.1 | convolution fusion | flops 301989888 | bytes 3637248 | tf_op jit(solution)/shard_map/dot_general | solution.py:65
  17.3 6.1 %all-to-all-done.kv_ref = bf16[8,72,128]{2,1,0:T(8,128)(2,1)S(1)} async-done(((bf16[8,72,128]{2,1,0:T(8,128)(2,1)}), bf16[8,72,128]{2,1,0:T(8,128)(2,1)S(1)}, u32[]{:S(2)}, u32[]{:S(2)}) %all-to-all-start) | async-done | bytes 147488 | tf_op jit(solution)/shard_map/all_to_all | solution.py:396
  23.4 5.7 %all-to-all-start.1 = ((bf16[16,72,128]{2,1,0:T(8,128)(2,1)}), bf16[16,72,128]{2,1,0:T(8,128)(2,1)S(1)}, u32[]{:S(2)}, u32[]{:S(2)}) async-start(bf16[16,72,128]{2,1,0:T(8,128)(2,1)} %get-tuple-element.32), calls=%async_computation.1 | async-start | bytes 589824 | tf_op jit(solution)/shard_map/all_to_all | solution.py:401
  29.1 3.0 %collective-permute-start = (bf16[8,72,128]{2,1,0:T(8,128)(2,1)S(1)}, bf16[8,72,128]{2,1,0:T(8,128)(2,1)S(1)}, u32[]{:S(2)}, u32[]{:S(2)}) collective-permute-start(bf16[8,72,128]{2,1,0:T(8,128)(2,1)S(1)} %all-to-all-done.kv_ref), channel_id=1, source_target_pairs={{0,16},{16,0},{32,48},{48,32},{64,80},{80,64},{96,112},{112,96},{1... | collective-permute-start | bytes 442376 | tf_op jit(solution)/shard_map/ppermute | solution.py:402
  32.1 1.0 collective-permute-done.partner_ref
  33.1 2.6 %shard_map.102 = (f32[16,48,128]{2,1,0:T(8,128)S(1)}, f32[16,48,128]{2,1,0:T(8,128)S(1)}) custom-call(s32[1]{0:T(128)} %bitcast.4.row_ref.core_ref, bf16[8,72,128]{2,1,0:T(8,128)(2,1)S(1)} %all-to-all-done.kv_ref, bf16[8,72,128]{2,1,0:T(8,128)(2,1)S(1)} %collective-permute-done.partner_ref), custom_call_target="tpu_custom_call" | custom-call | flops 1000000000 | bytes 2000000 | tf_op jit(solution)/shard_map/pallas_call | solution.py:35
  35.7 2.0 %all-to-all-done.1.qo_ref = bf16[16,72,128]{2,1,0:T(8,128)(2,1)S(1)} async-done(((bf16[16,72,128]{2,1,0:T(8,128)(2,1)}), bf16[16,72,128]{2,1,0:T(8,128)(2,1)S(1)}, u32[]{:S(2)}, u32[]{:S(2)}) %all-to-all-start.1) | async-done | bytes 294944 | tf_op jit(solution)/shard_map/all_to_all | solution.py:401
  37.6 5.3 %shard_map.103 = (f32[2304,128]{1,0:T(8,128)S(1)}, f32[2304,128]{1,0:T(8,128)S(1)}, f32[3,48,128]{2,1,0:T(8,128)S(1)}, bf16[16,112,128]{2,1,0:T(8,128)(2,1)S(1)}...) custom-call(bf16[16,72,128]{2,1,0:T(8,128)(2,1)S(1)} %all-to-all-done.1.qo_ref, ...), custom_call_target="tpu_custom_call" | custom-call | tf_op jit(solution)/shard_map/pallas_call | solution.py:35
  42.9 19.0 %all_to_all.30.stat_ref = bf16[16,112,128]{2,1,0:T(8,128)(2,1)S(1)} all-to-all(bf16[16,112,128]{2,1,0:T(8,128)(2,1)S(1)} %get-tuple-element.37), channel_id=1, replica_groups=mesh['row'=16,'col'=16] {'col'}, dimensions={0} | all-to-all | bytes 917504 | tf_op jit(solution)/shard_map/all_to_all | solution.py:422
  62.0 3.0 %shard_map.104 = (bf16[2304,128]{1,0:T(8,128)(2,1)S(1)}, bf16[2304,128]{1,0:T(8,128)(2,1)S(1)}, bf16[16,24,128]{2,1,0:T(8,128)(2,1)}) custom-call(bf16[16,112,128]{2,1,0:T(8,128)(2,1)S(1)} %all_to_all.30.stat_ref, f32[3,48,128]{2,1,0:T(8,128)S(1)} %get-tuple-element.38.own_ref, f32[2304,128]{1,0:T(8,128)S(1)} %get-tuple-element.39.e_ref, ...), custom_call_target="tpu_custom_call" | custom-call | tf_op jit(solution)/shard_map/pallas_call | solution.py:424
  65.0 3.5 %all-to-all-start.3 = ((bf16[16,24,128]{2,1,0:T(8,128)(2,1)}), bf16[16,24,128]{2,1,0:T(8,128)(2,1)S(1)}, u32[]{:S(2)}, u32[]{:S(2)}) async-start(bf16[16,24,128]{2,1,0:T(8,128)(2,1)} %get-tuple-element.42), calls=%async_computation.3 | async-start | bytes 196608 | tf_op jit(solution)/shard_map/all_to_all | solution.py:433
  68.5 5.8 %shard_map.105 = (bf16[8,72,128]{2,1,0:T(8,128)(2,1)S(1)}, bf16[8,72,128]{2,1,0:T(8,128)(2,1)S(1)}) custom-call(s32[1]{0:T(128)} %bitcast.4.row_ref.core_ref, bf16[2304,128]{1,0:T(8,128)(2,1)S(1)} %get-tuple-element.41.score_ref, bf16[2304,128]{1,0:T(8,128)(2,1)S(1)} %get-tuple-element.43.weight_ref, f32[16,48,128]{2,1,0:T(8,128)S(1)} %get-tuple-element.44.q2_ref, ...), custom_call_target="tpu_custom_call" | custom-call | flops 4000000000 | bytes 4000000 | tf_op jit(solution)/shard_map/pallas_call | solution.py:35
  74.3 2.1 %collective-permute-start.1 = (bf16[8,72,128]{2,1,0:T(8,128)(2,1)S(1)}, bf16[8,72,128]{2,1,0:T(8,128)(2,1)S(1)}, u32[]{:S(2)}, u32[]{:S(2)}) collective-permute-start(bf16[8,72,128]{2,1,0:T(8,128)(2,1)S(1)} %get-tuple-element.47), channel_id=1, source_target_pairs={{0,16},{16,0},{32,48},{48,32},{64,80},{80,64},{96,112},{112,96},{1... | collective-permute-start | bytes 442376 | tf_op jit(solution)/shard_map/ppermute | solution.py:445
  76.4 1.0 collective-permute-done.1.partner_ref
  77.4 0.0 all-to-all-done.3.part_ref
  77.4 0.7 shard_map.106
  78.2 3.4 %all-to-all-start.4 = ((bf16[8,96,128]{2,1,0:T(8,128)(2,1)}), bf16[8,96,128]{2,1,0:T(8,128)(2,1)S(1)}, u32[]{:S(2)}, u32[]{:S(2)}) async-start(bf16[8,96,128]{2,1,0:T(8,128)(2,1)} %shard_map.106), calls=%async_computation.4 | async-start | bytes 393216 | tf_op jit(solution)/shard_map/all_to_all | solution.py:449
  81.6 4.0 %shard_map.107.query_ref = bf16[16,48,128]{2,1,0:T(8,128)(2,1)S(1)} custom-call(bf16[2304,128]{1,0:T(8,128)(2,1)S(1)} %get-tuple-element.41.score_ref, f32[16,48,128]{2,1,0:T(8,128)S(1)} %get-tuple-element.34.k2_ref), custom_call_target="tpu_custom_call" | custom-call | flops 4000000000 | bytes 4000000 | tf_op jit(solution)/shard_map/pallas_call | solution.py:35
  85.6 5.7 %all-to-all-done.4.recv_ref = bf16[8,96,128]{2,1,0:T(8,128)(2,1)S(1)} async-done(((bf16[8,96,128]{2,1,0:T(8,128)(2,1)}), bf16[8,96,128]{2,1,0:T(8,128)(2,1)S(1)}, u32[]{:S(2)}, u32[]{:S(2)}) %all-to-all-start.4) | async-done | bytes 196640 | tf_op jit(solution)/shard_map/all_to_all | solution.py:449
  91.3 0.8 shard_map.108
  92.1 2.8 %collective-permute-start.2 = (f32[24,128]{1,0:T(8,128)S(1)}, f32[24,128]{1,0:T(8,128)S(1)}, u32[]{:S(2)}, u32[]{:S(2)}) collective-permute-start(f32[24,128]{1,0:T(8,128)S(1)} %get-tuple-element.49.shard_ref), channel_id=1, source_target_pairs={{0,16},{16,0},{32,48},{48,32},{64,80},{80,64},{96,112},{112,96},{1... | collective-permute-start | bytes 36872 | tf_op jit(solution)/shard_map/ppermute | solution.py:468
  94.9 0.8 collective-permute-done.2.partner_ref
  95.7 0.7 shard_map.109
  96.4 7.2 %all-to-all-start.5 = ((bf16[16,72,128]{2,1,0:T(8,128)(2,1)}), bf16[16,72,128]{2,1,0:T(8,128)(2,1)S(1)}, u32[]{:S(2)}, u32[]{:S(2)}) async-start(bf16[16,72,128]{2,1,0:T(8,128)(2,1)} %shard_map.109), calls=%async_computation.5 | async-start | bytes 589824 | tf_op jit(solution)/shard_map/all_to_all | solution.py:470
  103.7 2.2 %convolution_convert_fusion = bf16[2304,512]{1,0:T(8,128)(2,1)} fusion(bf16[2304,128]{1,0:T(8,128)(2,1)S(1)} %get-tuple-element.41.score_ref, bf16[16,6,512]{2,1,0:T(8,128)(2,1)S(1)} %reshape.25), kind=kOutput, calls=%fused_computation | convolution fusion | flops 303169536 | bytes 3047424 | tf_op jit(solution)/shard_map/dot_general | solution.py:458
  105.9 8.3 %all-to-all-done.5.recv_ref = bf16[16,72,128]{2,1,0:T(8,128)(2,1)S(1)} async-done(((bf16[16,72,128]{2,1,0:T(8,128)(2,1)}), bf16[16,72,128]{2,1,0:T(8,128)(2,1)S(1)}, u32[]{:S(2)}, u32[]{:S(2)}) %all-to-all-start.5) | async-done | bytes 294944 | tf_op jit(solution)/shard_map/all_to_all | solution.py:470
  114.2 0.9 shard_map.110
Async XLA Ops:
  2.4 21.0 %all-to-all-start = ((bf16[8,72,128]{2,1,0:T(8,128)(2,1)}), bf16[8,72,128]{2,1,0:T(8,128)(2,1)S(1)}, u32[]{:S(2)}, u32[]{:S(2)}) async-start(bf16[8,72,128]{2,1,0:T(8,128)(2,1)} %get-tuple-element.31), calls=%async_computation | async-start | bytes 294912 | tf_op jit(solution)/shard_map/all_to_all | solution.py:396
  23.4 14.2 %all-to-all-start.1 = ((bf16[16,72,128]{2,1,0:T(8,128)(2,1)}), bf16[16,72,128]{2,1,0:T(8,128)(2,1)S(1)}, u32[]{:S(2)}, u32[]{:S(2)}) async-start(bf16[16,72,128]{2,1,0:T(8,128)(2,1)} %get-tuple-element.32), calls=%async_computation.1 | async-start | bytes 589824 | tf_op jit(solution)/shard_map/all_to_all | solution.py:401
  29.1 4.0 %collective-permute-start = (bf16[8,72,128]{2,1,0:T(8,128)(2,1)S(1)}, bf16[8,72,128]{2,1,0:T(8,128)(2,1)S(1)}, u32[]{:S(2)}, u32[]{:S(2)}) collective-permute-start(bf16[8,72,128]{2,1,0:T(8,128)(2,1)S(1)} %all-to-all-done.kv_ref), channel_id=1, source_target_pairs={{0,16},{16,0},{32,48},{48,32},{64,80},{80,64},{96,112},{112,96},{1... | collective-permute-start | bytes 442376 | tf_op jit(solution)/shard_map/ppermute | solution.py:402
  65.0 12.4 %all-to-all-start.3 = ((bf16[16,24,128]{2,1,0:T(8,128)(2,1)}), bf16[16,24,128]{2,1,0:T(8,128)(2,1)S(1)}, u32[]{:S(2)}, u32[]{:S(2)}) async-start(bf16[16,24,128]{2,1,0:T(8,128)(2,1)} %get-tuple-element.42), calls=%async_computation.3 | async-start | bytes 196608 | tf_op jit(solution)/shard_map/all_to_all | solution.py:433
  74.3 3.1 %collective-permute-start.1 = (bf16[8,72,128]{2,1,0:T(8,128)(2,1)S(1)}, bf16[8,72,128]{2,1,0:T(8,128)(2,1)S(1)}, u32[]{:S(2)}, u32[]{:S(2)}) collective-permute-start(bf16[8,72,128]{2,1,0:T(8,128)(2,1)S(1)} %get-tuple-element.47), channel_id=1, source_target_pairs={{0,16},{16,0},{32,48},{48,32},{64,80},{80,64},{96,112},{112,96},{1... | collective-permute-start | bytes 442376 | tf_op jit(solution)/shard_map/ppermute | solution.py:445
  78.2 13.1 %all-to-all-start.4 = ((bf16[8,96,128]{2,1,0:T(8,128)(2,1)}), bf16[8,96,128]{2,1,0:T(8,128)(2,1)S(1)}, u32[]{:S(2)}, u32[]{:S(2)}) async-start(bf16[8,96,128]{2,1,0:T(8,128)(2,1)} %shard_map.106), calls=%async_computation.4 | async-start | bytes 393216 | tf_op jit(solution)/shard_map/all_to_all | solution.py:449
  92.1 3.6 %collective-permute-start.2 = (f32[24,128]{1,0:T(8,128)S(1)}, f32[24,128]{1,0:T(8,128)S(1)}, u32[]{:S(2)}, u32[]{:S(2)}) collective-permute-start(f32[24,128]{1,0:T(8,128)S(1)} %get-tuple-element.49.shard_ref), channel_id=1, source_target_pairs={{0,16},{16,0},{32,48},{48,32},{64,80},{80,64},{96,112},{112,96},{1... | collective-permute-start | bytes 36872 | tf_op jit(solution)/shard_map/ppermute | solution.py:468
  96.4 17.7 %all-to-all-start.5 = ((bf16[16,72,128]{2,1,0:T(8,128)(2,1)}), bf16[16,72,128]{2,1,0:T(8,128)(2,1)S(1)}, u32[]{:S(2)}, u32[]{:S(2)}) async-start(bf16[16,72,128]{2,1,0:T(8,128)(2,1)} %shard_map.109), calls=%async_computation.5 | async-start | bytes 589824 | tf_op jit(solution)/shard_map/all_to_all | solution.py:470

commit v7 on v6

--- a/solution.py
+++ b/solution.py
@@ -131,16 +131,16 @@
 
 
 def unpack_features(wide_ref, first_ref, second_ref):
-    place = place_of((8, LANES))
+    half = N_I // 2
+    place = place_of((half, LANES))
     used = place < PLACES
-    for t in range(N_I // 8):
-        at = slice(8 * t, 8 * t + 8)
-        half = N_I + 8 * (t % 3)
+    for t in range(2):
+        at = slice(half * t, half * t + half)
         first, second = [], []
         for c in range(SIDE):
             top = wide_ref[c, at, :]
-            bottom = wide_ref[c, half : half + 8, :]
-            if t >= 3:
+            bottom = wide_ref[c, N_I:, :]
+            if t:
                 bottom = pltpu.roll(bottom, LANES - 4, 1)
             bottom = jnp.where(place < 2, pltpu.roll(top, LANES - 6, 1), bottom)
             first.append(jnp.where(used, top, 0.0))
@@ -230,7 +230,7 @@
             own_ref[2, pl.ds(i, 1), :] = upper / total
         return carry
 
-    lax.fori_loop(0, N_I // 2, rows, 0)
+    lax.fori_loop(0, N_I // 2, rows, 0, unroll=8)
     packed = [x.astype(LOW) for x in pack_stats(own_ref[0], own_ref[1], own_ref[2])]
     for c in range(SIDE):
         stat_ref[c, :N_I, :] = packed[0]
@@ -296,7 +296,7 @@
 D_BLOCK = 4
 
 
-def weighted_sums(count, load, rows_ref, out_ref):
+def weighted_sums(load, rows_ref, out_ref, unroll):
     for first in range(0, HD, D_BLOCK):
 
         def step(x, sums):
@@ -306,14 +306,14 @@
             )
 
         zero = jnp.zeros((N_J, LANES), F32)
-        sums = lax.fori_loop(0, count, step, (zero,) * D_BLOCK, unroll=2)
+        sums = lax.fori_loop(0, N_I, step, (zero,) * D_BLOCK, unroll=unroll)
         for k in range(D_BLOCK):
             out_ref[first + k] = sums[k]
 
 
-def blocks_of(sum_ref, out_ref):
-    for t in range(N_J // 8):
-        at = slice(8 * t, 8 * t + 8)
+def blocks_of(sum_ref, out_ref, rows):
+    for t in range(N_J // rows):
+        at = slice(rows * t, rows * t + rows)
         for c, part in enumerate(swap_blocks([sum_ref[d, at, :] for d in range(HD)])):
             out_ref[c, at, :] = part
 
@@ -322,10 +322,10 @@
     def tile_of(ref):
         return lambda i: ref[pl.ds(pl.multiple_of(i * N_J, N_J), N_J), :].astype(F32)
 
-    weighted_sums(N_I, tile_of(score_ref), q2_ref, sum_ref)
-    blocks_of(sum_ref, key_ref)
-    weighted_sums(N_I, tile_of(weight_ref), o2_ref, sum_ref)
-    blocks_of(sum_ref, value_ref)
+    weighted_sums(tile_of(score_ref), q2_ref, sum_ref, N_I)
+    blocks_of(sum_ref, key_ref, N_J)
+    weighted_sums(tile_of(weight_ref), o2_ref, sum_ref, N_I)
+    blocks_of(sum_ref, value_ref, N_J)
     first_core = (core_ref[0] & 1) == 0
     for k in range(8):
         even = pack_two(key_ref[2 * k], value_ref[2 * k])
@@ -336,16 +336,16 @@
 
 def query_kernel(score_ref, k2_ref, out_ref, wide_ref, sum_ref, block_ref):
     wide_ref[...] = score_ref[...].astype(F32)
-    weighted_sums(N_J, lambda j: wide_ref[pl.ds(j, N_I, stride=N_J), :], k2_ref, sum_ref)
-    blocks_of(sum_ref, block_ref)
+    weighted_sums(lambda j: wide_ref[pl.ds(j, N_I, stride=N_J), :], k2_ref, sum_ref, 8)
+    blocks_of(sum_ref, block_ref, N_I // 2)
     for c in range(SIDE):
         out_ref[c] = block_ref[c].astype(LOW)
 
 
-def row_send_kernel(part_ref, mine_ref, partner_ref, out_ref):
-    total = part_ref[0].astype(F32)
+def row_send_kernel(part_ref, part_partner_ref, mine_ref, partner_ref, out_ref):
+    total = part_ref[0].astype(F32) + part_partner_ref[0].astype(F32)
     for c in range(1, SIDE):
-        total = total + part_ref[c].astype(F32)
+        total = total + (part_ref[c].astype(F32) + part_partner_ref[c].astype(F32))
     for k in range(8):
         both = mine_ref[k].astype(F32) + partner_ref[k].astype(F32)
         out_ref[k] = jnp.concatenate([both, total], axis=0).astype(LOW)
@@ -355,18 +355,14 @@
     return contract(x.astype(LOW), one_hot_features(), 1, 1).astype(LOW)
 
 
-def row_sum_kernel(recv_ref, key_ref, value_ref, shard_ref):
+def row_sum_kernel(recv_ref, query_ref, key_ref, value_ref, out_ref):
     total = recv_ref[0].astype(F32)
     for k in range(1, 8):
         total = total + recv_ref[k].astype(F32)
     key, value = unpack_two(total[:PAIR_ROWS])
     key_ref[...] = from_block(key)
     value_ref[...] = from_block(value)
-    shard_ref[...] = total[PAIR_ROWS:]
-
-
-def col_send_kernel(shard_ref, partner_ref, query_ref, out_ref):
-    shard = shard_ref[...] + partner_ref[...]
+    shard = total[PAIR_ROWS:]
     for c in range(SIDE):
         out_ref[c] = jnp.concatenate([shard, query_ref[c].astype(F32)], axis=0).astype(LOW)
 
@@ -443,8 +439,11 @@
         cost=vpu_cost,
     )
     partner = lax.ppermute(other, "row", CORE_SWAP)
+    part_partner = lax.ppermute(part, "row", CORE_SWAP)
     row_send = call(
-        row_send_kernel, array((8, PAIR_ROWS + W_ROWS, LANES), LOW), part, mine, partner
+        row_send_kernel,
+        array((8, PAIR_ROWS + W_ROWS, LANES), LOW),
+        part, part_partner, mine, partner,
     )
     row_recv = lax.all_to_all(row_send, "row", 0, 0, axis_index_groups=CORE_APART)
     query_blocks = call(
@@ -456,16 +455,10 @@
         cost=vpu_cost,
     )
     d_pair = jnp.dot(score, wide, preferred_element_type=F32).astype(LOW)
-    row_recv, query_blocks = lax.optimization_barrier((row_recv, query_blocks))
-    d_keys, d_values, shard = call(
+    d_keys, d_values, col_send = call(
         row_sum_kernel,
-        [array((N_J, H), LOW)] * 2 + [array((W_ROWS, LANES), F32)],
-        row_recv,
-    )
-    col_send = call(
-        col_send_kernel,
-        array((SIDE, W_ROWS + N_I, LANES), LOW),
-        shard, lax.ppermute(shard, "row", CORE_SWAP), query_blocks,
+        [array((N_J, H), LOW)] * 2 + [array((SIDE, W_ROWS + N_I, LANES), LOW)],
+        row_recv, query_blocks,
     )
     col_recv = lax.all_to_all(col_send, "col", 0, 0)
     d_queries, d_wbias = call(

time: 116 us -> 110 us (0.948)
  Pallas kernels: 25.7 us -> 19.1 us
  waiting for transfers between devices: 24.9 us -> 27.6 us
  blocking collectives: 19 us -> 16.7 us
    pallas_call x8 -> x7, Pallas kernels: 20.9 us -> 14.3 us  [call(): pl.pallas_call(kernel, out_shape=out_shape, in_specs=specs, out_specs=out...]
    all_to_all x1, starting transfers between devices: 7.24 us -> 4.87 us  [on_device(): col_recv = lax.all_to_all(col_send, 'col', 0, 0)]
    all_to_all x1, blocking collectives: 19 us -> 16.7 us  [on_device(): stats = lax.all_to_all(stats, 'col', 0, 0)]
    all_to_all x1, waiting for transfers between devices: 5.67 us -> 7.05 us  [on_device(): lax.all_to_all(row_send, 'row', 0, 0, axis_index_groups=CORE_APART)]
    all_to_all x1, waiting for transfers between devices: 0.01 us -> 1.22 us  [on_device(): part = lax.all_to_all(part, 'col', 0, 0)]
  transfers between devices with their start and end apart: 8 -> 8, of which waited for: 7 -> 7; matrix products, arithmetic and copies ran while one was open for 5% -> 5% of each run, Pallas kernels for 11% -> 7%
where the time goes in v7:
time: 110 us; the launch traced here: 109 us
  starting transfers between devices  39.7 us (36%)
  waiting for transfers between devices  27.6 us (25%)
  Pallas kernels  19.1 us (17%)
  blocking collectives  16.7 us (15%)
  matrix products  4.6 us (4%)
    all_to_all x1, blocking collectives, on_device(): stats = lax.all_to_all(stats, 'col', 0, 0)  16.7 us
    pallas_call x7, Pallas kernels, call(): pl.pallas_call(kernel, out_shape=out_shape, in_specs=specs, out_specs=out...  14.3 us
    all_to_all x1, starting transfers between devices, on_device(): kv = lax.all_to_all(kv_send, 'row', 0, 0, axis_index_groups=CORE_APART)  11.5 us
    all_to_all x1, waiting for transfers between devices, on_device(): col_recv = lax.all_to_all(col_send, 'col', 0, 0)  8.2 us
    all_to_all x1, waiting for transfers between devices, on_device(): lax.all_to_all(row_send, 'row', 0, 0, axis_index_groups=CORE_APART)  7.05 us
    all_to_all x1, waiting for transfers between devices, on_device(): kv = lax.all_to_all(kv_send, 'row', 0, 0, axis_index_groups=CORE_APART)  6.14 us
    all_to_all x1, starting transfers between devices, on_device(): qo = lax.all_to_all(qo_send, 'col', 0, 0)  5.66 us
    all_to_all x1, starting transfers between devices, on_device(): col_recv = lax.all_to_all(col_send, 'col', 0, 0)  4.87 us
  transfers between devices with their start and end apart: 8, of which 7 were waited for; matrix products, arithmetic and copies ran while one was open for 5% of the time, Pallas kernels for 7%

profile of v7, /device:TPU:1, one launch (start us, length us, event | category | flops | bytes accessed | tf_op | source)
XLA Modules:
  0.0 109.4 jit_solution(2792482053520476314)
XLA Ops:
  0.6 1.8 %shard_map.101 = (bf16[16,72,128]{2,1,0:T(8,128)(2,1)}, bf16[8,72,128]{2,1,0:T(8,128)(2,1)}) custom-call(bf16[48,96]{1,0:T(8,128)(2,1)} %q_hbm.1, bf16[48,96]{1,0:T(8,128)(2,1)} %o_hbm.1, bf16[48,96]{1,0:T(8,128)(2,1)} %k_hbm.1, bf16[48,96]{1,0:T(8,128)(2,1)} %v_hbm.1), custom_call_target="tpu_custom_call" | custom-call | tf_op jit(solution)/shard_map/pallas_call | solution.py:385
  2.4 11.5 %all-to-all-start = ((bf16[8,72,128]{2,1,0:T(8,128)(2,1)}), bf16[8,72,128]{2,1,0:T(8,128)(2,1)S(1)}, u32[]{:S(2)}, u32[]{:S(2)}) async-start(bf16[8,72,128]{2,1,0:T(8,128)(2,1)} %get-tuple-element.29), calls=%async_computation | async-start | bytes 294912 | tf_op jit(solution)/shard_map/all_to_all | solution.py:392
  13.9 0.9 reshape.25
  14.8 2.4 %convolution_bitcast_fusion.bias_ref = f32[2304,128]{1,0:T(8,128)S(1)} fusion(bf16[2304,512]{1,0:T(8,128)(2,1)} %bitcast.14, bf16[16,6,512]{2,1,0:T(8,128)(2,1)S(1)} %reshape.25), kind=kOutput, calls=%fused_computation.1 | convolution fusion | flops 301989888 | bytes 3637248 | tf_op jit(solution)/shard_map/dot_general | solution.py:65
  17.3 6.1 %all-to-all-done.kv_ref = bf16[8,72,128]{2,1,0:T(8,128)(2,1)S(1)} async-done(((bf16[8,72,128]{2,1,0:T(8,128)(2,1)}), bf16[8,72,128]{2,1,0:T(8,128)(2,1)S(1)}, u32[]{:S(2)}, u32[]{:S(2)}) %all-to-all-start) | async-done | bytes 147488 | tf_op jit(solution)/shard_map/all_to_all | solution.py:392
  23.4 5.7 %all-to-all-start.1 = ((bf16[16,72,128]{2,1,0:T(8,128)(2,1)}), bf16[16,72,128]{2,1,0:T(8,128)(2,1)S(1)}, u32[]{:S(2)}, u32[]{:S(2)}) async-start(bf16[16,72,128]{2,1,0:T(8,128)(2,1)} %get-tuple-element.30), calls=%async_computation.1 | async-start | bytes 589824 | tf_op jit(solution)/shard_map/all_to_all | solution.py:397
  29.1 3.0 %collective-permute-start = (bf16[8,72,128]{2,1,0:T(8,128)(2,1)S(1)}, bf16[8,72,128]{2,1,0:T(8,128)(2,1)S(1)}, u32[]{:S(2)}, u32[]{:S(2)}) collective-permute-start(bf16[8,72,128]{2,1,0:T(8,128)(2,1)S(1)} %all-to-all-done.kv_ref), channel_id=1, source_target_pairs={{0,16},{16,0},{32,48},{48,32},{64,80},{80,64},{96,112},{112,96},{1... | collective-permute-start | bytes 442376 | tf_op jit(solution)/shard_map/ppermute | solution.py:398
  32.1 1.0 collective-permute-done.partner_ref
  33.1 1.5 %shard_map.102 = (f32[16,48,128]{2,1,0:T(8,128)S(1)}, f32[16,48,128]{2,1,0:T(8,128)S(1)}) custom-call(s32[1]{0:T(128)} %bitcast.4.row_ref.core_ref, bf16[8,72,128]{2,1,0:T(8,128)(2,1)S(1)} %all-to-all-done.kv_ref, bf16[8,72,128]{2,1,0:T(8,128)(2,1)S(1)} %collective-permute-done.partner_ref), custom_call_target="tpu_custom_call" | custom-call | flops 1000000000 | bytes 2000000 | tf_op jit(solution)/shard_map/pallas_call | solution.py:35
  34.5 3.1 %all-to-all-done.1.qo_ref = bf16[16,72,128]{2,1,0:T(8,128)(2,1)S(1)} async-done(((bf16[16,72,128]{2,1,0:T(8,128)(2,1)}), bf16[16,72,128]{2,1,0:T(8,128)(2,1)S(1)}, u32[]{:S(2)}, u32[]{:S(2)}) %all-to-all-start.1) | async-done | bytes 294944 | tf_op jit(solution)/shard_map/all_to_all | solution.py:397
  37.6 4.1 %shard_map.103 = (f32[2304,128]{1,0:T(8,128)S(1)}, f32[2304,128]{1,0:T(8,128)S(1)}, f32[3,48,128]{2,1,0:T(8,128)S(1)}, bf16[16,112,128]{2,1,0:T(8,128)(2,1)S(1)}...) custom-call(bf16[16,72,128]{2,1,0:T(8,128)(2,1)S(1)} %all-to-all-done.1.qo_ref, ...), custom_call_target="tpu_custom_call" | custom-call | tf_op jit(solution)/shard_map/pallas_call | solution.py:35
  41.7 16.7 %all_to_all.30.stat_ref = bf16[16,112,128]{2,1,0:T(8,128)(2,1)S(1)} all-to-all(bf16[16,112,128]{2,1,0:T(8,128)(2,1)S(1)} %get-tuple-element.35), channel_id=1, replica_groups=mesh['row'=16,'col'=16] {'col'}, dimensions={0} | all-to-all | bytes 917504 | tf_op jit(solution)/shard_map/all_to_all | solution.py:418
  58.4 3.0 %shard_map.104 = (bf16[2304,128]{1,0:T(8,128)(2,1)S(1)}, bf16[2304,128]{1,0:T(8,128)(2,1)S(1)}, bf16[16,24,128]{2,1,0:T(8,128)(2,1)}) custom-call(bf16[16,112,128]{2,1,0:T(8,128)(2,1)S(1)} %all_to_all.30.stat_ref, f32[3,48,128]{2,1,0:T(8,128)S(1)} %get-tuple-element.36.own_ref, f32[2304,128]{1,0:T(8,128)S(1)} %get-tuple-element.37.e_ref, ...), custom_call_target="tpu_custom_call" | custom-call | tf_op jit(solution)/shard_map/pallas_call | solution.py:420
  61.4 4.5 %all-to-all-start.3 = ((bf16[16,24,128]{2,1,0:T(8,128)(2,1)}), bf16[16,24,128]{2,1,0:T(8,128)(2,1)S(1)}, u32[]{:S(2)}, u32[]{:S(2)}) async-start(bf16[16,24,128]{2,1,0:T(8,128)(2,1)} %get-tuple-element.40), calls=%async_computation.3 | async-start | bytes 196608 | tf_op jit(solution)/shard_map/all_to_all | solution.py:429
  65.9 3.5 %shard_map.105 = (bf16[8,72,128]{2,1,0:T(8,128)(2,1)S(1)}, bf16[8,72,128]{2,1,0:T(8,128)(2,1)S(1)}) custom-call(s32[1]{0:T(128)} %bitcast.4.row_ref.core_ref, bf16[2304,128]{1,0:T(8,128)(2,1)S(1)} %get-tuple-element.39.score_ref, bf16[2304,128]{1,0:T(8,128)(2,1)S(1)} %get-tuple-element.41.weight_ref, f32[16,48,128]{2,1,0:T(8,128)S(1)} %get-tuple-element.42.q2_ref, ...), custom_call_target="tpu_custom_call" | custom-call | flops 4000000000 | bytes 4000000 | tf_op jit(solution)/shard_map/pallas_call | solution.py:35
  69.4 2.4 %collective-permute-start.2 = (bf16[8,72,128]{2,1,0:T(8,128)(2,1)S(1)}, bf16[8,72,128]{2,1,0:T(8,128)(2,1)S(1)}, u32[]{:S(2)}, u32[]{:S(2)}) collective-permute-start(bf16[8,72,128]{2,1,0:T(8,128)(2,1)S(1)} %get-tuple-element.45), channel_id=1, source_target_pairs={{0,16},{16,0},{32,48},{48,32},{64,80},{80,64},{96,112},{112,96},{1... | collective-permute-start | bytes 442376 | tf_op jit(solution)/shard_map/ppermute | solution.py:441
  71.8 1.2 %all-to-all-done.3.part_ref = bf16[16,24,128]{2,1,0:T(8,128)(2,1)S(1)} async-done(((bf16[16,24,128]{2,1,0:T(8,128)(2,1)}), bf16[16,24,128]{2,1,0:T(8,128)(2,1)S(1)}, u32[]{:S(2)}, u32[]{:S(2)}) %all-to-all-start.3) | async-done | bytes 98336 | tf_op jit(solution)/shard_map/all_to_all | solution.py:429
  73.0 3.4 %collective-permute-start.1 = (bf16[16,24,128]{2,1,0:T(8,128)(2,1)S(1)}, bf16[16,24,128]{2,1,0:T(8,128)(2,1)S(1)}, u32[]{:S(2)}, u32[]{:S(2)}) collective-permute-start(bf16[16,24,128]{2,1,0:T(8,128)(2,1)S(1)} %all-to-all-done.3.part_ref), channel_id=1, source_target_pairs={{0,16},{16,0},{32,48},{48,32},{64,80},{80,64},{96,112},{112,96},{1... | collective-permute-start | bytes 294920 | tf_op jit(solution)/shard_map/ppermute | solution.py:442
  76.4 0.0 collective-permute-done.2.partner_ref
  76.4 0.9 collective-permute-done.1.part_partner_ref
  77.3 0.7 shard_map.106
  78.1 4.5 %all-to-all-start.4 = ((bf16[8,96,128]{2,1,0:T(8,128)(2,1)}), bf16[8,96,128]{2,1,0:T(8,128)(2,1)S(1)}, u32[]{:S(2)}, u32[]{:S(2)}) async-start(bf16[8,96,128]{2,1,0:T(8,128)(2,1)} %shard_map.106), calls=%async_computation.4 | async-start | bytes 393216 | tf_op jit(solution)/shard_map/all_to_all | solution.py:448
  82.5 2.8 %shard_map.107.query_ref = bf16[16,48,128]{2,1,0:T(8,128)(2,1)S(1)} custom-call(bf16[2304,128]{1,0:T(8,128)(2,1)S(1)} %get-tuple-element.39.score_ref, f32[16,48,128]{2,1,0:T(8,128)S(1)} %get-tuple-element.32.k2_ref), custom_call_target="tpu_custom_call" | custom-call | flops 4000000000 | bytes 4000000 | tf_op jit(solution)/shard_map/pallas_call | solution.py:35
  85.3 7.1 %all-to-all-done.4.recv_ref = bf16[8,96,128]{2,1,0:T(8,128)(2,1)S(1)} async-done(((bf16[8,96,128]{2,1,0:T(8,128)(2,1)}), bf16[8,96,128]{2,1,0:T(8,128)(2,1)S(1)}, u32[]{:S(2)}, u32[]{:S(2)}) %all-to-all-start.4) | async-done | bytes 196640 | tf_op jit(solution)/shard_map/all_to_all | solution.py:448
  92.3 0.9 shard_map.108
  93.3 4.9 %all-to-all-start.5 = ((bf16[16,72,128]{2,1,0:T(8,128)(2,1)}), bf16[16,72,128]{2,1,0:T(8,128)(2,1)S(1)}, u32[]{:S(2)}, u32[]{:S(2)}) async-start(bf16[16,72,128]{2,1,0:T(8,128)(2,1)} %get-tuple-element.46), calls=%async_computation.5 | async-start | bytes 589824 | tf_op jit(solution)/shard_map/all_to_all | solution.py:463
  98.2 2.2 %convolution_convert_fusion = bf16[2304,512]{1,0:T(8,128)(2,1)} fusion(bf16[2304,128]{1,0:T(8,128)(2,1)S(1)} %get-tuple-element.39.score_ref, bf16[16,6,512]{2,1,0:T(8,128)(2,1)S(1)} %reshape.25), kind=kOutput, calls=%fused_computation | convolution fusion | flops 303169536 | bytes 3047424 | tf_op jit(solution)/shard_map/dot_general | solution.py:457
  100.3 8.2 %all-to-all-done.5.recv_ref = bf16[16,72,128]{2,1,0:T(8,128)(2,1)S(1)} async-done(((bf16[16,72,128]{2,1,0:T(8,128)(2,1)}), bf16[16,72,128]{2,1,0:T(8,128)(2,1)S(1)}, u32[]{:S(2)}, u32[]{:S(2)}) %all-to-all-start.5) | async-done | bytes 294944 | tf_op jit(solution)/shard_map/all_to_all | solution.py:463
  108.5 0.9 shard_map.109
Async XLA Ops:
  2.4 21.0 %all-to-all-start = ((bf16[8,72,128]{2,1,0:T(8,128)(2,1)}), bf16[8,72,128]{2,1,0:T(8,128)(2,1)S(1)}, u32[]{:S(2)}, u32[]{:S(2)}) async-start(bf16[8,72,128]{2,1,0:T(8,128)(2,1)} %get-tuple-element.29), calls=%async_computation | async-start | bytes 294912 | tf_op jit(solution)/shard_map/all_to_all | solution.py:392
  23.4 14.2 %all-to-all-start.1 = ((bf16[16,72,128]{2,1,0:T(8,128)(2,1)}), bf16[16,72,128]{2,1,0:T(8,128)(2,1)S(1)}, u32[]{:S(2)}, u32[]{:S(2)}) async-start(bf16[16,72,128]{2,1,0:T(8,128)(2,1)} %get-tuple-element.30), calls=%async_computation.1 | async-start | bytes 589824 | tf_op jit(solution)/shard_map/all_to_all | solution.py:397
  29.1 4.0 %collective-permute-start = (bf16[8,72,128]{2,1,0:T(8,128)(2,1)S(1)}, bf16[8,72,128]{2,1,0:T(8,128)(2,1)S(1)}, u32[]{:S(2)}, u32[]{:S(2)}) collective-permute-start(bf16[8,72,128]{2,1,0:T(8,128)(2,1)S(1)} %all-to-all-done.kv_ref), channel_id=1, source_target_pairs={{0,16},{16,0},{32,48},{48,32},{64,80},{80,64},{96,112},{112,96},{1... | collective-permute-start | bytes 442376 | tf_op jit(solution)/shard_map/ppermute | solution.py:398
  61.4 11.6 %all-to-all-start.3 = ((bf16[16,24,128]{2,1,0:T(8,128)(2,1)}), bf16[16,24,128]{2,1,0:T(8,128)(2,1)S(1)}, u32[]{:S(2)}, u32[]{:S(2)}) async-start(bf16[16,24,128]{2,1,0:T(8,128)(2,1)} %get-tuple-element.40), calls=%async_computation.3 | async-start | bytes 196608 | tf_op jit(solution)/shard_map/all_to_all | solution.py:429
  69.4 7.0 %collective-permute-start.2 = (bf16[8,72,128]{2,1,0:T(8,128)(2,1)S(1)}, bf16[8,72,128]{2,1,0:T(8,128)(2,1)S(1)}, u32[]{:S(2)}, u32[]{:S(2)}) collective-permute-start(bf16[8,72,128]{2,1,0:T(8,128)(2,1)S(1)} %get-tuple-element.45), channel_id=1, source_target_pairs={{0,16},{16,0},{32,48},{48,32},{64,80},{80,64},{96,112},{112,96},{1... | collective-permute-start | bytes 442376 | tf_op jit(solution)/shard_map/ppermute | solution.py:441
  73.0 4.3 %collective-permute-start.1 = (bf16[16,24,128]{2,1,0:T(8,128)(2,1)S(1)}, bf16[16,24,128]{2,1,0:T(8,128)(2,1)S(1)}, u32[]{:S(2)}, u32[]{:S(2)}) collective-permute-start(bf16[16,24,128]{2,1,0:T(8,128)(2,1)S(1)} %all-to-all-done.3.part_ref), channel_id=1, source_target_pairs={{0,16},{16,0},{32,48},{48,32},{64,80},{80,64},{96,112},{112,96},{1... | collective-permute-start | bytes 294920 | tf_op jit(solution)/shard_map/ppermute | solution.py:442
  78.1 14.3 %all-to-all-start.4 = ((bf16[8,96,128]{2,1,0:T(8,128)(2,1)}), bf16[8,96,128]{2,1,0:T(8,128)(2,1)S(1)}, u32[]{:S(2)}, u32[]{:S(2)}) async-start(bf16[8,96,128]{2,1,0:T(8,128)(2,1)} %shard_map.106), calls=%async_computation.4 | async-start | bytes 393216 | tf_op jit(solution)/shard_map/all_to_all | solution.py:448
  93.3 15.2 %all-to-all-start.5 = ((bf16[16,72,128]{2,1,0:T(8,128)(2,1)}), bf16[16,72,128]{2,1,0:T(8,128)(2,1)S(1)}, u32[]{:S(2)}, u32[]{:S(2)}) async-start(bf16[16,72,128]{2,1,0:T(8,128)(2,1)} %get-tuple-element.46), calls=%async_computation.5 | async-start | bytes 589824 | tf_op jit(solution)/shard_map/all_to_all | solution.py:463

commit v8 on v7

--- a/solution.py
+++ b/solution.py
@@ -1,3 +1,5 @@
+import functools
+
 import jax
 import jax.numpy as jnp
 from jax import lax
@@ -83,27 +85,35 @@
     return parts
 
 
-def prepare_kernel(q_hbm, o_hbm, k_hbm, v_hbm, qo_ref, kv_ref, q_ref, o_ref, k_ref, v_ref, sems):
+def load_all(sources, targets, sems):
     copies = [
-        pltpu.make_async_copy(src, dst, sems.at[n])
-        for n, (src, dst) in enumerate(
-            ((q_hbm, q_ref), (o_hbm, o_ref), (k_hbm, k_ref), (v_hbm, v_ref))
-        )
+        pltpu.make_async_copy(source, target, sems.at[n])
+        for n, (source, target) in enumerate(zip(sources, targets))
     ]
     for copy in copies:
         copy.start()
     hot = one_hot_features()
     for copy in copies:
         copy.wait()
-    q, o, k, v = (
-        jnp.dot(ref[...], hot, preferred_element_type=F32) for ref in (q_ref, o_ref, k_ref, v_ref)
-    )
-    packed = pack_two(q * (1.0 / HD**0.5), o).astype(LOW)
-    for c in range(SIDE):
-        qo_ref[c] = packed
-    packed = pack_two(k, v).astype(LOW)
-    for r in range(8):
-        kv_ref[r] = packed
+    return [jnp.dot(target[...], hot, preferred_element_type=F32) for target in targets]
+
+
+def prepare_kernel(scale, first_hbm, second_hbm, out_ref, first_ref, second_ref, sems):
+    first, second = load_all((first_hbm, second_hbm), (first_ref, second_ref), sems)
+    packed = pack_two(first * scale, second).astype(LOW)
+    for n in range(out_ref.shape[0]):
+        out_ref[n] = packed
+
+
+def prepare(first, second, copies, scale):
+    return pl.pallas_call(
+        functools.partial(prepare_kernel, scale),
+        out_shape=array((copies, PAIR_ROWS, LANES), LOW),
+        in_specs=[pl.BlockSpec(memory_space=pl.ANY)] * 2,
+        out_specs=pl.BlockSpec(memory_space=pltpu.VMEM),
+        scratch_shapes=[pltpu.VMEM((N_I, H), LOW)] * 2 + [pltpu.SemaphoreType.DMA((2,))],
+        cost_estimate=pl.CostEstimate(flops=10_000_000, bytes_accessed=400_000, transcendentals=0),
+    )(first, second)
 
 
 def place_of(shape):
@@ -128,6 +138,27 @@
     second = jnp.where(place < 2, pltpu.roll(top, LANES - 6, 1), second)
     used = place < PLACES
     return jnp.where(used, top, 0.0), jnp.where(used, second, 0.0)
+
+
+def fold(x):
+    place = place_of((8, LANES))
+    last = x[40:]
+    tops = [
+        jnp.where(place < PLACES, x[8 * t : 8 * t + 8], pltpu.roll(last, 6 - 2 * t, 1)) for t in range(3)
+    ]
+    return jnp.concatenate(tops + [x[24:40]], axis=0)
+
+
+def unfold(packed):
+    place = place_of((8, LANES))
+    last = pltpu.roll(packed[16:24], LANES - 2, 1)
+    last = jnp.where(place < 4, pltpu.roll(packed[8:16], LANES - 4, 1), last)
+    last = jnp.where(place < 2, pltpu.roll(packed[:8], LANES - 6, 1), last)
+    used = place_of((N_I, LANES)) < PLACES
+    return jnp.where(used, jnp.concatenate([packed, last], axis=0), 0.0)
+
+
+FOLD_ROWS = 40
 
 
 def unpack_features(wide_ref, first_ref, second_ref):
@@ -241,7 +272,7 @@
 PAIR_CUTS = 8
 
 
-def grad_kernel(stat_ref, own_ref, e_ref, gp_ref, pair_hbm, score_ref, weight_ref, part_ref, factor_ref, offset_ref, pair_ref, sems):
+def bias_kernel(pair_hbm, wide_ref, bias_ref, pair_ref, sems):
     cut = CELLS // PAIR_CUTS
     copies = [
         pltpu.make_async_copy(
@@ -251,7 +282,28 @@
     ]
     for copy in copies:
         copy.start()
-
+    for n, copy in enumerate(copies):
+        copy.wait()
+        at = slice(n * cut, n * cut + cut)
+        bias_ref[at, :] = contract(pair_ref[at, :], wide_ref[...], 1, 1)
+
+
+def pair_bias(flat_pair, wide):
+    vmem = pl.BlockSpec(memory_space=pltpu.VMEM)
+    return pl.pallas_call(
+        bias_kernel,
+        out_shape=[array((CELLS, LANES), F32), array((CELLS, P_SIZE), LOW)],
+        in_specs=[pl.BlockSpec(memory_space=pl.ANY), vmem],
+        out_specs=[vmem] * 2,
+        scratch_shapes=[pltpu.SemaphoreType.DMA((PAIR_CUTS,))],
+        cost_estimate=pl.CostEstimate(
+            flops=2 * CELLS * P_SIZE * LANES, bytes_accessed=5_000_000, transcendentals=0
+        ),
+        compiler_params=pltpu.CompilerParams(vmem_limit_bytes=VMEM_LIMIT),
+    )(flat_pair, wide)
+
+
+def grad_kernel(stat_ref, own_ref, e_ref, gp_ref, pair_ref, score_ref, weight_ref, part_ref, factor_ref, offset_ref):
     def stats_of(c):
         return unpack_stats(
             stat_ref[c, :N_I, :].astype(F32),
@@ -286,8 +338,6 @@
         return carry
 
     lax.fori_loop(0, N_I, row, 0, unroll=2)
-    for copy in copies:
-        copy.wait()
     term = contract(score_ref[...], pair_ref[...], 0, 0)
     for c in range(SIDE):
         part_ref[c] = pack_shard(term[8 * c : 8 * c + 8]).astype(LOW)
@@ -339,7 +389,7 @@
     weighted_sums(lambda j: wide_ref[pl.ds(j, N_I, stride=N_J), :], k2_ref, sum_ref, 8)
     blocks_of(sum_ref, block_ref, N_I // 2)
     for c in range(SIDE):
-        out_ref[c] = block_ref[c].astype(LOW)
+        out_ref[c] = fold(block_ref[c]).astype(LOW)
 
 
 def row_send_kernel(part_ref, part_partner_ref, mine_ref, partner_ref, out_ref):
@@ -368,31 +418,25 @@
 
 
 def final_kernel(recv_ref, query_ref, w_ref, wide_ref):
-    total = jnp.zeros((N_I, LANES), F32)
+    total = jnp.zeros((FOLD_ROWS, LANES), F32)
     for c in range(SIDE):
         block = recv_ref[c].astype(F32)
         total = total + block[W_ROWS:]
         for t, tile in enumerate(unpack_shard(block[:W_ROWS])):
             wide_ref[8 * c : 8 * c + 8, LANES * t : LANES * (t + 1)] = tile
-    query_ref[...] = from_block(total * (1.0 / HD**0.5))
+    query_ref[...] = from_block(unfold(total) * (1.0 / HD**0.5))
     w_ref[...] = contract(one_hot_heads(), wide_ref[...].astype(LOW), 1, 0)
 
 
 def on_device(pair, w_bias, queries, keys, values, d_out):
     flat_pair = pair.reshape(CELLS, P_SIZE)
     row_at = lax.axis_index("row").astype(jnp.int32).reshape(1)
-    own = pltpu.VMEM((N_I, H), LOW)
-    qo_send, kv_send = pl.pallas_call(
-        prepare_kernel,
-        out_shape=[array((SIDE, PAIR_ROWS, LANES), LOW), array((8, PAIR_ROWS, LANES), LOW)],
-        in_specs=[pl.BlockSpec(memory_space=pl.ANY)] * 4,
-        out_specs=[pl.BlockSpec(memory_space=pltpu.VMEM)] * 2,
-        scratch_shapes=[own] * 4 + [pltpu.SemaphoreType.DMA((4,))],
-    )(queries, d_out, keys, values)
+    kv_send = prepare(keys, values, 8, 1.0)
+    qo_send = prepare(queries, d_out, SIDE, 1.0 / HD**0.5)
     kv = lax.all_to_all(kv_send, "row", 0, 0, axis_index_groups=CORE_APART)
     wide = jnp.pad(w_bias.T.reshape(SIDE, PLACES, P_SIZE), ((0, 0), (0, 2), (0, 0)))
     wide = wide.reshape(LANES, P_SIZE)
-    bias = contract(flat_pair, wide, 1, 1)
+    bias, held_pair = pair_bias(flat_pair, wide)
     qo_send, kv, bias = lax.optimization_barrier((qo_send, kv, bias))
     qo = lax.all_to_all(qo_send, "col", 0, 0)
     kv_partner = lax.ppermute(kv, "row", CORE_SWAP)
@@ -416,16 +460,12 @@
         scratch=[wide_blocks],
     )
     stats = lax.all_to_all(stats, "col", 0, 0)
-    vmem = pl.BlockSpec(memory_space=pltpu.VMEM)
-    score, weight, part = pl.pallas_call(
+    score, weight, part = call(
         grad_kernel,
-        out_shape=[array((CELLS, LANES), LOW)] * 2 + [array((SIDE, W_ROWS, LANES), LOW)],
-        in_specs=[vmem] * 4 + [pl.BlockSpec(memory_space=pl.ANY)],
-        out_specs=[vmem] * 3,
-        scratch_shapes=[pltpu.VMEM((N_I, LANES), F32)] * 2
-        + [pltpu.VMEM((CELLS, P_SIZE), LOW), pltpu.SemaphoreType.DMA((PAIR_CUTS,))],
-        compiler_params=pltpu.CompilerParams(vmem_limit_bytes=VMEM_LIMIT),
-    )(stats, own_stats, e, gp, flat_pair)
+        [array((CELLS, LANES), LOW)] * 2 + [array((SIDE, W_ROWS, LANES), LOW)],
+        stats, own_stats, e, gp, held_pair,
+        scratch=[pltpu.VMEM((N_I, LANES), F32)] * 2,
+    )
     part = lax.all_to_all(part, "col", 0, 0)
     vpu_cost = pl.CostEstimate(flops=4_000_000_000, bytes_accessed=4_000_000, transcendentals=0)
     blocks = pltpu.VMEM((SIDE, N_J, LANES), F32)
@@ -448,7 +488,7 @@
     row_recv = lax.all_to_all(row_send, "row", 0, 0, axis_index_groups=CORE_APART)
     query_blocks = call(
         query_kernel,
-        array((SIDE, N_I, LANES), LOW),
+        array((SIDE, FOLD_ROWS, LANES), LOW),
         score, k2,
         limit=VMEM_LIMIT,
         scratch=[pltpu.VMEM((CELLS, LANES), F32), pltpu.VMEM((HD, N_I, LANES), F32), blocks],
@@ -457,7 +497,7 @@
     d_pair = jnp.dot(score, wide, preferred_element_type=F32).astype(LOW)
     d_keys, d_values, col_send = call(
         row_sum_kernel,
-        [array((N_J, H), LOW)] * 2 + [array((SIDE, W_ROWS + N_I, LANES), LOW)],
+        [array((N_J, H), LOW)] * 2 + [array((SIDE, W_ROWS + FOLD_ROWS, LANES), LOW)],
         row_recv, query_blocks,
     )
     col_recv = lax.all_to_all(col_send, "col", 0, 0)

time: 110 us -> 114 us (1.036)
  waiting for transfers between devices: 27.6 us -> 20.4 us
  starting transfers between devices: 39.7 us -> 45 us
  Pallas kernels: 19.1 us -> 24.1 us
  local copies, waits for them, and re-layouts: 0.93 us -> 4.01 us
  matrix products: 4.6 us -> 2.17 us
    all_to_all x1, waiting for transfers between devices: 6.14 us -> 0.85 us  [on_device(): kv = lax.all_to_all(kv_send, 'row', 0, 0, axis_index_groups=CORE_APART)]
    all_to_all x1, starting transfers between devices: 4.46 us -> 9.74 us  [on_device(): lax.all_to_all(row_send, 'row', 0, 0, axis_index_groups=CORE_APART)]
    pallas_call x7 -> x8, Pallas kernels: 14.3 us -> 17.9 us  [call(): pl.pallas_call(kernel, out_shape=out_shape, in_specs=specs, out_specs=out...]
    unnamed x0 -> x4, local copies, waits for them, and re-layouts: none -> 3.06 us
    dot_general x1 -> x0, matrix products: 2.44 us -> none  [contract(): lax.dot_general(a, b, (((a_dim,), (b_dim,)), ((), ())), preferred_element...]
    all_to_all x1, waiting for transfers between devices: 8.2 us -> 6.39 us  [on_device(): col_recv = lax.all_to_all(col_send, 'col', 0, 0)]
    pallas_call x2 -> x3, Pallas kernels: 4.78 us -> 6.22 us  [the longest x2 3.28 us: prepare(): pl.pallas_call(functools.partial(prepare_kernel, scale), out_shape=array(...]
  transfers between devices with their start and end apart: 8 -> 8, of which waited for: 7 -> 7; matrix products, arithmetic and copies ran while one was open for 5% -> 3% of each run, Pallas kernels for 7% -> 11%
where the time goes in v8:
time: 114 us; the launch traced here: 113 us
  starting transfers between devices  45 us (39%)
  Pallas kernels  24.1 us (21%)
  waiting for transfers between devices  20.4 us (18%)
  blocking collectives  16.7 us (15%)
  local copies, waits for them, and re-layouts  4.01 us (4%)
  matrix products  2.17 us (2%)
    pallas_call x8, Pallas kernels, call(): pl.pallas_call(kernel, out_shape=out_shape, in_specs=specs, out_specs=out...  17.9 us
    all_to_all x1, blocking collectives, on_device(): stats = lax.all_to_all(stats, 'col', 0, 0)  16.7 us
    all_to_all x1, starting transfers between devices, on_device(): kv = lax.all_to_all(kv_send, 'row', 0, 0, axis_index_groups=CORE_APART)  11.5 us
    all_to_all x1, starting transfers between devices, on_device(): lax.all_to_all(row_send, 'row', 0, 0, axis_index_groups=CORE_APART)  9.74 us
    all_to_all x1, waiting for transfers between devices, on_device(): lax.all_to_all(row_send, 'row', 0, 0, axis_index_groups=CORE_APART)  6.97 us
    all_to_all x1, waiting for transfers between devices, on_device(): col_recv = lax.all_to_all(col_send, 'col', 0, 0)  6.39 us
    all_to_all x1, starting transfers between devices, on_device(): qo = lax.all_to_all(qo_send, 'col', 0, 0)  5.66 us
    all_to_all x1, starting transfers between devices, on_device(): col_recv = lax.all_to_all(col_send, 'col', 0, 0)  4.87 us
  transfers between devices with their start and end apart: 8, of which 7 were waited for; matrix products, arithmetic and copies ran while one was open for 3% of the time, Pallas kernels for 11%

profile of v8, /device:TPU:1, one launch (start us, length us, event | category | flops | bytes accessed | tf_op | source)
XLA Modules:
  0.0 113.1 jit_solution(14807853399181948135)
XLA Ops:
  0.6 1.6 %shard_map.102 = bf16[8,72,128]{2,1,0:T(8,128)(2,1)} custom-call(bf16[48,96]{1,0:T(8,128)(2,1)} %first_hbm.3, bf16[48,96]{1,0:T(8,128)(2,1)} %second_hbm.3), custom_call_target="tpu_custom_call" | custom-call | flops 10000000 | bytes 400000 | tf_op jit(solution)/shard_map/pallas_call | solution.py:109
  2.2 11.5 %all-to-all-start = ((bf16[8,72,128]{2,1,0:T(8,128)(2,1)}), bf16[8,72,128]{2,1,0:T(8,128)(2,1)S(1)}, u32[]{:S(2)}, u32[]{:S(2)}) async-start(bf16[8,72,128]{2,1,0:T(8,128)(2,1)} %shard_map.102), calls=%async_computation | async-start | bytes 294912 | tf_op jit(solution)/shard_map/all_to_all | solution.py:436
  13.7 0.9 reshape.26
  14.7 1.7 %shard_map.101 = bf16[16,72,128]{2,1,0:T(8,128)(2,1)} custom-call(bf16[48,96]{1,0:T(8,128)(2,1)} %first_hbm.2, bf16[48,96]{1,0:T(8,128)(2,1)} %second_hbm.2), custom_call_target="tpu_custom_call" | custom-call | flops 10000000 | bytes 400000 | tf_op jit(solution)/shard_map/pallas_call | solution.py:109
  16.4 0.0 copy-start.1
  16.4 1.7 %copy-done.1 = bf16[48,48,512]{2,1,0:T(8,128)(2,1)S(1)} copy-done((bf16[48,48,512]{2,1,0:T(8,128)(2,1)S(1)}, bf16[48,48,512]{2,1,0:T(8,128)(2,1)}, u32[]{:S(2)}) %copy-start.1) | copy-done | bytes 2359320
  18.1 2.9 %shard_map.103 = (f32[2304,128]{1,0:T(8,128)S(1)}, bf16[2304,512]{1,0:T(8,128)(2,1)S(1)}) custom-call(bf16[2304,512]{1,0:T(8,128)(2,1)S(1)} %bitcast.9, bf16[128,512]{1,0:T(8,128)(2,1)S(1)} %pad_bitcast_fusion.wide_ref), custom_call_target="tpu_custom_call" | custom-call | flops 301989888 | bytes 5000000 | tf_op jit(solution)/shard_map/pallas_call | solution.py:293
  21.0 0.0 copy-start
  21.0 1.4 %copy-done = bf16[2304,512]{1,0:T(8,128)(2,1)} copy-done((bf16[2304,512]{1,0:T(8,128)(2,1)}, bf16[2304,512]{1,0:T(8,128)(2,1)S(1)}, u32[]{:S(2)}) %copy-start) | copy-done | bytes 2359320
  22.4 0.8 all-to-all-done.kv_ref
  23.3 5.7 %all-to-all-start.1 = ((bf16[16,72,128]{2,1,0:T(8,128)(2,1)}), bf16[16,72,128]{2,1,0:T(8,128)(2,1)S(1)}, u32[]{:S(2)}, u32[]{:S(2)}) async-start(bf16[16,72,128]{2,1,0:T(8,128)(2,1)} %shard_map.101), calls=%async_computation.1 | async-start | bytes 589824 | tf_op jit(solution)/shard_map/all_to_all | solution.py:441
  28.9 3.0 %collective-permute-start = (bf16[8,72,128]{2,1,0:T(8,128)(2,1)S(1)}, bf16[8,72,128]{2,1,0:T(8,128)(2,1)S(1)}, u32[]{:S(2)}, u32[]{:S(2)}) collective-permute-start(bf16[8,72,128]{2,1,0:T(8,128)(2,1)S(1)} %all-to-all-done.kv_ref), channel_id=1, source_target_pairs={{0,16},{16,0},{32,48},{48,32},{64,80},{80,64},{96,112},{112,96},{1... | collective-permute-start | bytes 442376 | tf_op jit(solution)/shard_map/ppermute | solution.py:442
  31.9 1.0 collective-permute-done.partner_ref
  32.9 1.5 %shard_map.104 = (f32[16,48,128]{2,1,0:T(8,128)S(1)}, f32[16,48,128]{2,1,0:T(8,128)S(1)}) custom-call(s32[1]{0:T(128)} %bitcast.3.row_ref.core_ref, bf16[8,72,128]{2,1,0:T(8,128)(2,1)S(1)} %all-to-all-done.kv_ref, bf16[8,72,128]{2,1,0:T(8,128)(2,1)S(1)} %collective-permute-done.partner_ref), custom_call_target="tpu_custom_call" | custom-call | flops 1000000000 | bytes 2000000 | tf_op jit(solution)/shard_map/pallas_call | solution.py:37
  34.4 3.1 %all-to-all-done.1.qo_ref = bf16[16,72,128]{2,1,0:T(8,128)(2,1)S(1)} async-done(((bf16[16,72,128]{2,1,0:T(8,128)(2,1)}), bf16[16,72,128]{2,1,0:T(8,128)(2,1)S(1)}, u32[]{:S(2)}, u32[]{:S(2)}) %all-to-all-start.1) | async-done | bytes 294944 | tf_op jit(solution)/shard_map/all_to_all | solution.py:441
  37.4 4.1 %shard_map.105 = (f32[2304,128]{1,0:T(8,128)S(1)}, f32[2304,128]{1,0:T(8,128)S(1)}, f32[3,48,128]{2,1,0:T(8,128)S(1)}, bf16[16,112,128]{2,1,0:T(8,128)(2,1)S(1)}...) custom-call(bf16[16,72,128]{2,1,0:T(8,128)(2,1)S(1)} %all-to-all-done.1.qo_ref, ...), custom_call_target="tpu_custom_call" | custom-call | tf_op jit(solution)/shard_map/pallas_call | solution.py:37
  41.5 16.7 %all_to_all.30.stat_ref = bf16[16,112,128]{2,1,0:T(8,128)(2,1)S(1)} all-to-all(bf16[16,112,128]{2,1,0:T(8,128)(2,1)S(1)} %get-tuple-element.34), channel_id=1, replica_groups=mesh['row'=16,'col'=16] {'col'}, dimensions={0} | all-to-all | bytes 917504 | tf_op jit(solution)/shard_map/all_to_all | solution.py:462
  58.2 3.4 %shard_map.106 = (bf16[2304,128]{1,0:T(8,128)(2,1)S(1)}, bf16[2304,128]{1,0:T(8,128)(2,1)S(1)}, bf16[16,24,128]{2,1,0:T(8,128)(2,1)}) custom-call(bf16[16,112,128]{2,1,0:T(8,128)(2,1)S(1)} %all_to_all.30.stat_ref, f32[3,48,128]{2,1,0:T(8,128)S(1)} %get-tuple-element.35.own_ref, f32[2304,128]{1,0:T(8,128)S(1)} %get-tuple-element.36.e_ref, ...), custom_call_target="tpu_custom_call" | custom-call | tf_op jit(solution)/shard_map/pallas_call | solution.py:37
  61.6 4.4 %all-to-all-start.3 = ((bf16[16,24,128]{2,1,0:T(8,128)(2,1)}), bf16[16,24,128]{2,1,0:T(8,128)(2,1)S(1)}, u32[]{:S(2)}, u32[]{:S(2)}) async-start(bf16[16,24,128]{2,1,0:T(8,128)(2,1)} %get-tuple-element.40), calls=%async_computation.3 | async-start | bytes 196608 | tf_op jit(solution)/shard_map/all_to_all | solution.py:469
  66.1 3.5 %shard_map.107 = (bf16[8,72,128]{2,1,0:T(8,128)(2,1)S(1)}, bf16[8,72,128]{2,1,0:T(8,128)(2,1)S(1)}) custom-call(s32[1]{0:T(128)} %bitcast.3.row_ref.core_ref, bf16[2304,128]{1,0:T(8,128)(2,1)S(1)} %get-tuple-element.39.score_ref, bf16[2304,128]{1,0:T(8,128)(2,1)S(1)} %get-tuple-element.41.weight_ref, f32[16,48,128]{2,1,0:T(8,128)S(1)} %get-tuple-element.42.q2_ref, ...), custom_call_target="tpu_custom_call" | custom-call | flops 4000000000 | bytes 4000000 | tf_op jit(solution)/shard_map/pallas_call | solution.py:37
  69.6 2.4 %collective-permute-start.2 = (bf16[8,72,128]{2,1,0:T(8,128)(2,1)S(1)}, bf16[8,72,128]{2,1,0:T(8,128)(2,1)S(1)}, u32[]{:S(2)}, u32[]{:S(2)}) collective-permute-start(bf16[8,72,128]{2,1,0:T(8,128)(2,1)S(1)} %get-tuple-element.45), channel_id=1, source_target_pairs={{0,16},{16,0},{32,48},{48,32},{64,80},{80,64},{96,112},{112,96},{1... | collective-permute-start | bytes 442376 | tf_op jit(solution)/shard_map/ppermute | solution.py:481
  72.0 1.2 %all-to-all-done.3.part_ref = bf16[16,24,128]{2,1,0:T(8,128)(2,1)S(1)} async-done(((bf16[16,24,128]{2,1,0:T(8,128)(2,1)}), bf16[16,24,128]{2,1,0:T(8,128)(2,1)S(1)}, u32[]{:S(2)}, u32[]{:S(2)}) %all-to-all-start.3) | async-done | bytes 98336 | tf_op jit(solution)/shard_map/all_to_all | solution.py:469
  73.2 3.4 %collective-permute-start.1 = (bf16[16,24,128]{2,1,0:T(8,128)(2,1)S(1)}, bf16[16,24,128]{2,1,0:T(8,128)(2,1)S(1)}, u32[]{:S(2)}, u32[]{:S(2)}) collective-permute-start(bf16[16,24,128]{2,1,0:T(8,128)(2,1)S(1)} %all-to-all-done.3.part_ref), channel_id=1, source_target_pairs={{0,16},{16,0},{32,48},{48,32},{64,80},{80,64},{96,112},{112,96},{1... | collective-permute-start | bytes 294920 | tf_op jit(solution)/shard_map/ppermute | solution.py:482
  76.6 0.0 collective-permute-done.2.partner_ref
  76.6 0.9 collective-permute-done.1.part_partner_ref
  77.6 0.7 shard_map.108
  78.3 9.7 %all-to-all-start.4 = ((bf16[8,96,128]{2,1,0:T(8,128)(2,1)}), bf16[8,96,128]{2,1,0:T(8,128)(2,1)S(1)}, u32[]{:S(2)}, u32[]{:S(2)}) async-start(bf16[8,96,128]{2,1,0:T(8,128)(2,1)} %shard_map.108), calls=%async_computation.4 | async-start | bytes 393216 | tf_op jit(solution)/shard_map/all_to_all | solution.py:488
  88.0 2.9 %shard_map.109.query_ref = bf16[16,40,128]{2,1,0:T(8,128)(2,1)S(1)} custom-call(bf16[2304,128]{1,0:T(8,128)(2,1)S(1)} %get-tuple-element.39.score_ref, f32[16,48,128]{2,1,0:T(8,128)S(1)} %get-tuple-element.31.k2_ref), custom_call_target="tpu_custom_call" | custom-call | flops 4000000000 | bytes 4000000 | tf_op jit(solution)/shard_map/pallas_call | solution.py:37
  90.9 7.0 %all-to-all-done.4.recv_ref = bf16[8,96,128]{2,1,0:T(8,128)(2,1)S(1)} async-done(((bf16[8,96,128]{2,1,0:T(8,128)(2,1)}), bf16[8,96,128]{2,1,0:T(8,128)(2,1)S(1)}, u32[]{:S(2)}, u32[]{:S(2)}) %all-to-all-start.4) | async-done | bytes 196640 | tf_op jit(solution)/shard_map/all_to_all | solution.py:488
  97.9 0.9 shard_map.110
  98.8 4.9 %all-to-all-start.5 = ((bf16[16,64,128]{2,1,0:T(8,128)(2,1)}), bf16[16,64,128]{2,1,0:T(8,128)(2,1)S(1)}, u32[]{:S(2)}, u32[]{:S(2)}) async-start(bf16[16,64,128]{2,1,0:T(8,128)(2,1)} %get-tuple-element.46), calls=%async_computation.5 | async-start | bytes 524288 | tf_op jit(solution)/shard_map/all_to_all | solution.py:503
  103.7 2.2 %convolution_convert_fusion = bf16[2304,512]{1,0:T(8,128)(2,1)} fusion(bf16[2304,128]{1,0:T(8,128)(2,1)S(1)} %get-tuple-element.39.score_ref, bf16[16,6,512]{2,1,0:T(8,128)(2,1)S(1)} %reshape.26), kind=kOutput, calls=%fused_computation | convolution fusion | flops 303169536 | bytes 3047424 | tf_op jit(solution)/shard_map/dot_general | solution.py:497
  105.8 6.4 %all-to-all-done.5.recv_ref = bf16[16,64,128]{2,1,0:T(8,128)(2,1)S(1)} async-done(((bf16[16,64,128]{2,1,0:T(8,128)(2,1)}), bf16[16,64,128]{2,1,0:T(8,128)(2,1)S(1)}, u32[]{:S(2)}, u32[]{:S(2)}) %all-to-all-start.5) | async-done | bytes 262176 | tf_op jit(solution)/shard_map/all_to_all | solution.py:503
  112.2 0.9 shard_map.111
  (1 shorter events, 0.0 us)
Async XLA Ops:
  2.2 21.0 %all-to-all-start = ((bf16[8,72,128]{2,1,0:T(8,128)(2,1)}), bf16[8,72,128]{2,1,0:T(8,128)(2,1)S(1)}, u32[]{:S(2)}, u32[]{:S(2)}) async-start(bf16[8,72,128]{2,1,0:T(8,128)(2,1)} %shard_map.102), calls=%async_computation | async-start | bytes 294912 | tf_op jit(solution)/shard_map/all_to_all | solution.py:436
  16.4 1.7 %copy-start.1 = (bf16[48,48,512]{2,1,0:T(8,128)(2,1)S(1)}, bf16[48,48,512]{2,1,0:T(8,128)(2,1)}, u32[]{:S(2)}) copy-start(bf16[48,48,512]{2,1,0:T(8,128)(2,1)} %param.6) | copy-start | bytes 7077892
  21.0 1.4 %copy-start = (bf16[2304,512]{1,0:T(8,128)(2,1)}, bf16[2304,512]{1,0:T(8,128)(2,1)S(1)}, u32[]{:S(2)}) copy-start(bf16[2304,512]{1,0:T(8,128)(2,1)S(1)} %get-tuple-element.38.pair_ref) | copy-start | bytes 7077892
  23.3 14.2 %all-to-all-start.1 = ((bf16[16,72,128]{2,1,0:T(8,128)(2,1)}), bf16[16,72,128]{2,1,0:T(8,128)(2,1)S(1)}, u32[]{:S(2)}, u32[]{:S(2)}) async-start(bf16[16,72,128]{2,1,0:T(8,128)(2,1)} %shard_map.101), calls=%async_computation.1 | async-start | bytes 589824 | tf_op jit(solution)/shard_map/all_to_all | solution.py:441
  28.9 4.0 %collective-permute-start = (bf16[8,72,128]{2,1,0:T(8,128)(2,1)S(1)}, bf16[8,72,128]{2,1,0:T(8,128)(2,1)S(1)}, u32[]{:S(2)}, u32[]{:S(2)}) collective-permute-start(bf16[8,72,128]{2,1,0:T(8,128)(2,1)S(1)} %all-to-all-done.kv_ref), channel_id=1, source_target_pairs={{0,16},{16,0},{32,48},{48,32},{64,80},{80,64},{96,112},{112,96},{1... | collective-permute-start | bytes 442376 | tf_op jit(solution)/shard_map/ppermute | solution.py:442
  61.6 11.6 %all-to-all-start.3 = ((bf16[16,24,128]{2,1,0:T(8,128)(2,1)}), bf16[16,24,128]{2,1,0:T(8,128)(2,1)S(1)}, u32[]{:S(2)}, u32[]{:S(2)}) async-start(bf16[16,24,128]{2,1,0:T(8,128)(2,1)} %get-tuple-element.40), calls=%async_computation.3 | async-start | bytes 196608 | tf_op jit(solution)/shard_map/all_to_all | solution.py:469
  69.6 7.0 %collective-permute-start.2 = (bf16[8,72,128]{2,1,0:T(8,128)(2,1)S(1)}, bf16[8,72,128]{2,1,0:T(8,128)(2,1)S(1)}, u32[]{:S(2)}, u32[]{:S(2)}) collective-permute-start(bf16[8,72,128]{2,1,0:T(8,128)(2,1)S(1)} %get-tuple-element.45), channel_id=1, source_target_pairs={{0,16},{16,0},{32,48},{48,32},{64,80},{80,64},{96,112},{112,96},{1... | collective-permute-start | bytes 442376 | tf_op jit(solution)/shard_map/ppermute | solution.py:481
  73.2 4.3 %collective-permute-start.1 = (bf16[16,24,128]{2,1,0:T(8,128)(2,1)S(1)}, bf16[16,24,128]{2,1,0:T(8,128)(2,1)S(1)}, u32[]{:S(2)}, u32[]{:S(2)}) collective-permute-start(bf16[16,24,128]{2,1,0:T(8,128)(2,1)S(1)} %all-to-all-done.3.part_ref), channel_id=1, source_target_pairs={{0,16},{16,0},{32,48},{48,32},{64,80},{80,64},{96,112},{112,96},{1... | collective-permute-start | bytes 294920 | tf_op jit(solution)/shard_map/ppermute | solution.py:482
  78.3 19.6 %all-to-all-start.4 = ((bf16[8,96,128]{2,1,0:T(8,128)(2,1)}), bf16[8,96,128]{2,1,0:T(8,128)(2,1)S(1)}, u32[]{:S(2)}, u32[]{:S(2)}) async-start(bf16[8,96,128]{2,1,0:T(8,128)(2,1)} %shard_map.108), calls=%async_computation.4 | async-start | bytes 393216 | tf_op jit(solution)/shard_map/all_to_all | solution.py:488
  98.8 13.4 %all-to-all-start.5 = ((bf16[16,64,128]{2,1,0:T(8,128)(2,1)}), bf16[16,64,128]{2,1,0:T(8,128)(2,1)S(1)}, u32[]{:S(2)}, u32[]{:S(2)}) async-start(bf16[16,64,128]{2,1,0:T(8,128)(2,1)} %get-tuple-element.46), calls=%async_computation.5 | async-start | bytes 524288 | tf_op jit(solution)/shard_map/all_to_all | solution.py:503

commit v9 on v8

--- a/solution.py
+++ b/solution.py
@@ -272,7 +272,7 @@
 PAIR_CUTS = 8
 
 
-def bias_kernel(pair_hbm, wide_ref, bias_ref, pair_ref, sems):
+def grad_kernel(stat_ref, own_ref, e_ref, gp_ref, pair_hbm, score_ref, weight_ref, part_ref, factor_ref, offset_ref, pair_ref, sems):
     cut = CELLS // PAIR_CUTS
     copies = [
         pltpu.make_async_copy(
@@ -282,28 +282,7 @@
     ]
     for copy in copies:
         copy.start()
-    for n, copy in enumerate(copies):
-        copy.wait()
-        at = slice(n * cut, n * cut + cut)
-        bias_ref[at, :] = contract(pair_ref[at, :], wide_ref[...], 1, 1)
-
-
-def pair_bias(flat_pair, wide):
-    vmem = pl.BlockSpec(memory_space=pltpu.VMEM)
-    return pl.pallas_call(
-        bias_kernel,
-        out_shape=[array((CELLS, LANES), F32), array((CELLS, P_SIZE), LOW)],
-        in_specs=[pl.BlockSpec(memory_space=pl.ANY), vmem],
-        out_specs=[vmem] * 2,
-        scratch_shapes=[pltpu.SemaphoreType.DMA((PAIR_CUTS,))],
-        cost_estimate=pl.CostEstimate(
-            flops=2 * CELLS * P_SIZE * LANES, bytes_accessed=5_000_000, transcendentals=0
-        ),
-        compiler_params=pltpu.CompilerParams(vmem_limit_bytes=VMEM_LIMIT),
-    )(flat_pair, wide)
-
-
-def grad_kernel(stat_ref, own_ref, e_ref, gp_ref, pair_ref, score_ref, weight_ref, part_ref, factor_ref, offset_ref):
+
     def stats_of(c):
         return unpack_stats(
             stat_ref[c, :N_I, :].astype(F32),
@@ -338,6 +317,8 @@
         return carry
 
     lax.fori_loop(0, N_I, row, 0, unroll=2)
+    for copy in copies:
+        copy.wait()
     term = contract(score_ref[...], pair_ref[...], 0, 0)
     for c in range(SIDE):
         part_ref[c] = pack_shard(term[8 * c : 8 * c + 8]).astype(LOW)
@@ -436,7 +417,7 @@
     kv = lax.all_to_all(kv_send, "row", 0, 0, axis_index_groups=CORE_APART)
     wide = jnp.pad(w_bias.T.reshape(SIDE, PLACES, P_SIZE), ((0, 0), (0, 2), (0, 0)))
     wide = wide.reshape(LANES, P_SIZE)
-    bias, held_pair = pair_bias(flat_pair, wide)
+    bias = contract(flat_pair, wide, 1, 1)
     qo_send, kv, bias = lax.optimization_barrier((qo_send, kv, bias))
     qo = lax.all_to_all(qo_send, "col", 0, 0)
     kv_partner = lax.ppermute(kv, "row", CORE_SWAP)
@@ -460,12 +441,16 @@
         scratch=[wide_blocks],
     )
     stats = lax.all_to_all(stats, "col", 0, 0)
-    score, weight, part = call(
+    vmem = pl.BlockSpec(memory_space=pltpu.VMEM)
+    score, weight, part = pl.pallas_call(
         grad_kernel,
-        [array((CELLS, LANES), LOW)] * 2 + [array((SIDE, W_ROWS, LANES), LOW)],
-        stats, own_stats, e, gp, held_pair,
-        scratch=[pltpu.VMEM((N_I, LANES), F32)] * 2,
-    )
+        out_shape=[array((CELLS, LANES), LOW)] * 2 + [array((SIDE, W_ROWS, LANES), LOW)],
+        in_specs=[vmem] * 4 + [pl.BlockSpec(memory_space=pl.ANY)],
+        out_specs=[vmem] * 3,
+        scratch_shapes=[pltpu.VMEM((N_I, LANES), F32)] * 2
+        + [pltpu.VMEM((CELLS, P_SIZE), LOW), pltpu.SemaphoreType.DMA((PAIR_CUTS,))],
+        compiler_params=pltpu.CompilerParams(vmem_limit_bytes=VMEM_LIMIT),
+    )(stats, own_stats, e, gp, flat_pair)
     part = lax.all_to_all(part, "col", 0, 0)
     vpu_cost = pl.CostEstimate(flops=4_000_000_000, bytes_accessed=4_000_000, transcendentals=0)
     blocks = pltpu.VMEM((SIDE, N_J, LANES), F32)

time: 114 us -> 110 us (0.965)
  waiting for transfers between devices: 20.4 us -> 24.1 us
  starting transfers between devices: 45 us -> 41.4 us
  Pallas kernels: 24.1 us -> 20.7 us
  local copies, waits for them, and re-layouts: 4.01 us -> 0.93 us
  matrix products: 2.17 us -> 4.61 us
    all_to_all x1, waiting for transfers between devices: 0.85 us -> 4.47 us  [on_device(): kv = lax.all_to_all(kv_send, 'row', 0, 0, axis_index_groups=CORE_APART)]
    all_to_all x1, starting transfers between devices: 9.74 us -> 6.14 us  [on_device(): lax.all_to_all(row_send, 'row', 0, 0, axis_index_groups=CORE_APART)]
    pallas_call x8 -> x7, Pallas kernels: 17.9 us -> 14.5 us  [call(): pl.pallas_call(kernel, out_shape=out_shape, in_specs=specs, out_specs=out...]
    unnamed x4 -> x0, local copies, waits for them, and re-layouts: 3.06 us -> none
    dot_general x0 -> x1, matrix products: none -> 2.44 us  [contract(): lax.dot_general(a, b, (((a_dim,), (b_dim,)), ((), ())), preferred_element...]
  transfers between devices with their start and end apart: 8 -> 8, of which waited for: 7 -> 7; matrix products, arithmetic and copies ran while one was open for 3% -> 5% of each run, Pallas kernels for 11% -> 9%
where the time goes in v9:
time: 110 us; the launch traced here: 109 us
  starting transfers between devices  41.4 us (38%)
  waiting for transfers between devices  24.1 us (22%)
  Pallas kernels  20.7 us (19%)
  blocking collectives  16.7 us (15%)
  matrix products  4.61 us (4%)
    all_to_all x1, blocking collectives, on_device(): stats = lax.all_to_all(stats, 'col', 0, 0)  16.7 us
    pallas_call x7, Pallas kernels, call(): pl.pallas_call(kernel, out_shape=out_shape, in_specs=specs, out_specs=out...  14.5 us
    all_to_all x1, starting transfers between devices, on_device(): kv = lax.all_to_all(kv_send, 'row', 0, 0, axis_index_groups=CORE_APART)  11.5 us
    all_to_all x1, waiting for transfers between devices, on_device(): lax.all_to_all(row_send, 'row', 0, 0, axis_index_groups=CORE_APART)  6.97 us
    all_to_all x1, waiting for transfers between devices, on_device(): col_recv = lax.all_to_all(col_send, 'col', 0, 0)  6.39 us
    all_to_all x1, starting transfers between devices, on_device(): lax.all_to_all(row_send, 'row', 0, 0, axis_index_groups=CORE_APART)  6.14 us
    all_to_all x1, starting transfers between devices, on_device(): qo = lax.all_to_all(qo_send, 'col', 0, 0)  5.66 us
    all_to_all x1, starting transfers between devices, on_device(): col_recv = lax.all_to_all(col_send, 'col', 0, 0)  4.87 us
  transfers between devices with their start and end apart: 8, of which 7 were waited for; matrix products, arithmetic and copies ran while one was open for 5% of the time, Pallas kernels for 9%

profile of v9, /device:TPU:1, one launch (start us, length us, event | category | flops | bytes accessed | tf_op | source)
XLA Modules:
  0.0 109.1 jit_solution(4890960988842119401)
XLA Ops:
  0.6 1.6 %shard_map.102 = bf16[8,72,128]{2,1,0:T(8,128)(2,1)} custom-call(bf16[48,96]{1,0:T(8,128)(2,1)} %first_hbm.3, bf16[48,96]{1,0:T(8,128)(2,1)} %second_hbm.3), custom_call_target="tpu_custom_call" | custom-call | flops 10000000 | bytes 400000 | tf_op jit(solution)/shard_map/pallas_call | solution.py:109
  2.2 11.5 %all-to-all-start = ((bf16[8,72,128]{2,1,0:T(8,128)(2,1)}), bf16[8,72,128]{2,1,0:T(8,128)(2,1)S(1)}, u32[]{:S(2)}, u32[]{:S(2)}) async-start(bf16[8,72,128]{2,1,0:T(8,128)(2,1)} %shard_map.102), calls=%async_computation | async-start | bytes 294912 | tf_op jit(solution)/shard_map/all_to_all | solution.py:417
  13.7 0.9 reshape.25
  14.7 1.7 %shard_map.101 = bf16[16,72,128]{2,1,0:T(8,128)(2,1)} custom-call(bf16[48,96]{1,0:T(8,128)(2,1)} %first_hbm.2, bf16[48,96]{1,0:T(8,128)(2,1)} %second_hbm.2), custom_call_target="tpu_custom_call" | custom-call | flops 10000000 | bytes 400000 | tf_op jit(solution)/shard_map/pallas_call | solution.py:109
  16.3 2.4 %convolution_bitcast_fusion.bias_ref = f32[2304,128]{1,0:T(8,128)S(1)} fusion(bf16[2304,512]{1,0:T(8,128)(2,1)} %bitcast.14, bf16[16,6,512]{2,1,0:T(8,128)(2,1)S(1)} %reshape.25), kind=kOutput, calls=%fused_computation.1 | convolution fusion | flops 301989888 | bytes 3637248 | tf_op jit(solution)/shard_map/dot_general | solution.py:67
  18.8 4.5 %all-to-all-done.kv_ref = bf16[8,72,128]{2,1,0:T(8,128)(2,1)S(1)} async-done(((bf16[8,72,128]{2,1,0:T(8,128)(2,1)}), bf16[8,72,128]{2,1,0:T(8,128)(2,1)S(1)}, u32[]{:S(2)}, u32[]{:S(2)}) %all-to-all-start) | async-done | bytes 147488 | tf_op jit(solution)/shard_map/all_to_all | solution.py:417
  23.3 5.7 %all-to-all-start.1 = ((bf16[16,72,128]{2,1,0:T(8,128)(2,1)}), bf16[16,72,128]{2,1,0:T(8,128)(2,1)S(1)}, u32[]{:S(2)}, u32[]{:S(2)}) async-start(bf16[16,72,128]{2,1,0:T(8,128)(2,1)} %shard_map.101), calls=%async_computation.1 | async-start | bytes 589824 | tf_op jit(solution)/shard_map/all_to_all | solution.py:422
  28.9 3.0 %collective-permute-start = (bf16[8,72,128]{2,1,0:T(8,128)(2,1)S(1)}, bf16[8,72,128]{2,1,0:T(8,128)(2,1)S(1)}, u32[]{:S(2)}, u32[]{:S(2)}) collective-permute-start(bf16[8,72,128]{2,1,0:T(8,128)(2,1)S(1)} %all-to-all-done.kv_ref), channel_id=1, source_target_pairs={{0,16},{16,0},{32,48},{48,32},{64,80},{80,64},{96,112},{112,96},{1... | collective-permute-start | bytes 442376 | tf_op jit(solution)/shard_map/ppermute | solution.py:423
  31.9 1.0 collective-permute-done.partner_ref
  32.9 1.5 %shard_map.103 = (f32[16,48,128]{2,1,0:T(8,128)S(1)}, f32[16,48,128]{2,1,0:T(8,128)S(1)}) custom-call(s32[1]{0:T(128)} %bitcast.4.row_ref.core_ref, bf16[8,72,128]{2,1,0:T(8,128)(2,1)S(1)} %all-to-all-done.kv_ref, bf16[8,72,128]{2,1,0:T(8,128)(2,1)S(1)} %collective-permute-done.partner_ref), custom_call_target="tpu_custom_call" | custom-call | flops 1000000000 | bytes 2000000 | tf_op jit(solution)/shard_map/pallas_call | solution.py:37
  34.4 3.1 %all-to-all-done.1.qo_ref = bf16[16,72,128]{2,1,0:T(8,128)(2,1)S(1)} async-done(((bf16[16,72,128]{2,1,0:T(8,128)(2,1)}), bf16[16,72,128]{2,1,0:T(8,128)(2,1)S(1)}, u32[]{:S(2)}, u32[]{:S(2)}) %all-to-all-start.1) | async-done | bytes 294944 | tf_op jit(solution)/shard_map/all_to_all | solution.py:422
  37.4 4.1 %shard_map.104 = (f32[2304,128]{1,0:T(8,128)S(1)}, f32[2304,128]{1,0:T(8,128)S(1)}, f32[3,48,128]{2,1,0:T(8,128)S(1)}, bf16[16,112,128]{2,1,0:T(8,128)(2,1)S(1)}...) custom-call(bf16[16,72,128]{2,1,0:T(8,128)(2,1)S(1)} %all-to-all-done.1.qo_ref, ...), custom_call_target="tpu_custom_call" | custom-call | tf_op jit(solution)/shard_map/pallas_call | solution.py:37
  41.5 16.7 %all_to_all.30.stat_ref = bf16[16,112,128]{2,1,0:T(8,128)(2,1)S(1)} all-to-all(bf16[16,112,128]{2,1,0:T(8,128)(2,1)S(1)} %get-tuple-element.31), channel_id=1, replica_groups=mesh['row'=16,'col'=16] {'col'}, dimensions={0} | all-to-all | bytes 917504 | tf_op jit(solution)/shard_map/all_to_all | solution.py:443
  58.2 3.0 %shard_map.105 = (bf16[2304,128]{1,0:T(8,128)(2,1)S(1)}, bf16[2304,128]{1,0:T(8,128)(2,1)S(1)}, bf16[16,24,128]{2,1,0:T(8,128)(2,1)}) custom-call(bf16[16,112,128]{2,1,0:T(8,128)(2,1)S(1)} %all_to_all.30.stat_ref, f32[3,48,128]{2,1,0:T(8,128)S(1)} %get-tuple-element.32.own_ref, f32[2304,128]{1,0:T(8,128)S(1)} %get-tuple-element.33.e_ref, ...), custom_call_target="tpu_custom_call" | custom-call | tf_op jit(solution)/shard_map/pallas_call | solution.py:445
  61.2 4.5 %all-to-all-start.3 = ((bf16[16,24,128]{2,1,0:T(8,128)(2,1)}), bf16[16,24,128]{2,1,0:T(8,128)(2,1)S(1)}, u32[]{:S(2)}, u32[]{:S(2)}) async-start(bf16[16,24,128]{2,1,0:T(8,128)(2,1)} %get-tuple-element.36), calls=%async_computation.3 | async-start | bytes 196608 | tf_op jit(solution)/shard_map/all_to_all | solution.py:454
  65.7 3.5 %shard_map.106 = (bf16[8,72,128]{2,1,0:T(8,128)(2,1)S(1)}, bf16[8,72,128]{2,1,0:T(8,128)(2,1)S(1)}) custom-call(s32[1]{0:T(128)} %bitcast.4.row_ref.core_ref, bf16[2304,128]{1,0:T(8,128)(2,1)S(1)} %get-tuple-element.35.score_ref, bf16[2304,128]{1,0:T(8,128)(2,1)S(1)} %get-tuple-element.37.weight_ref, f32[16,48,128]{2,1,0:T(8,128)S(1)} %get-tuple-element.38.q2_ref, ...), custom_call_target="tpu_custom_call" | custom-call | flops 4000000000 | bytes 4000000 | tf_op jit(solution)/shard_map/pallas_call | solution.py:37
  69.2 2.4 %collective-permute-start.2 = (bf16[8,72,128]{2,1,0:T(8,128)(2,1)S(1)}, bf16[8,72,128]{2,1,0:T(8,128)(2,1)S(1)}, u32[]{:S(2)}, u32[]{:S(2)}) collective-permute-start(bf16[8,72,128]{2,1,0:T(8,128)(2,1)S(1)} %get-tuple-element.41), channel_id=1, source_target_pairs={{0,16},{16,0},{32,48},{48,32},{64,80},{80,64},{96,112},{112,96},{1... | collective-permute-start | bytes 442376 | tf_op jit(solution)/shard_map/ppermute | solution.py:466
  71.6 1.2 %all-to-all-done.3.part_ref = bf16[16,24,128]{2,1,0:T(8,128)(2,1)S(1)} async-done(((bf16[16,24,128]{2,1,0:T(8,128)(2,1)}), bf16[16,24,128]{2,1,0:T(8,128)(2,1)S(1)}, u32[]{:S(2)}, u32[]{:S(2)}) %all-to-all-start.3) | async-done | bytes 98336 | tf_op jit(solution)/shard_map/all_to_all | solution.py:454
  72.8 3.4 %collective-permute-start.1 = (bf16[16,24,128]{2,1,0:T(8,128)(2,1)S(1)}, bf16[16,24,128]{2,1,0:T(8,128)(2,1)S(1)}, u32[]{:S(2)}, u32[]{:S(2)}) collective-permute-start(bf16[16,24,128]{2,1,0:T(8,128)(2,1)S(1)} %all-to-all-done.3.part_ref), channel_id=1, source_target_pairs={{0,16},{16,0},{32,48},{48,32},{64,80},{80,64},{96,112},{112,96},{1... | collective-permute-start | bytes 294920 | tf_op jit(solution)/shard_map/ppermute | solution.py:467
  76.2 0.0 collective-permute-done.2.partner_ref
  76.2 0.9 collective-permute-done.1.part_partner_ref
  77.1 0.7 shard_map.107
  77.9 6.1 %all-to-all-start.4 = ((bf16[8,96,128]{2,1,0:T(8,128)(2,1)}), bf16[8,96,128]{2,1,0:T(8,128)(2,1)S(1)}, u32[]{:S(2)}, u32[]{:S(2)}) async-start(bf16[8,96,128]{2,1,0:T(8,128)(2,1)} %shard_map.107), calls=%async_computation.4 | async-start | bytes 393216 | tf_op jit(solution)/shard_map/all_to_all | solution.py:473
  84.0 2.9 %shard_map.108.query_ref = bf16[16,40,128]{2,1,0:T(8,128)(2,1)S(1)} custom-call(bf16[2304,128]{1,0:T(8,128)(2,1)S(1)} %get-tuple-element.35.score_ref, f32[16,48,128]{2,1,0:T(8,128)S(1)} %get-tuple-element.28.k2_ref), custom_call_target="tpu_custom_call" | custom-call | flops 4000000000 | bytes 4000000 | tf_op jit(solution)/shard_map/pallas_call | solution.py:37
  86.9 7.0 %all-to-all-done.4.recv_ref = bf16[8,96,128]{2,1,0:T(8,128)(2,1)S(1)} async-done(((bf16[8,96,128]{2,1,0:T(8,128)(2,1)}), bf16[8,96,128]{2,1,0:T(8,128)(2,1)S(1)}, u32[]{:S(2)}, u32[]{:S(2)}) %all-to-all-start.4) | async-done | bytes 196640 | tf_op jit(solution)/shard_map/all_to_all | solution.py:473
  93.9 0.9 shard_map.109
  94.8 4.9 %all-to-all-start.5 = ((bf16[16,64,128]{2,1,0:T(8,128)(2,1)}), bf16[16,64,128]{2,1,0:T(8,128)(2,1)S(1)}, u32[]{:S(2)}, u32[]{:S(2)}) async-start(bf16[16,64,128]{2,1,0:T(8,128)(2,1)} %get-tuple-element.42), calls=%async_computation.5 | async-start | bytes 524288 | tf_op jit(solution)/shard_map/all_to_all | solution.py:488
  99.7 2.2 %convolution_convert_fusion = bf16[2304,512]{1,0:T(8,128)(2,1)} fusion(bf16[2304,128]{1,0:T(8,128)(2,1)S(1)} %get-tuple-element.35.score_ref, bf16[16,6,512]{2,1,0:T(8,128)(2,1)S(1)} %reshape.25), kind=kOutput, calls=%fused_computation | convolution fusion | flops 303169536 | bytes 3047424 | tf_op jit(solution)/shard_map/dot_general | solution.py:482
  101.8 6.4 %all-to-all-done.5.recv_ref = bf16[16,64,128]{2,1,0:T(8,128)(2,1)S(1)} async-done(((bf16[16,64,128]{2,1,0:T(8,128)(2,1)}), bf16[16,64,128]{2,1,0:T(8,128)(2,1)S(1)}, u32[]{:S(2)}, u32[]{:S(2)}) %all-to-all-start.5) | async-done | bytes 262176 | tf_op jit(solution)/shard_map/all_to_all | solution.py:488
  108.2 0.9 shard_map.110
Async XLA Ops:
  2.2 21.0 %all-to-all-start = ((bf16[8,72,128]{2,1,0:T(8,128)(2,1)}), bf16[8,72,128]{2,1,0:T(8,128)(2,1)S(1)}, u32[]{:S(2)}, u32[]{:S(2)}) async-start(bf16[8,72,128]{2,1,0:T(8,128)(2,1)} %shard_map.102), calls=%async_computation | async-start | bytes 294912 | tf_op jit(solution)/shard_map/all_to_all | solution.py:417
  23.3 14.2 %all-to-all-start.1 = ((bf16[16,72,128]{2,1,0:T(8,128)(2,1)}), bf16[16,72,128]{2,1,0:T(8,128)(2,1)S(1)}, u32[]{:S(2)}, u32[]{:S(2)}) async-start(bf16[16,72,128]{2,1,0:T(8,128)(2,1)} %shard_map.101), calls=%async_computation.1 | async-start | bytes 589824 | tf_op jit(solution)/shard_map/all_to_all | solution.py:422
  28.9 4.0 %collective-permute-start = (bf16[8,72,128]{2,1,0:T(8,128)(2,1)S(1)}, bf16[8,72,128]{2,1,0:T(8,128)(2,1)S(1)}, u32[]{:S(2)}, u32[]{:S(2)}) collective-permute-start(bf16[8,72,128]{2,1,0:T(8,128)(2,1)S(1)} %all-to-all-done.kv_ref), channel_id=1, source_target_pairs={{0,16},{16,0},{32,48},{48,32},{64,80},{80,64},{96,112},{112,96},{1... | collective-permute-start | bytes 442376 | tf_op jit(solution)/shard_map/ppermute | solution.py:423
  61.2 11.6 %all-to-all-start.3 = ((bf16[16,24,128]{2,1,0:T(8,128)(2,1)}), bf16[16,24,128]{2,1,0:T(8,128)(2,1)S(1)}, u32[]{:S(2)}, u32[]{:S(2)}) async-start(bf16[16,24,128]{2,1,0:T(8,128)(2,1)} %get-tuple-element.36), calls=%async_computation.3 | async-start | bytes 196608 | tf_op jit(solution)/shard_map/all_to_all | solution.py:454
  69.2 7.0 %collective-permute-start.2 = (bf16[8,72,128]{2,1,0:T(8,128)(2,1)S(1)}, bf16[8,72,128]{2,1,0:T(8,128)(2,1)S(1)}, u32[]{:S(2)}, u32[]{:S(2)}) collective-permute-start(bf16[8,72,128]{2,1,0:T(8,128)(2,1)S(1)} %get-tuple-element.41), channel_id=1, source_target_pairs={{0,16},{16,0},{32,48},{48,32},{64,80},{80,64},{96,112},{112,96},{1... | collective-permute-start | bytes 442376 | tf_op jit(solution)/shard_map/ppermute | solution.py:466
  72.8 4.3 %collective-permute-start.1 = (bf16[16,24,128]{2,1,0:T(8,128)(2,1)S(1)}, bf16[16,24,128]{2,1,0:T(8,128)(2,1)S(1)}, u32[]{:S(2)}, u32[]{:S(2)}) collective-permute-start(bf16[16,24,128]{2,1,0:T(8,128)(2,1)S(1)} %all-to-all-done.3.part_ref), channel_id=1, source_target_pairs={{0,16},{16,0},{32,48},{48,32},{64,80},{80,64},{96,112},{112,96},{1... | collective-permute-start | bytes 294920 | tf_op jit(solution)/shard_map/ppermute | solution.py:467
  77.9 16.0 %all-to-all-start.4 = ((bf16[8,96,128]{2,1,0:T(8,128)(2,1)}), bf16[8,96,128]{2,1,0:T(8,128)(2,1)S(1)}, u32[]{:S(2)}, u32[]{:S(2)}) async-start(bf16[8,96,128]{2,1,0:T(8,128)(2,1)} %shard_map.107), calls=%async_computation.4 | async-start | bytes 393216 | tf_op jit(solution)/shard_map/all_to_all | solution.py:473
  94.8 13.4 %all-to-all-start.5 = ((bf16[16,64,128]{2,1,0:T(8,128)(2,1)}), bf16[16,64,128]{2,1,0:T(8,128)(2,1)S(1)}, u32[]{:S(2)}, u32[]{:S(2)}) async-start(bf16[16,64,128]{2,1,0:T(8,128)(2,1)} %get-tuple-element.42), calls=%async_computation.5 | async-start | bytes 524288 | tf_op jit(solution)/shard_map/all_to_all | solution.py:488

commit v10 on v8

--- a/solution.py
+++ b/solution.py
@@ -19,8 +19,8 @@
 CELLS = N_I * N_J
 LOW = jnp.bfloat16
 F32 = jnp.float32
-VMEM_LIMIT = 48 * 1024 * 1024
-VMEM_SMALL = 48 * 1024 * 1024
+VMEM_LIMIT = 46 * 1024 * 1024
+VMEM_SMALL = 46 * 1024 * 1024
 
 CORE_APART = [[2 * k + c for k in range(8)] for c in range(2)]
 CORE_SWAP = [(r, r ^ 1) for r in range(SIDE)]
@@ -234,7 +234,19 @@
     unpack_features(wide_ref, k2_ref, v2_ref)
 
 
-def scores_kernel(qo_ref, k2_ref, v2_ref, bias_ref, e_ref, gp_ref, own_ref, stat_ref, q2_ref, o2_ref, wide_ref):
+PAIR_CUTS = 8
+
+
+def scores_kernel(qo_ref, k2_ref, v2_ref, bias_ref, pair_hbm, e_ref, gp_ref, own_ref, stat_ref, q2_ref, o2_ref, pair_ref, wide_ref, sems):
+    cut = CELLS // PAIR_CUTS
+    copies = [
+        pltpu.make_async_copy(
+            pair_hbm.at[pl.ds(n * cut, cut)], pair_ref.at[pl.ds(n * cut, cut)], sems.at[n]
+        )
+        for n in range(PAIR_CUTS)
+    ]
+    for copy in copies:
+        copy.start()
     for c in range(SIDE):
         wide_ref[c] = qo_ref[c].astype(F32)
     unpack_features(wide_ref, q2_ref, o2_ref)
@@ -261,46 +273,14 @@
             own_ref[2, pl.ds(i, 1), :] = upper / total
         return carry
 
-    lax.fori_loop(0, N_I // 2, rows, 0, unroll=8)
+    lax.fori_loop(0, N_I // 2, rows, 0, unroll=2)
     packed = [x.astype(LOW) for x in pack_stats(own_ref[0], own_ref[1], own_ref[2])]
     for c in range(SIDE):
         stat_ref[c, :N_I, :] = packed[0]
         stat_ref[c, N_I : 2 * N_I, :] = packed[1]
         stat_ref[c, 2 * N_I :, :] = packed[2]
-
-
-PAIR_CUTS = 8
-
-
-def bias_kernel(pair_hbm, wide_ref, bias_ref, pair_ref, sems):
-    cut = CELLS // PAIR_CUTS
-    copies = [
-        pltpu.make_async_copy(
-            pair_hbm.at[pl.ds(n * cut, cut)], pair_ref.at[pl.ds(n * cut, cut)], sems.at[n]
-        )
-        for n in range(PAIR_CUTS)
-    ]
     for copy in copies:
-        copy.start()
-    for n, copy in enumerate(copies):
         copy.wait()
-        at = slice(n * cut, n * cut + cut)
-        bias_ref[at, :] = contract(pair_ref[at, :], wide_ref[...], 1, 1)
-
-
-def pair_bias(flat_pair, wide):
-    vmem = pl.BlockSpec(memory_space=pltpu.VMEM)
-    return pl.pallas_call(
-        bias_kernel,
-        out_shape=[array((CELLS, LANES), F32), array((CELLS, P_SIZE), LOW)],
-        in_specs=[pl.BlockSpec(memory_space=pl.ANY), vmem],
-        out_specs=[vmem] * 2,
-        scratch_shapes=[pltpu.SemaphoreType.DMA((PAIR_CUTS,))],
-        cost_estimate=pl.CostEstimate(
-            flops=2 * CELLS * P_SIZE * LANES, bytes_accessed=5_000_000, transcendentals=0
-        ),
-        compiler_params=pltpu.CompilerParams(vmem_limit_bytes=VMEM_LIMIT),
-    )(flat_pair, wide)
 
 
 def grad_kernel(stat_ref, own_ref, e_ref, gp_ref, pair_ref, score_ref, weight_ref, part_ref, factor_ref, offset_ref):
@@ -372,9 +352,9 @@
     def tile_of(ref):
         return lambda i: ref[pl.ds(pl.multiple_of(i * N_J, N_J), N_J), :].astype(F32)
 
-    weighted_sums(tile_of(score_ref), q2_ref, sum_ref, N_I)
+    weighted_sums(tile_of(score_ref), q2_ref, sum_ref, 8)
     blocks_of(sum_ref, key_ref, N_J)
-    weighted_sums(tile_of(weight_ref), o2_ref, sum_ref, N_I)
+    weighted_sums(tile_of(weight_ref), o2_ref, sum_ref, 8)
     blocks_of(sum_ref, value_ref, N_J)
     first_core = (core_ref[0] & 1) == 0
     for k in range(8):
@@ -386,7 +366,7 @@
 
 def query_kernel(score_ref, k2_ref, out_ref, wide_ref, sum_ref, block_ref):
     wide_ref[...] = score_ref[...].astype(F32)
-    weighted_sums(lambda j: wide_ref[pl.ds(j, N_I, stride=N_J), :], k2_ref, sum_ref, 8)
+    weighted_sums(lambda j: wide_ref[pl.ds(j, N_I, stride=N_J), :], k2_ref, sum_ref, 4)
     blocks_of(sum_ref, block_ref, N_I // 2)
     for c in range(SIDE):
         out_ref[c] = fold(block_ref[c]).astype(LOW)
@@ -436,7 +416,7 @@
     kv = lax.all_to_all(kv_send, "row", 0, 0, axis_index_groups=CORE_APART)
     wide = jnp.pad(w_bias.T.reshape(SIDE, PLACES, P_SIZE), ((0, 0), (0, 2), (0, 0)))
     wide = wide.reshape(LANES, P_SIZE)
-    bias, held_pair = pair_bias(flat_pair, wide)
+    bias = contract(flat_pair, wide, 1, 1)
     qo_send, kv, bias = lax.optimization_barrier((qo_send, kv, bias))
     qo = lax.all_to_all(qo_send, "col", 0, 0)
     kv_partner = lax.ppermute(kv, "row", CORE_SWAP)
@@ -451,14 +431,18 @@
         scratch=[wide_blocks],
         cost=pl.CostEstimate(flops=1_000_000_000, bytes_accessed=2_000_000, transcendentals=0),
     )
-    e, gp, own_stats, stats, q2, o2 = call(
+    vmem = pl.BlockSpec(memory_space=pltpu.VMEM)
+    e, gp, own_stats, stats, q2, o2, held_pair = pl.pallas_call(
         scores_kernel,
-        [array((CELLS, LANES), F32)] * 2
+        out_shape=[array((CELLS, LANES), F32)] * 2
         + [array((3, N_I, LANES), F32), array((SIDE, STAT_ROWS, LANES), LOW)]
-        + [feature] * 2,
-        qo, k2, v2, bias,
-        scratch=[wide_blocks],
-    )
+        + [feature] * 2
+        + [array((CELLS, P_SIZE), LOW)],
+        in_specs=[vmem] * 4 + [pl.BlockSpec(memory_space=pl.ANY)],
+        out_specs=[vmem] * 7,
+        scratch_shapes=[wide_blocks, pltpu.SemaphoreType.DMA((PAIR_CUTS,))],
+        compiler_params=pltpu.CompilerParams(vmem_limit_bytes=VMEM_LIMIT),
+    )(qo, k2, v2, bias, flat_pair)
     stats = lax.all_to_all(stats, "col", 0, 0)
     score, weight, part = call(
         grad_kernel,

time: 114 us -> 109 us (0.956)
  starting transfers between devices: 45 us -> 41.4 us
  Pallas kernels: 24.1 us -> 20.9 us
  local copies, waits for them, and re-layouts: 4.01 us -> 0.93 us
  waiting for transfers between devices: 20.4 us -> 23 us
  matrix products: 2.17 us -> 4.6 us
    pallas_call x8 -> x7, Pallas kernels: 17.9 us -> 13.2 us  [call(): pl.pallas_call(kernel, out_shape=out_shape, in_specs=specs, out_specs=out...]
    all_to_all x1, waiting for transfers between devices: 0.85 us -> 4.47 us  [on_device(): kv = lax.all_to_all(kv_send, 'row', 0, 0, axis_index_groups=CORE_APART)]
    all_to_all x1, starting transfers between devices: 9.74 us -> 6.14 us  [on_device(): lax.all_to_all(row_send, 'row', 0, 0, axis_index_groups=CORE_APART)]
    unnamed x4 -> x0, local copies, waits for them, and re-layouts: 3.06 us -> none
    dot_general x0 -> x1, matrix products: none -> 2.44 us  [contract(): lax.dot_general(a, b, (((a_dim,), (b_dim,)), ((), ())), preferred_element...]
    pallas_call x1, Pallas kernels: 2.94 us -> 4.42 us  [on_device(): pl.pallas_call(scores_kernel, out_shape=[array((CELLS, LANES), F32)] * 2...]
  transfers between devices with their start and end apart: 8 -> 8, of which waited for: 7 -> 7; matrix products, arithmetic and copies ran while one was open for 3% -> 5% of each run, Pallas kernels for 11% -> 10%
where the time goes in v10:
time: 109 us; the launch traced here: 108 us
  starting transfers between devices  41.4 us (38%)
  waiting for transfers between devices  23 us (21%)
  Pallas kernels  20.9 us (19%)
  blocking collectives  16.7 us (15%)
  matrix products  4.6 us (4%)
    all_to_all x1, blocking collectives, on_device(): stats = lax.all_to_all(stats, 'col', 0, 0)  16.7 us
    pallas_call x7, Pallas kernels, call(): pl.pallas_call(kernel, out_shape=out_shape, in_specs=specs, out_specs=out...  13.2 us
    all_to_all x1, starting transfers between devices, on_device(): kv = lax.all_to_all(kv_send, 'row', 0, 0, axis_index_groups=CORE_APART)  11.5 us
    all_to_all x1, waiting for transfers between devices, on_device(): lax.all_to_all(row_send, 'row', 0, 0, axis_index_groups=CORE_APART)  6.54 us
    all_to_all x1, waiting for transfers between devices, on_device(): col_recv = lax.all_to_all(col_send, 'col', 0, 0)  6.38 us
    all_to_all x1, starting transfers between devices, on_device(): lax.all_to_all(row_send, 'row', 0, 0, axis_index_groups=CORE_APART)  6.14 us
    all_to_all x1, starting transfers between devices, on_device(): qo = lax.all_to_all(qo_send, 'col', 0, 0)  5.66 us
    all_to_all x1, starting transfers between devices, on_device(): col_recv = lax.all_to_all(col_send, 'col', 0, 0)  4.87 us
  transfers between devices with their start and end apart: 8, of which 7 were waited for; matrix products, arithmetic and copies ran while one was open for 5% of the time, Pallas kernels for 10%

profile of v10, /device:TPU:1, one launch (start us, length us, event | category | flops | bytes accessed | tf_op | source)
XLA Modules:
  0.0 108.3 jit_solution(1606064989717580997)
XLA Ops:
  0.6 1.6 %shard_map.102 = bf16[8,72,128]{2,1,0:T(8,128)(2,1)} custom-call(bf16[48,96]{1,0:T(8,128)(2,1)} %first_hbm.3, bf16[48,96]{1,0:T(8,128)(2,1)} %second_hbm.3), custom_call_target="tpu_custom_call" | custom-call | flops 10000000 | bytes 400000 | tf_op jit(solution)/shard_map/pallas_call | solution.py:109
  2.2 11.5 %all-to-all-start = ((bf16[8,72,128]{2,1,0:T(8,128)(2,1)}), bf16[8,72,128]{2,1,0:T(8,128)(2,1)S(1)}, u32[]{:S(2)}, u32[]{:S(2)}) async-start(bf16[8,72,128]{2,1,0:T(8,128)(2,1)} %shard_map.102), calls=%async_computation | async-start | bytes 294912 | tf_op jit(solution)/shard_map/all_to_all | solution.py:416
  13.7 0.9 reshape.25
  14.7 1.7 %shard_map.101 = bf16[16,72,128]{2,1,0:T(8,128)(2,1)} custom-call(bf16[48,96]{1,0:T(8,128)(2,1)} %first_hbm.2, bf16[48,96]{1,0:T(8,128)(2,1)} %second_hbm.2), custom_call_target="tpu_custom_call" | custom-call | flops 10000000 | bytes 400000 | tf_op jit(solution)/shard_map/pallas_call | solution.py:109
  16.3 2.4 %convolution_bitcast_fusion.bias_ref = f32[2304,128]{1,0:T(8,128)S(1)} fusion(bf16[2304,512]{1,0:T(8,128)(2,1)} %bitcast.14, bf16[16,6,512]{2,1,0:T(8,128)(2,1)S(1)} %reshape.25), kind=kOutput, calls=%fused_computation.1 | convolution fusion | flops 301989888 | bytes 3637248 | tf_op jit(solution)/shard_map/dot_general | solution.py:67
  18.8 4.5 %all-to-all-done.kv_ref = bf16[8,72,128]{2,1,0:T(8,128)(2,1)S(1)} async-done(((bf16[8,72,128]{2,1,0:T(8,128)(2,1)}), bf16[8,72,128]{2,1,0:T(8,128)(2,1)S(1)}, u32[]{:S(2)}, u32[]{:S(2)}) %all-to-all-start) | async-done | bytes 147488 | tf_op jit(solution)/shard_map/all_to_all | solution.py:416
  23.3 5.7 %all-to-all-start.1 = ((bf16[16,72,128]{2,1,0:T(8,128)(2,1)}), bf16[16,72,128]{2,1,0:T(8,128)(2,1)S(1)}, u32[]{:S(2)}, u32[]{:S(2)}) async-start(bf16[16,72,128]{2,1,0:T(8,128)(2,1)} %shard_map.101), calls=%async_computation.1 | async-start | bytes 589824 | tf_op jit(solution)/shard_map/all_to_all | solution.py:421
  28.9 3.0 %collective-permute-start = (bf16[8,72,128]{2,1,0:T(8,128)(2,1)S(1)}, bf16[8,72,128]{2,1,0:T(8,128)(2,1)S(1)}, u32[]{:S(2)}, u32[]{:S(2)}) collective-permute-start(bf16[8,72,128]{2,1,0:T(8,128)(2,1)S(1)} %all-to-all-done.kv_ref), channel_id=1, source_target_pairs={{0,16},{16,0},{32,48},{48,32},{64,80},{80,64},{96,112},{112,96},{1... | collective-permute-start | bytes 442376 | tf_op jit(solution)/shard_map/ppermute | solution.py:422
  31.9 1.0 collective-permute-done.partner_ref
  32.9 1.5 %shard_map.103 = (f32[16,48,128]{2,1,0:T(8,128)S(1)}, f32[16,48,128]{2,1,0:T(8,128)S(1)}) custom-call(s32[1]{0:T(128)} %bitcast.4.row_ref.core_ref, bf16[8,72,128]{2,1,0:T(8,128)(2,1)S(1)} %all-to-all-done.kv_ref, bf16[8,72,128]{2,1,0:T(8,128)(2,1)S(1)} %collective-permute-done.partner_ref), custom_call_target="tpu_custom_call" | custom-call | flops 1000000000 | bytes 2000000 | tf_op jit(solution)/shard_map/pallas_call | solution.py:37
  34.4 3.1 %all-to-all-done.1.qo_ref = bf16[16,72,128]{2,1,0:T(8,128)(2,1)S(1)} async-done(((bf16[16,72,128]{2,1,0:T(8,128)(2,1)}), bf16[16,72,128]{2,1,0:T(8,128)(2,1)S(1)}, u32[]{:S(2)}, u32[]{:S(2)}) %all-to-all-start.1) | async-done | bytes 294944 | tf_op jit(solution)/shard_map/all_to_all | solution.py:421
  37.4 4.4 %shard_map.104 = (f32[2304,128]{1,0:T(8,128)S(1)}, f32[2304,128]{1,0:T(8,128)S(1)}, f32[3,48,128]{2,1,0:T(8,128)S(1)}, bf16[16,112,128]{2,1,0:T(8,128)(2,1)S(1)}...) custom-call(bf16[16,72,128]{2,1,0:T(8,128)(2,1)S(1)} %all-to-all-done.1.qo_ref, ...), custom_call_target="tpu_custom_call" | custom-call | tf_op jit(solution)/shard_map/pallas_call | solution.py:435
  41.9 16.7 %all_to_all.30.stat_ref = bf16[16,112,128]{2,1,0:T(8,128)(2,1)S(1)} all-to-all(bf16[16,112,128]{2,1,0:T(8,128)(2,1)S(1)} %get-tuple-element.32), channel_id=1, replica_groups=mesh['row'=16,'col'=16] {'col'}, dimensions={0} | all-to-all | bytes 917504 | tf_op jit(solution)/shard_map/all_to_all | solution.py:446
  58.6 1.8 %shard_map.105 = (bf16[2304,128]{1,0:T(8,128)(2,1)S(1)}, bf16[2304,128]{1,0:T(8,128)(2,1)S(1)}, bf16[16,24,128]{2,1,0:T(8,128)(2,1)}) custom-call(bf16[16,112,128]{2,1,0:T(8,128)(2,1)S(1)} %all_to_all.30.stat_ref, f32[3,48,128]{2,1,0:T(8,128)S(1)} %get-tuple-element.33.own_ref, f32[2304,128]{1,0:T(8,128)S(1)} %get-tuple-element.34.e_ref, ...), custom_call_target="tpu_custom_call" | custom-call | tf_op jit(solution)/shard_map/pallas_call | solution.py:37
  60.4 4.4 %all-to-all-start.3 = ((bf16[16,24,128]{2,1,0:T(8,128)(2,1)}), bf16[16,24,128]{2,1,0:T(8,128)(2,1)S(1)}, u32[]{:S(2)}, u32[]{:S(2)}) async-start(bf16[16,24,128]{2,1,0:T(8,128)(2,1)} %get-tuple-element.38), calls=%async_computation.3 | async-start | bytes 196608 | tf_op jit(solution)/shard_map/all_to_all | solution.py:453
  64.8 4.1 %shard_map.106 = (bf16[8,72,128]{2,1,0:T(8,128)(2,1)S(1)}, bf16[8,72,128]{2,1,0:T(8,128)(2,1)S(1)}) custom-call(s32[1]{0:T(128)} %bitcast.4.row_ref.core_ref, bf16[2304,128]{1,0:T(8,128)(2,1)S(1)} %get-tuple-element.37.score_ref, bf16[2304,128]{1,0:T(8,128)(2,1)S(1)} %get-tuple-element.39.weight_ref, f32[16,48,128]{2,1,0:T(8,128)S(1)} %get-tuple-element.40.q2_ref, ...), custom_call_target="tpu_custom_call" | custom-call | flops 4000000000 | bytes 4000000 | tf_op jit(solution)/shard_map/pallas_call | solution.py:37
  69.0 2.4 %collective-permute-start.2 = (bf16[8,72,128]{2,1,0:T(8,128)(2,1)S(1)}, bf16[8,72,128]{2,1,0:T(8,128)(2,1)S(1)}, u32[]{:S(2)}, u32[]{:S(2)}) collective-permute-start(bf16[8,72,128]{2,1,0:T(8,128)(2,1)S(1)} %get-tuple-element.43), channel_id=1, source_target_pairs={{0,16},{16,0},{32,48},{48,32},{64,80},{80,64},{96,112},{112,96},{1... | collective-permute-start | bytes 442376 | tf_op jit(solution)/shard_map/ppermute | solution.py:465
  71.3 0.6 all-to-all-done.3.part_ref
  71.9 3.4 %collective-permute-start.1 = (bf16[16,24,128]{2,1,0:T(8,128)(2,1)S(1)}, bf16[16,24,128]{2,1,0:T(8,128)(2,1)S(1)}, u32[]{:S(2)}, u32[]{:S(2)}) collective-permute-start(bf16[16,24,128]{2,1,0:T(8,128)(2,1)S(1)} %all-to-all-done.3.part_ref), channel_id=1, source_target_pairs={{0,16},{16,0},{32,48},{48,32},{64,80},{80,64},{96,112},{112,96},{1... | collective-permute-start | bytes 294920 | tf_op jit(solution)/shard_map/ppermute | solution.py:466
  75.3 0.0 collective-permute-done.2.partner_ref
  75.3 0.9 collective-permute-done.1.part_partner_ref
  76.3 0.7 shard_map.107
  77.0 6.1 %all-to-all-start.4 = ((bf16[8,96,128]{2,1,0:T(8,128)(2,1)}), bf16[8,96,128]{2,1,0:T(8,128)(2,1)S(1)}, u32[]{:S(2)}, u32[]{:S(2)}) async-start(bf16[8,96,128]{2,1,0:T(8,128)(2,1)} %shard_map.107), calls=%async_computation.4 | async-start | bytes 393216 | tf_op jit(solution)/shard_map/all_to_all | solution.py:472
  83.2 3.3 %shard_map.108.query_ref = bf16[16,40,128]{2,1,0:T(8,128)(2,1)S(1)} custom-call(bf16[2304,128]{1,0:T(8,128)(2,1)S(1)} %get-tuple-element.37.score_ref, f32[16,48,128]{2,1,0:T(8,128)S(1)} %get-tuple-element.29.k2_ref), custom_call_target="tpu_custom_call" | custom-call | flops 4000000000 | bytes 4000000 | tf_op jit(solution)/shard_map/pallas_call | solution.py:37
  86.4 6.5 %all-to-all-done.4.recv_ref = bf16[8,96,128]{2,1,0:T(8,128)(2,1)S(1)} async-done(((bf16[8,96,128]{2,1,0:T(8,128)(2,1)}), bf16[8,96,128]{2,1,0:T(8,128)(2,1)S(1)}, u32[]{:S(2)}, u32[]{:S(2)}) %all-to-all-start.4) | async-done | bytes 196640 | tf_op jit(solution)/shard_map/all_to_all | solution.py:472
  93.0 0.9 shard_map.109
  93.9 4.9 %all-to-all-start.5 = ((bf16[16,64,128]{2,1,0:T(8,128)(2,1)}), bf16[16,64,128]{2,1,0:T(8,128)(2,1)S(1)}, u32[]{:S(2)}, u32[]{:S(2)}) async-start(bf16[16,64,128]{2,1,0:T(8,128)(2,1)} %get-tuple-element.44), calls=%async_computation.5 | async-start | bytes 524288 | tf_op jit(solution)/shard_map/all_to_all | solution.py:487
  98.8 2.2 %convolution_convert_fusion = bf16[2304,512]{1,0:T(8,128)(2,1)} fusion(bf16[2304,128]{1,0:T(8,128)(2,1)S(1)} %get-tuple-element.37.score_ref, bf16[16,6,512]{2,1,0:T(8,128)(2,1)S(1)} %reshape.25), kind=kOutput, calls=%fused_computation | convolution fusion | flops 303169536 | bytes 3047424 | tf_op jit(solution)/shard_map/dot_general | solution.py:481
  101.0 6.4 %all-to-all-done.5.recv_ref = bf16[16,64,128]{2,1,0:T(8,128)(2,1)S(1)} async-done(((bf16[16,64,128]{2,1,0:T(8,128)(2,1)}), bf16[16,64,128]{2,1,0:T(8,128)(2,1)S(1)}, u32[]{:S(2)}, u32[]{:S(2)}) %all-to-all-start.5) | async-done | bytes 262176 | tf_op jit(solution)/shard_map/all_to_all | solution.py:487
  107.4 0.9 shard_map.110
Async XLA Ops:
  2.2 21.0 %all-to-all-start = ((bf16[8,72,128]{2,1,0:T(8,128)(2,1)}), bf16[8,72,128]{2,1,0:T(8,128)(2,1)S(1)}, u32[]{:S(2)}, u32[]{:S(2)}) async-start(bf16[8,72,128]{2,1,0:T(8,128)(2,1)} %shard_map.102), calls=%async_computation | async-start | bytes 294912 | tf_op jit(solution)/shard_map/all_to_all | solution.py:416
  23.3 14.2 %all-to-all-start.1 = ((bf16[16,72,128]{2,1,0:T(8,128)(2,1)}), bf16[16,72,128]{2,1,0:T(8,128)(2,1)S(1)}, u32[]{:S(2)}, u32[]{:S(2)}) async-start(bf16[16,72,128]{2,1,0:T(8,128)(2,1)} %shard_map.101), calls=%async_computation.1 | async-start | bytes 589824 | tf_op jit(solution)/shard_map/all_to_all | solution.py:421
  28.9 4.0 %collective-permute-start = (bf16[8,72,128]{2,1,0:T(8,128)(2,1)S(1)}, bf16[8,72,128]{2,1,0:T(8,128)(2,1)S(1)}, u32[]{:S(2)}, u32[]{:S(2)}) collective-permute-start(bf16[8,72,128]{2,1,0:T(8,128)(2,1)S(1)} %all-to-all-done.kv_ref), channel_id=1, source_target_pairs={{0,16},{16,0},{32,48},{48,32},{64,80},{80,64},{96,112},{112,96},{1... | collective-permute-start | bytes 442376 | tf_op jit(solution)/shard_map/ppermute | solution.py:422
  60.4 11.6 %all-to-all-start.3 = ((bf16[16,24,128]{2,1,0:T(8,128)(2,1)}), bf16[16,24,128]{2,1,0:T(8,128)(2,1)S(1)}, u32[]{:S(2)}, u32[]{:S(2)}) async-start(bf16[16,24,128]{2,1,0:T(8,128)(2,1)} %get-tuple-element.38), calls=%async_computation.3 | async-start | bytes 196608 | tf_op jit(solution)/shard_map/all_to_all | solution.py:453
  69.0 6.4 %collective-permute-start.2 = (bf16[8,72,128]{2,1,0:T(8,128)(2,1)S(1)}, bf16[8,72,128]{2,1,0:T(8,128)(2,1)S(1)}, u32[]{:S(2)}, u32[]{:S(2)}) collective-permute-start(bf16[8,72,128]{2,1,0:T(8,128)(2,1)S(1)} %get-tuple-element.43), channel_id=1, source_target_pairs={{0,16},{16,0},{32,48},{48,32},{64,80},{80,64},{96,112},{112,96},{1... | collective-permute-start | bytes 442376 | tf_op jit(solution)/shard_map/ppermute | solution.py:465
  71.9 4.3 %collective-permute-start.1 = (bf16[16,24,128]{2,1,0:T(8,128)(2,1)S(1)}, bf16[16,24,128]{2,1,0:T(8,128)(2,1)S(1)}, u32[]{:S(2)}, u32[]{:S(2)}) collective-permute-start(bf16[16,24,128]{2,1,0:T(8,128)(2,1)S(1)} %all-to-all-done.3.part_ref), channel_id=1, source_target_pairs={{0,16},{16,0},{32,48},{48,32},{64,80},{80,64},{96,112},{112,96},{1... | collective-permute-start | bytes 294920 | tf_op jit(solution)/shard_map/ppermute | solution.py:466
  77.0 16.0 %all-to-all-start.4 = ((bf16[8,96,128]{2,1,0:T(8,128)(2,1)}), bf16[8,96,128]{2,1,0:T(8,128)(2,1)S(1)}, u32[]{:S(2)}, u32[]{:S(2)}) async-start(bf16[8,96,128]{2,1,0:T(8,128)(2,1)} %shard_map.107), calls=%async_computation.4 | async-start | bytes 393216 | tf_op jit(solution)/shard_map/all_to_all | solution.py:472
  93.9 13.4 %all-to-all-start.5 = ((bf16[16,64,128]{2,1,0:T(8,128)(2,1)}), bf16[16,64,128]{2,1,0:T(8,128)(2,1)S(1)}, u32[]{:S(2)}, u32[]{:S(2)}) async-start(bf16[16,64,128]{2,1,0:T(8,128)(2,1)} %get-tuple-element.44), calls=%async_computation.5 | async-start | bytes 524288 | tf_op jit(solution)/shard_map/all_to_all | solution.py:487

commit v11 on v10

--- a/solution.py
+++ b/solution.py
@@ -1,5 +1,3 @@
-import functools
-
 import jax
 import jax.numpy as jnp
 from jax import lax
@@ -98,22 +96,25 @@
     return [jnp.dot(target[...], hot, preferred_element_type=F32) for target in targets]
 
 
-def prepare_kernel(scale, first_hbm, second_hbm, out_ref, first_ref, second_ref, sems):
-    first, second = load_all((first_hbm, second_hbm), (first_ref, second_ref), sems)
-    packed = pack_two(first * scale, second).astype(LOW)
-    for n in range(out_ref.shape[0]):
-        out_ref[n] = packed
-
-
-def prepare(first, second, copies, scale):
+def prepare_kernel(q_hbm, o_hbm, k_hbm, v_hbm, qo_ref, kv_ref, q_ref, o_ref, k_ref, v_ref, sems):
+    q, o, k, v = load_all((q_hbm, o_hbm, k_hbm, v_hbm), (q_ref, o_ref, k_ref, v_ref), sems)
+    packed = pack_two(k, v).astype(LOW)
+    for n in range(8):
+        kv_ref[n] = packed
+    packed = pack_two(q * (1.0 / HD**0.5), o).astype(LOW)
+    for n in range(SIDE):
+        qo_ref[n] = packed
+
+
+def prepare(queries, d_out, keys, values):
+    vmem = pl.BlockSpec(memory_space=pltpu.VMEM)
     return pl.pallas_call(
-        functools.partial(prepare_kernel, scale),
-        out_shape=array((copies, PAIR_ROWS, LANES), LOW),
-        in_specs=[pl.BlockSpec(memory_space=pl.ANY)] * 2,
-        out_specs=pl.BlockSpec(memory_space=pltpu.VMEM),
-        scratch_shapes=[pltpu.VMEM((N_I, H), LOW)] * 2 + [pltpu.SemaphoreType.DMA((2,))],
-        cost_estimate=pl.CostEstimate(flops=10_000_000, bytes_accessed=400_000, transcendentals=0),
-    )(first, second)
+        prepare_kernel,
+        out_shape=[array((SIDE, PAIR_ROWS, LANES), LOW), array((8, PAIR_ROWS, LANES), LOW)],
+        in_specs=[pl.BlockSpec(memory_space=pl.ANY)] * 4,
+        out_specs=[vmem] * 2,
+        scratch_shapes=[pltpu.VMEM((N_I, H), LOW)] * 4 + [pltpu.SemaphoreType.DMA((4,))],
+    )(queries, d_out, keys, values)
 
 
 def place_of(shape):
@@ -411,8 +412,7 @@
 def on_device(pair, w_bias, queries, keys, values, d_out):
     flat_pair = pair.reshape(CELLS, P_SIZE)
     row_at = lax.axis_index("row").astype(jnp.int32).reshape(1)
-    kv_send = prepare(keys, values, 8, 1.0)
-    qo_send = prepare(queries, d_out, SIDE, 1.0 / HD**0.5)
+    qo_send, kv_send = prepare(queries, d_out, keys, values)
     kv = lax.all_to_all(kv_send, "row", 0, 0, axis_index_groups=CORE_APART)
     wide = jnp.pad(w_bias.T.reshape(SIDE, PLACES, P_SIZE), ((0, 0), (0, 2), (0, 0)))
     wide = wide.reshape(LANES, P_SIZE)

time: 109 us -> 108 us (level)
  waiting for transfers between devices: 23 us -> 24.7 us
  starting transfers between devices: 41.4 us -> 39.7 us
  Pallas kernels: 20.9 us -> 19.4 us
    all_to_all x1, starting transfers between devices: 6.14 us -> 4.45 us  [on_device(): lax.all_to_all(row_send, 'row', 0, 0, axis_index_groups=CORE_APART)]
    all_to_all x1, waiting for transfers between devices: 4.47 us -> 6.15 us  [on_device(): kv = lax.all_to_all(kv_send, 'row', 0, 0, axis_index_groups=CORE_APART)]
    pallas_call x2 -> x1, Pallas kernels: 3.28 us -> 1.79 us  [prepare(): pl.pallas_call(prepare_kernel, out_shape=[array((SIDE, PAIR_ROWS, LANES),...]
  transfers between devices with their start and end apart: 8 -> 8, of which waited for: 7 -> 7; matrix products, arithmetic and copies ran while one was open for 5% -> 5% of each run, Pallas kernels for 10% -> 8%
where the time goes in v11:
time: 108 us; the launch traced here: 107 us
  starting transfers between devices  39.7 us (37%)
  waiting for transfers between devices  24.7 us (23%)
  Pallas kernels  19.4 us (18%)
  blocking collectives  16.7 us (15%)
  matrix products  4.6 us (4%)
    all_to_all x1, blocking collectives, on_device(): stats = lax.all_to_all(stats, 'col', 0, 0)  16.7 us
    pallas_call x7, Pallas kernels, call(): pl.pallas_call(kernel, out_shape=out_shape, in_specs=specs, out_specs=out...  13.2 us
    all_to_all x1, starting transfers between devices, on_device(): kv = lax.all_to_all(kv_send, 'row', 0, 0, axis_index_groups=CORE_APART)  11.5 us
    all_to_all x1, waiting for transfers between devices, on_device(): lax.all_to_all(row_send, 'row', 0, 0, axis_index_groups=CORE_APART)  6.54 us
    all_to_all x1, waiting for transfers between devices, on_device(): col_recv = lax.all_to_all(col_send, 'col', 0, 0)  6.38 us
    all_to_all x1, waiting for transfers between devices, on_device(): kv = lax.all_to_all(kv_send, 'row', 0, 0, axis_index_groups=CORE_APART)  6.15 us
    all_to_all x1, starting transfers between devices, on_device(): qo = lax.all_to_all(qo_send, 'col', 0, 0)  5.66 us
    all_to_all x1, starting transfers between devices, on_device(): col_recv = lax.all_to_all(col_send, 'col', 0, 0)  4.87 us
  transfers between devices with their start and end apart: 8, of which 7 were waited for; matrix products, arithmetic and copies ran while one was open for 5% of the time, Pallas kernels for 8%

profile of v11, /device:TPU:1, one launch (start us, length us, event | category | flops | bytes accessed | tf_op | source)
XLA Modules:
  0.0 106.7 jit_solution(10501844343035865754)
XLA Ops:
  0.6 1.8 %shard_map.101 = (bf16[16,72,128]{2,1,0:T(8,128)(2,1)}, bf16[8,72,128]{2,1,0:T(8,128)(2,1)}) custom-call(bf16[48,96]{1,0:T(8,128)(2,1)} %q_hbm.1, bf16[48,96]{1,0:T(8,128)(2,1)} %o_hbm.1, bf16[48,96]{1,0:T(8,128)(2,1)} %k_hbm.1, bf16[48,96]{1,0:T(8,128)(2,1)} %v_hbm.1), custom_call_target="tpu_custom_call" | custom-call | tf_op jit(solution)/shard_map/pallas_call | solution.py:111
  2.4 11.5 %all-to-all-start = ((bf16[8,72,128]{2,1,0:T(8,128)(2,1)}), bf16[8,72,128]{2,1,0:T(8,128)(2,1)S(1)}, u32[]{:S(2)}, u32[]{:S(2)}) async-start(bf16[8,72,128]{2,1,0:T(8,128)(2,1)} %get-tuple-element.30), calls=%async_computation | async-start | bytes 294912 | tf_op jit(solution)/shard_map/all_to_all | solution.py:416
  13.9 0.9 reshape.25
  14.8 2.4 %convolution_bitcast_fusion.bias_ref = f32[2304,128]{1,0:T(8,128)S(1)} fusion(bf16[2304,512]{1,0:T(8,128)(2,1)} %bitcast.14, bf16[16,6,512]{2,1,0:T(8,128)(2,1)S(1)} %reshape.25), kind=kOutput, calls=%fused_computation.1 | convolution fusion | flops 301989888 | bytes 3637248 | tf_op jit(solution)/shard_map/dot_general | solution.py:65
  17.3 6.2 %all-to-all-done.kv_ref = bf16[8,72,128]{2,1,0:T(8,128)(2,1)S(1)} async-done(((bf16[8,72,128]{2,1,0:T(8,128)(2,1)}), bf16[8,72,128]{2,1,0:T(8,128)(2,1)S(1)}, u32[]{:S(2)}, u32[]{:S(2)}) %all-to-all-start) | async-done | bytes 147488 | tf_op jit(solution)/shard_map/all_to_all | solution.py:416
  23.4 5.7 %all-to-all-start.1 = ((bf16[16,72,128]{2,1,0:T(8,128)(2,1)}), bf16[16,72,128]{2,1,0:T(8,128)(2,1)S(1)}, u32[]{:S(2)}, u32[]{:S(2)}) async-start(bf16[16,72,128]{2,1,0:T(8,128)(2,1)} %get-tuple-element.31), calls=%async_computation.1 | async-start | bytes 589824 | tf_op jit(solution)/shard_map/all_to_all | solution.py:421
  29.1 3.0 %collective-permute-start = (bf16[8,72,128]{2,1,0:T(8,128)(2,1)S(1)}, bf16[8,72,128]{2,1,0:T(8,128)(2,1)S(1)}, u32[]{:S(2)}, u32[]{:S(2)}) collective-permute-start(bf16[8,72,128]{2,1,0:T(8,128)(2,1)S(1)} %all-to-all-done.kv_ref), channel_id=1, source_target_pairs={{0,16},{16,0},{32,48},{48,32},{64,80},{80,64},{96,112},{112,96},{1... | collective-permute-start | bytes 442376 | tf_op jit(solution)/shard_map/ppermute | solution.py:422
  32.1 1.0 collective-permute-done.partner_ref
  33.1 1.5 %shard_map.102 = (f32[16,48,128]{2,1,0:T(8,128)S(1)}, f32[16,48,128]{2,1,0:T(8,128)S(1)}) custom-call(s32[1]{0:T(128)} %bitcast.4.row_ref.core_ref, bf16[8,72,128]{2,1,0:T(8,128)(2,1)S(1)} %all-to-all-done.kv_ref, bf16[8,72,128]{2,1,0:T(8,128)(2,1)S(1)} %collective-permute-done.partner_ref), custom_call_target="tpu_custom_call" | custom-call | flops 1000000000 | bytes 2000000 | tf_op jit(solution)/shard_map/pallas_call | solution.py:35
  34.6 3.1 %all-to-all-done.1.qo_ref = bf16[16,72,128]{2,1,0:T(8,128)(2,1)S(1)} async-done(((bf16[16,72,128]{2,1,0:T(8,128)(2,1)}), bf16[16,72,128]{2,1,0:T(8,128)(2,1)S(1)}, u32[]{:S(2)}, u32[]{:S(2)}) %all-to-all-start.1) | async-done | bytes 294944 | tf_op jit(solution)/shard_map/all_to_all | solution.py:421
  37.6 4.4 %shard_map.103 = (f32[2304,128]{1,0:T(8,128)S(1)}, f32[2304,128]{1,0:T(8,128)S(1)}, f32[3,48,128]{2,1,0:T(8,128)S(1)}, bf16[16,112,128]{2,1,0:T(8,128)(2,1)S(1)}...) custom-call(bf16[16,72,128]{2,1,0:T(8,128)(2,1)S(1)} %all-to-all-done.1.qo_ref, ...), custom_call_target="tpu_custom_call" | custom-call | tf_op jit(solution)/shard_map/pallas_call | solution.py:435
  42.1 16.7 %all_to_all.30.stat_ref = bf16[16,112,128]{2,1,0:T(8,128)(2,1)S(1)} all-to-all(bf16[16,112,128]{2,1,0:T(8,128)(2,1)S(1)} %get-tuple-element.36), channel_id=1, replica_groups=mesh['row'=16,'col'=16] {'col'}, dimensions={0} | all-to-all | bytes 917504 | tf_op jit(solution)/shard_map/all_to_all | solution.py:446
  58.8 1.8 %shard_map.104 = (bf16[2304,128]{1,0:T(8,128)(2,1)S(1)}, bf16[2304,128]{1,0:T(8,128)(2,1)S(1)}, bf16[16,24,128]{2,1,0:T(8,128)(2,1)}) custom-call(bf16[16,112,128]{2,1,0:T(8,128)(2,1)S(1)} %all_to_all.30.stat_ref, f32[3,48,128]{2,1,0:T(8,128)S(1)} %get-tuple-element.37.own_ref, f32[2304,128]{1,0:T(8,128)S(1)} %get-tuple-element.38.e_ref, ...), custom_call_target="tpu_custom_call" | custom-call | tf_op jit(solution)/shard_map/pallas_call | solution.py:35
  60.5 4.4 %all-to-all-start.3 = ((bf16[16,24,128]{2,1,0:T(8,128)(2,1)}), bf16[16,24,128]{2,1,0:T(8,128)(2,1)S(1)}, u32[]{:S(2)}, u32[]{:S(2)}) async-start(bf16[16,24,128]{2,1,0:T(8,128)(2,1)} %get-tuple-element.42), calls=%async_computation.3 | async-start | bytes 196608 | tf_op jit(solution)/shard_map/all_to_all | solution.py:453
  65.0 4.1 %shard_map.105 = (bf16[8,72,128]{2,1,0:T(8,128)(2,1)S(1)}, bf16[8,72,128]{2,1,0:T(8,128)(2,1)S(1)}) custom-call(s32[1]{0:T(128)} %bitcast.4.row_ref.core_ref, bf16[2304,128]{1,0:T(8,128)(2,1)S(1)} %get-tuple-element.41.score_ref, bf16[2304,128]{1,0:T(8,128)(2,1)S(1)} %get-tuple-element.43.weight_ref, f32[16,48,128]{2,1,0:T(8,128)S(1)} %get-tuple-element.44.q2_ref, ...), custom_call_target="tpu_custom_call" | custom-call | flops 4000000000 | bytes 4000000 | tf_op jit(solution)/shard_map/pallas_call | solution.py:35
  69.1 2.4 %collective-permute-start.2 = (bf16[8,72,128]{2,1,0:T(8,128)(2,1)S(1)}, bf16[8,72,128]{2,1,0:T(8,128)(2,1)S(1)}, u32[]{:S(2)}, u32[]{:S(2)}) collective-permute-start(bf16[8,72,128]{2,1,0:T(8,128)(2,1)S(1)} %get-tuple-element.47), channel_id=1, source_target_pairs={{0,16},{16,0},{32,48},{48,32},{64,80},{80,64},{96,112},{112,96},{1... | collective-permute-start | bytes 442376 | tf_op jit(solution)/shard_map/ppermute | solution.py:465
  71.5 0.6 all-to-all-done.3.part_ref
  72.1 3.4 %collective-permute-start.1 = (bf16[16,24,128]{2,1,0:T(8,128)(2,1)S(1)}, bf16[16,24,128]{2,1,0:T(8,128)(2,1)S(1)}, u32[]{:S(2)}, u32[]{:S(2)}) collective-permute-start(bf16[16,24,128]{2,1,0:T(8,128)(2,1)S(1)} %all-to-all-done.3.part_ref), channel_id=1, source_target_pairs={{0,16},{16,0},{32,48},{48,32},{64,80},{80,64},{96,112},{112,96},{1... | collective-permute-start | bytes 294920 | tf_op jit(solution)/shard_map/ppermute | solution.py:466
  75.5 0.0 collective-permute-done.2.partner_ref
  75.5 0.9 collective-permute-done.1.part_partner_ref
  76.5 0.7 shard_map.106
  77.2 4.5 %all-to-all-start.4 = ((bf16[8,96,128]{2,1,0:T(8,128)(2,1)}), bf16[8,96,128]{2,1,0:T(8,128)(2,1)S(1)}, u32[]{:S(2)}, u32[]{:S(2)}) async-start(bf16[8,96,128]{2,1,0:T(8,128)(2,1)} %shard_map.106), calls=%async_computation.4 | async-start | bytes 393216 | tf_op jit(solution)/shard_map/all_to_all | solution.py:472
  81.6 3.3 %shard_map.107.query_ref = bf16[16,40,128]{2,1,0:T(8,128)(2,1)S(1)} custom-call(bf16[2304,128]{1,0:T(8,128)(2,1)S(1)} %get-tuple-element.41.score_ref, f32[16,48,128]{2,1,0:T(8,128)S(1)} %get-tuple-element.33.k2_ref), custom_call_target="tpu_custom_call" | custom-call | flops 4000000000 | bytes 4000000 | tf_op jit(solution)/shard_map/pallas_call | solution.py:35
  84.9 6.5 %all-to-all-done.4.recv_ref = bf16[8,96,128]{2,1,0:T(8,128)(2,1)S(1)} async-done(((bf16[8,96,128]{2,1,0:T(8,128)(2,1)}), bf16[8,96,128]{2,1,0:T(8,128)(2,1)S(1)}, u32[]{:S(2)}, u32[]{:S(2)}) %all-to-all-start.4) | async-done | bytes 196640 | tf_op jit(solution)/shard_map/all_to_all | solution.py:472
  91.5 0.9 shard_map.108
  92.4 4.9 %all-to-all-start.5 = ((bf16[16,64,128]{2,1,0:T(8,128)(2,1)}), bf16[16,64,128]{2,1,0:T(8,128)(2,1)S(1)}, u32[]{:S(2)}, u32[]{:S(2)}) async-start(bf16[16,64,128]{2,1,0:T(8,128)(2,1)} %get-tuple-element.48), calls=%async_computation.5 | async-start | bytes 524288 | tf_op jit(solution)/shard_map/all_to_all | solution.py:487
  97.3 2.2 %convolution_convert_fusion = bf16[2304,512]{1,0:T(8,128)(2,1)} fusion(bf16[2304,128]{1,0:T(8,128)(2,1)S(1)} %get-tuple-element.41.score_ref, bf16[16,6,512]{2,1,0:T(8,128)(2,1)S(1)} %reshape.25), kind=kOutput, calls=%fused_computation | convolution fusion | flops 303169536 | bytes 3047424 | tf_op jit(solution)/shard_map/dot_general | solution.py:481
  99.4 6.4 %all-to-all-done.5.recv_ref = bf16[16,64,128]{2,1,0:T(8,128)(2,1)S(1)} async-done(((bf16[16,64,128]{2,1,0:T(8,128)(2,1)}), bf16[16,64,128]{2,1,0:T(8,128)(2,1)S(1)}, u32[]{:S(2)}, u32[]{:S(2)}) %all-to-all-start.5) | async-done | bytes 262176 | tf_op jit(solution)/shard_map/all_to_all | solution.py:487
  105.8 0.9 shard_map.109
Async XLA Ops:
  2.4 21.0 %all-to-all-start = ((bf16[8,72,128]{2,1,0:T(8,128)(2,1)}), bf16[8,72,128]{2,1,0:T(8,128)(2,1)S(1)}, u32[]{:S(2)}, u32[]{:S(2)}) async-start(bf16[8,72,128]{2,1,0:T(8,128)(2,1)} %get-tuple-element.30), calls=%async_computation | async-start | bytes 294912 | tf_op jit(solution)/shard_map/all_to_all | solution.py:416
  23.4 14.2 %all-to-all-start.1 = ((bf16[16,72,128]{2,1,0:T(8,128)(2,1)}), bf16[16,72,128]{2,1,0:T(8,128)(2,1)S(1)}, u32[]{:S(2)}, u32[]{:S(2)}) async-start(bf16[16,72,128]{2,1,0:T(8,128)(2,1)} %get-tuple-element.31), calls=%async_computation.1 | async-start | bytes 589824 | tf_op jit(solution)/shard_map/all_to_all | solution.py:421
  29.1 4.0 %collective-permute-start = (bf16[8,72,128]{2,1,0:T(8,128)(2,1)S(1)}, bf16[8,72,128]{2,1,0:T(8,128)(2,1)S(1)}, u32[]{:S(2)}, u32[]{:S(2)}) collective-permute-start(bf16[8,72,128]{2,1,0:T(8,128)(2,1)S(1)} %all-to-all-done.kv_ref), channel_id=1, source_target_pairs={{0,16},{16,0},{32,48},{48,32},{64,80},{80,64},{96,112},{112,96},{1... | collective-permute-start | bytes 442376 | tf_op jit(solution)/shard_map/ppermute | solution.py:422
  60.5 11.6 %all-to-all-start.3 = ((bf16[16,24,128]{2,1,0:T(8,128)(2,1)}), bf16[16,24,128]{2,1,0:T(8,128)(2,1)S(1)}, u32[]{:S(2)}, u32[]{:S(2)}) async-start(bf16[16,24,128]{2,1,0:T(8,128)(2,1)} %get-tuple-element.42), calls=%async_computation.3 | async-start | bytes 196608 | tf_op jit(solution)/shard_map/all_to_all | solution.py:453
  69.1 6.4 %collective-permute-start.2 = (bf16[8,72,128]{2,1,0:T(8,128)(2,1)S(1)}, bf16[8,72,128]{2,1,0:T(8,128)(2,1)S(1)}, u32[]{:S(2)}, u32[]{:S(2)}) collective-permute-start(bf16[8,72,128]{2,1,0:T(8,128)(2,1)S(1)} %get-tuple-element.47), channel_id=1, source_target_pairs={{0,16},{16,0},{32,48},{48,32},{64,80},{80,64},{96,112},{112,96},{1... | collective-permute-start | bytes 442376 | tf_op jit(solution)/shard_map/ppermute | solution.py:465
  72.1 4.3 %collective-permute-start.1 = (bf16[16,24,128]{2,1,0:T(8,128)(2,1)S(1)}, bf16[16,24,128]{2,1,0:T(8,128)(2,1)S(1)}, u32[]{:S(2)}, u32[]{:S(2)}) collective-permute-start(bf16[16,24,128]{2,1,0:T(8,128)(2,1)S(1)} %all-to-all-done.3.part_ref), channel_id=1, source_target_pairs={{0,16},{16,0},{32,48},{48,32},{64,80},{80,64},{96,112},{112,96},{1... | collective-permute-start | bytes 294920 | tf_op jit(solution)/shard_map/ppermute | solution.py:466
  77.2 14.3 %all-to-all-start.4 = ((bf16[8,96,128]{2,1,0:T(8,128)(2,1)}), bf16[8,96,128]{2,1,0:T(8,128)(2,1)S(1)}, u32[]{:S(2)}, u32[]{:S(2)}) async-start(bf16[8,96,128]{2,1,0:T(8,128)(2,1)} %shard_map.106), calls=%async_computation.4 | async-start | bytes 393216 | tf_op jit(solution)/shard_map/all_to_all | solution.py:472
  92.4 13.4 %all-to-all-start.5 = ((bf16[16,64,128]{2,1,0:T(8,128)(2,1)}), bf16[16,64,128]{2,1,0:T(8,128)(2,1)S(1)}, u32[]{:S(2)}, u32[]{:S(2)}) async-start(bf16[16,64,128]{2,1,0:T(8,128)(2,1)} %get-tuple-element.48), calls=%async_computation.5 | async-start | bytes 524288 | tf_op jit(solution)/shard_map/all_to_all | solution.py:487

commit v12 on v11

--- a/solution.py
+++ b/solution.py
@@ -274,7 +274,7 @@
             own_ref[2, pl.ds(i, 1), :] = upper / total
         return carry
 
-    lax.fori_loop(0, N_I // 2, rows, 0, unroll=2)
+    lax.fori_loop(0, N_I // 2, rows, 0, unroll=8)
     packed = [x.astype(LOW) for x in pack_stats(own_ref[0], own_ref[1], own_ref[2])]
     for c in range(SIDE):
         stat_ref[c, :N_I, :] = packed[0]
@@ -353,9 +353,9 @@
     def tile_of(ref):
         return lambda i: ref[pl.ds(pl.multiple_of(i * N_J, N_J), N_J), :].astype(F32)
 
-    weighted_sums(tile_of(score_ref), q2_ref, sum_ref, 8)
+    weighted_sums(tile_of(score_ref), q2_ref, sum_ref, N_I)
     blocks_of(sum_ref, key_ref, N_J)
-    weighted_sums(tile_of(weight_ref), o2_ref, sum_ref, 8)
+    weighted_sums(tile_of(weight_ref), o2_ref, sum_ref, N_I)
     blocks_of(sum_ref, value_ref, N_J)
     first_core = (core_ref[0] & 1) == 0
     for k in range(8):

time: 108 us -> 107 us (level)
  no operation moved by 1% of the time
where the time goes in v12:
time: 107 us; the launch traced here: 106 us
  starting transfers between devices  39.7 us (37%)
  waiting for transfers between devices  25.3 us (24%)
  Pallas kernels  18.5 us (17%)
  blocking collectives  16.7 us (16%)
  matrix products  4.61 us (4%)
    all_to_all x1, blocking collectives, on_device(): stats = lax.all_to_all(stats, 'col', 0, 0)  16.7 us
    pallas_call x7, Pallas kernels, call(): pl.pallas_call(kernel, out_shape=out_shape, in_specs=specs, out_specs=out...  12.6 us
    all_to_all x1, starting transfers between devices, on_device(): kv = lax.all_to_all(kv_send, 'row', 0, 0, axis_index_groups=CORE_APART)  11.5 us
    all_to_all x1, waiting for transfers between devices, on_device(): lax.all_to_all(row_send, 'row', 0, 0, axis_index_groups=CORE_APART)  6.54 us
    all_to_all x1, waiting for transfers between devices, on_device(): col_recv = lax.all_to_all(col_send, 'col', 0, 0)  6.39 us
    all_to_all x1, waiting for transfers between devices, on_device(): kv = lax.all_to_all(kv_send, 'row', 0, 0, axis_index_groups=CORE_APART)  6.15 us
    all_to_all x1, starting transfers between devices, on_device(): qo = lax.all_to_all(qo_send, 'col', 0, 0)  5.66 us
    all_to_all x1, starting transfers between devices, on_device(): col_recv = lax.all_to_all(col_send, 'col', 0, 0)  4.87 us
  transfers between devices with their start and end apart: 8, of which 7 were waited for; matrix products, arithmetic and copies ran while one was open for 5% of the time, Pallas kernels for 8%

profile of v12, /device:TPU:1, one launch (start us, length us, event | category | flops | bytes accessed | tf_op | source)
XLA Modules:
  0.0 106.5 jit_solution(9366518419046972964)
XLA Ops:
  0.6 1.8 %shard_map.101 = (bf16[16,72,128]{2,1,0:T(8,128)(2,1)}, bf16[8,72,128]{2,1,0:T(8,128)(2,1)}) custom-call(bf16[48,96]{1,0:T(8,128)(2,1)} %q_hbm.1, bf16[48,96]{1,0:T(8,128)(2,1)} %o_hbm.1, bf16[48,96]{1,0:T(8,128)(2,1)} %k_hbm.1, bf16[48,96]{1,0:T(8,128)(2,1)} %v_hbm.1), custom_call_target="tpu_custom_call" | custom-call | tf_op jit(solution)/shard_map/pallas_call | solution.py:111
  2.4 11.5 %all-to-all-start = ((bf16[8,72,128]{2,1,0:T(8,128)(2,1)}), bf16[8,72,128]{2,1,0:T(8,128)(2,1)S(1)}, u32[]{:S(2)}, u32[]{:S(2)}) async-start(bf16[8,72,128]{2,1,0:T(8,128)(2,1)} %get-tuple-element.30), calls=%async_computation | async-start | bytes 294912 | tf_op jit(solution)/shard_map/all_to_all | solution.py:416
  13.9 0.9 reshape.25
  14.8 2.4 %convolution_bitcast_fusion.bias_ref = f32[2304,128]{1,0:T(8,128)S(1)} fusion(bf16[2304,512]{1,0:T(8,128)(2,1)} %bitcast.14, bf16[16,6,512]{2,1,0:T(8,128)(2,1)S(1)} %reshape.25), kind=kOutput, calls=%fused_computation.1 | convolution fusion | flops 301989888 | bytes 3637248 | tf_op jit(solution)/shard_map/dot_general | solution.py:65
  17.3 6.2 %all-to-all-done.kv_ref = bf16[8,72,128]{2,1,0:T(8,128)(2,1)S(1)} async-done(((bf16[8,72,128]{2,1,0:T(8,128)(2,1)}), bf16[8,72,128]{2,1,0:T(8,128)(2,1)S(1)}, u32[]{:S(2)}, u32[]{:S(2)}) %all-to-all-start) | async-done | bytes 147488 | tf_op jit(solution)/shard_map/all_to_all | solution.py:416
  23.4 5.7 %all-to-all-start.1 = ((bf16[16,72,128]{2,1,0:T(8,128)(2,1)}), bf16[16,72,128]{2,1,0:T(8,128)(2,1)S(1)}, u32[]{:S(2)}, u32[]{:S(2)}) async-start(bf16[16,72,128]{2,1,0:T(8,128)(2,1)} %get-tuple-element.31), calls=%async_computation.1 | async-start | bytes 589824 | tf_op jit(solution)/shard_map/all_to_all | solution.py:421
  29.1 3.0 %collective-permute-start = (bf16[8,72,128]{2,1,0:T(8,128)(2,1)S(1)}, bf16[8,72,128]{2,1,0:T(8,128)(2,1)S(1)}, u32[]{:S(2)}, u32[]{:S(2)}) collective-permute-start(bf16[8,72,128]{2,1,0:T(8,128)(2,1)S(1)} %all-to-all-done.kv_ref), channel_id=1, source_target_pairs={{0,16},{16,0},{32,48},{48,32},{64,80},{80,64},{96,112},{112,96},{1... | collective-permute-start | bytes 442376 | tf_op jit(solution)/shard_map/ppermute | solution.py:422
  32.1 1.0 collective-permute-done.partner_ref
  33.1 1.5 %shard_map.102 = (f32[16,48,128]{2,1,0:T(8,128)S(1)}, f32[16,48,128]{2,1,0:T(8,128)S(1)}) custom-call(s32[1]{0:T(128)} %bitcast.4.row_ref.core_ref, bf16[8,72,128]{2,1,0:T(8,128)(2,1)S(1)} %all-to-all-done.kv_ref, bf16[8,72,128]{2,1,0:T(8,128)(2,1)S(1)} %collective-permute-done.partner_ref), custom_call_target="tpu_custom_call" | custom-call | flops 1000000000 | bytes 2000000 | tf_op jit(solution)/shard_map/pallas_call | solution.py:35
  34.6 3.1 %all-to-all-done.1.qo_ref = bf16[16,72,128]{2,1,0:T(8,128)(2,1)S(1)} async-done(((bf16[16,72,128]{2,1,0:T(8,128)(2,1)}), bf16[16,72,128]{2,1,0:T(8,128)(2,1)S(1)}, u32[]{:S(2)}, u32[]{:S(2)}) %all-to-all-start.1) | async-done | bytes 294944 | tf_op jit(solution)/shard_map/all_to_all | solution.py:421
  37.6 4.1 %shard_map.103 = (f32[2304,128]{1,0:T(8,128)S(1)}, f32[2304,128]{1,0:T(8,128)S(1)}, f32[3,48,128]{2,1,0:T(8,128)S(1)}, bf16[16,112,128]{2,1,0:T(8,128)(2,1)S(1)}...) custom-call(bf16[16,72,128]{2,1,0:T(8,128)(2,1)S(1)} %all-to-all-done.1.qo_ref, ...), custom_call_target="tpu_custom_call" | custom-call | tf_op jit(solution)/shard_map/pallas_call | solution.py:435
  41.8 16.7 %all_to_all.30.stat_ref = bf16[16,112,128]{2,1,0:T(8,128)(2,1)S(1)} all-to-all(bf16[16,112,128]{2,1,0:T(8,128)(2,1)S(1)} %get-tuple-element.36), channel_id=1, replica_groups=mesh['row'=16,'col'=16] {'col'}, dimensions={0} | all-to-all | bytes 917504 | tf_op jit(solution)/shard_map/all_to_all | solution.py:446
  58.5 1.8 %shard_map.104 = (bf16[2304,128]{1,0:T(8,128)(2,1)S(1)}, bf16[2304,128]{1,0:T(8,128)(2,1)S(1)}, bf16[16,24,128]{2,1,0:T(8,128)(2,1)}) custom-call(bf16[16,112,128]{2,1,0:T(8,128)(2,1)S(1)} %all_to_all.30.stat_ref, f32[3,48,128]{2,1,0:T(8,128)S(1)} %get-tuple-element.37.own_ref, f32[2304,128]{1,0:T(8,128)S(1)} %get-tuple-element.38.e_ref, ...), custom_call_target="tpu_custom_call" | custom-call | tf_op jit(solution)/shard_map/pallas_call | solution.py:35
  60.3 4.4 %all-to-all-start.3 = ((bf16[16,24,128]{2,1,0:T(8,128)(2,1)}), bf16[16,24,128]{2,1,0:T(8,128)(2,1)S(1)}, u32[]{:S(2)}, u32[]{:S(2)}) async-start(bf16[16,24,128]{2,1,0:T(8,128)(2,1)} %get-tuple-element.42), calls=%async_computation.3 | async-start | bytes 196608 | tf_op jit(solution)/shard_map/all_to_all | solution.py:453
  64.7 3.5 %shard_map.105 = (bf16[8,72,128]{2,1,0:T(8,128)(2,1)S(1)}, bf16[8,72,128]{2,1,0:T(8,128)(2,1)S(1)}) custom-call(s32[1]{0:T(128)} %bitcast.4.row_ref.core_ref, bf16[2304,128]{1,0:T(8,128)(2,1)S(1)} %get-tuple-element.41.score_ref, bf16[2304,128]{1,0:T(8,128)(2,1)S(1)} %get-tuple-element.43.weight_ref, f32[16,48,128]{2,1,0:T(8,128)S(1)} %get-tuple-element.44.q2_ref, ...), custom_call_target="tpu_custom_call" | custom-call | flops 4000000000 | bytes 4000000 | tf_op jit(solution)/shard_map/pallas_call | solution.py:35
  68.2 2.4 %collective-permute-start.2 = (bf16[8,72,128]{2,1,0:T(8,128)(2,1)S(1)}, bf16[8,72,128]{2,1,0:T(8,128)(2,1)S(1)}, u32[]{:S(2)}, u32[]{:S(2)}) collective-permute-start(bf16[8,72,128]{2,1,0:T(8,128)(2,1)S(1)} %get-tuple-element.47), channel_id=1, source_target_pairs={{0,16},{16,0},{32,48},{48,32},{64,80},{80,64},{96,112},{112,96},{1... | collective-permute-start | bytes 442376 | tf_op jit(solution)/shard_map/ppermute | solution.py:465
  70.6 1.2 %all-to-all-done.3.part_ref = bf16[16,24,128]{2,1,0:T(8,128)(2,1)S(1)} async-done(((bf16[16,24,128]{2,1,0:T(8,128)(2,1)}), bf16[16,24,128]{2,1,0:T(8,128)(2,1)S(1)}, u32[]{:S(2)}, u32[]{:S(2)}) %all-to-all-start.3) | async-done | bytes 98336 | tf_op jit(solution)/shard_map/all_to_all | solution.py:453
  71.8 3.4 %collective-permute-start.1 = (bf16[16,24,128]{2,1,0:T(8,128)(2,1)S(1)}, bf16[16,24,128]{2,1,0:T(8,128)(2,1)S(1)}, u32[]{:S(2)}, u32[]{:S(2)}) collective-permute-start(bf16[16,24,128]{2,1,0:T(8,128)(2,1)S(1)} %all-to-all-done.3.part_ref), channel_id=1, source_target_pairs={{0,16},{16,0},{32,48},{48,32},{64,80},{80,64},{96,112},{112,96},{1... | collective-permute-start | bytes 294920 | tf_op jit(solution)/shard_map/ppermute | solution.py:466
  75.2 0.0 collective-permute-done.2.partner_ref
  75.2 0.9 collective-permute-done.1.part_partner_ref
  76.2 0.7 shard_map.106
  76.9 4.5 %all-to-all-start.4 = ((bf16[8,96,128]{2,1,0:T(8,128)(2,1)}), bf16[8,96,128]{2,1,0:T(8,128)(2,1)S(1)}, u32[]{:S(2)}, u32[]{:S(2)}) async-start(bf16[8,96,128]{2,1,0:T(8,128)(2,1)} %shard_map.106), calls=%async_computation.4 | async-start | bytes 393216 | tf_op jit(solution)/shard_map/all_to_all | solution.py:472
  81.4 3.3 %shard_map.107.query_ref = bf16[16,40,128]{2,1,0:T(8,128)(2,1)S(1)} custom-call(bf16[2304,128]{1,0:T(8,128)(2,1)S(1)} %get-tuple-element.41.score_ref, f32[16,48,128]{2,1,0:T(8,128)S(1)} %get-tuple-element.33.k2_ref), custom_call_target="tpu_custom_call" | custom-call | flops 4000000000 | bytes 4000000 | tf_op jit(solution)/shard_map/pallas_call | solution.py:35
  84.7 6.5 %all-to-all-done.4.recv_ref = bf16[8,96,128]{2,1,0:T(8,128)(2,1)S(1)} async-done(((bf16[8,96,128]{2,1,0:T(8,128)(2,1)}), bf16[8,96,128]{2,1,0:T(8,128)(2,1)S(1)}, u32[]{:S(2)}, u32[]{:S(2)}) %all-to-all-start.4) | async-done | bytes 196640 | tf_op jit(solution)/shard_map/all_to_all | solution.py:472
  91.2 0.9 shard_map.108
  92.1 4.9 %all-to-all-start.5 = ((bf16[16,64,128]{2,1,0:T(8,128)(2,1)}), bf16[16,64,128]{2,1,0:T(8,128)(2,1)S(1)}, u32[]{:S(2)}, u32[]{:S(2)}) async-start(bf16[16,64,128]{2,1,0:T(8,128)(2,1)} %get-tuple-element.48), calls=%async_computation.5 | async-start | bytes 524288 | tf_op jit(solution)/shard_map/all_to_all | solution.py:487
  97.0 2.2 %convolution_convert_fusion = bf16[2304,512]{1,0:T(8,128)(2,1)} fusion(bf16[2304,128]{1,0:T(8,128)(2,1)S(1)} %get-tuple-element.41.score_ref, bf16[16,6,512]{2,1,0:T(8,128)(2,1)S(1)} %reshape.25), kind=kOutput, calls=%fused_computation | convolution fusion | flops 303169536 | bytes 3047424 | tf_op jit(solution)/shard_map/dot_general | solution.py:481
  99.2 6.4 %all-to-all-done.5.recv_ref = bf16[16,64,128]{2,1,0:T(8,128)(2,1)S(1)} async-done(((bf16[16,64,128]{2,1,0:T(8,128)(2,1)}), bf16[16,64,128]{2,1,0:T(8,128)(2,1)S(1)}, u32[]{:S(2)}, u32[]{:S(2)}) %all-to-all-start.5) | async-done | bytes 262176 | tf_op jit(solution)/shard_map/all_to_all | solution.py:487
  105.6 0.9 shard_map.109
Async XLA Ops:
  2.4 21.0 %all-to-all-start = ((bf16[8,72,128]{2,1,0:T(8,128)(2,1)}), bf16[8,72,128]{2,1,0:T(8,128)(2,1)S(1)}, u32[]{:S(2)}, u32[]{:S(2)}) async-start(bf16[8,72,128]{2,1,0:T(8,128)(2,1)} %get-tuple-element.30), calls=%async_computation | async-start | bytes 294912 | tf_op jit(solution)/shard_map/all_to_all | solution.py:416
  23.4 14.2 %all-to-all-start.1 = ((bf16[16,72,128]{2,1,0:T(8,128)(2,1)}), bf16[16,72,128]{2,1,0:T(8,128)(2,1)S(1)}, u32[]{:S(2)}, u32[]{:S(2)}) async-start(bf16[16,72,128]{2,1,0:T(8,128)(2,1)} %get-tuple-element.31), calls=%async_computation.1 | async-start | bytes 589824 | tf_op jit(solution)/shard_map/all_to_all | solution.py:421
  29.1 4.0 %collective-permute-start = (bf16[8,72,128]{2,1,0:T(8,128)(2,1)S(1)}, bf16[8,72,128]{2,1,0:T(8,128)(2,1)S(1)}, u32[]{:S(2)}, u32[]{:S(2)}) collective-permute-start(bf16[8,72,128]{2,1,0:T(8,128)(2,1)S(1)} %all-to-all-done.kv_ref), channel_id=1, source_target_pairs={{0,16},{16,0},{32,48},{48,32},{64,80},{80,64},{96,112},{112,96},{1... | collective-permute-start | bytes 442376 | tf_op jit(solution)/shard_map/ppermute | solution.py:422
  60.3 11.6 %all-to-all-start.3 = ((bf16[16,24,128]{2,1,0:T(8,128)(2,1)}), bf16[16,24,128]{2,1,0:T(8,128)(2,1)S(1)}, u32[]{:S(2)}, u32[]{:S(2)}) async-start(bf16[16,24,128]{2,1,0:T(8,128)(2,1)} %get-tuple-element.42), calls=%async_computation.3 | async-start | bytes 196608 | tf_op jit(solution)/shard_map/all_to_all | solution.py:453
  68.2 7.0 %collective-permute-start.2 = (bf16[8,72,128]{2,1,0:T(8,128)(2,1)S(1)}, bf16[8,72,128]{2,1,0:T(8,128)(2,1)S(1)}, u32[]{:S(2)}, u32[]{:S(2)}) collective-permute-start(bf16[8,72,128]{2,1,0:T(8,128)(2,1)S(1)} %get-tuple-element.47), channel_id=1, source_target_pairs={{0,16},{16,0},{32,48},{48,32},{64,80},{80,64},{96,112},{112,96},{1... | collective-permute-start | bytes 442376 | tf_op jit(solution)/shard_map/ppermute | solution.py:465
  71.8 4.3 %collective-permute-start.1 = (bf16[16,24,128]{2,1,0:T(8,128)(2,1)S(1)}, bf16[16,24,128]{2,1,0:T(8,128)(2,1)S(1)}, u32[]{:S(2)}, u32[]{:S(2)}) collective-permute-start(bf16[16,24,128]{2,1,0:T(8,128)(2,1)S(1)} %all-to-all-done.3.part_ref), channel_id=1, source_target_pairs={{0,16},{16,0},{32,48},{48,32},{64,80},{80,64},{96,112},{112,96},{1... | collective-permute-start | bytes 294920 | tf_op jit(solution)/shard_map/ppermute | solution.py:466
  76.9 14.3 %all-to-all-start.4 = ((bf16[8,96,128]{2,1,0:T(8,128)(2,1)}), bf16[8,96,128]{2,1,0:T(8,128)(2,1)S(1)}, u32[]{:S(2)}, u32[]{:S(2)}) async-start(bf16[8,96,128]{2,1,0:T(8,128)(2,1)} %shard_map.106), calls=%async_computation.4 | async-start | bytes 393216 | tf_op jit(solution)/shard_map/all_to_all | solution.py:472
  92.1 13.4 %all-to-all-start.5 = ((bf16[16,64,128]{2,1,0:T(8,128)(2,1)}), bf16[16,64,128]{2,1,0:T(8,128)(2,1)S(1)}, u32[]{:S(2)}, u32[]{:S(2)}) async-start(bf16[16,64,128]{2,1,0:T(8,128)(2,1)} %get-tuple-element.48), calls=%async_computation.5 | async-start | bytes 524288 | tf_op jit(solution)/shard_map/all_to_all | solution.py:487
